TPU v7x, 256 devices: a whole 4x4x8 slice. The times are simulated.
256 devices in a mesh: seq: 16 (over x_lo, y, core), exp: 16 (over x_hi, z).
Axes of the slice: x: 4 (x_hi: 2, x_lo: 2; x = x_hi * 2 + x_lo), y: 4, z: 8, core: 2. Of those that a mesh axis runs over, the one named last changes fastest.
Arguments:
- q_nope: bfloat16 [1024, 16384], P('seq', 'exp'), may hold values from -6 to 6
- q_rope: bfloat16 [1024, 8192], P('seq', 'exp'), may hold values from -8 to 8
- slab_latent: bfloat16 [1024, 512], P('seq'), may hold values from -6 to 6
- slab_rope: bfloat16 [1024, 64], P('seq'), may hold values from -6 to 6
- kv_gain: float32 [512], replicated, may hold values from 0.1 to 1.9
- cache_latent: bfloat16 [1024, 512], P('seq'), may hold values from -6 to 6
- cache_rope: bfloat16 [1024, 64], P('seq'), may hold values from -8 to 8
- w_uk: bfloat16 [128, 128, 512], P('exp'), may hold values from -0.5 to 0.5
- w_uv: bfloat16 [128, 512, 128], P('exp'), may hold values from -1.5 to 1.5
- prev_rows: bfloat16 [768, 5120], P('exp'), may hold values from -6 to 6
- expert_ids: int32 [768, 6], P('exp'), may hold values from 0 to 15, all different within a row; in each aligned block of 48 rows (0 to 47, 48 to 95, ...) at most 24 rows name the same one
- gate_scores: float32 [768, 6], P('exp'), may hold values from 0.02 to 0.5
- w_gate: bfloat16 [16, 1536, 5120], P('exp', 'seq'), may hold values from -0.078125 to 0.078125
- w_up: bfloat16 [16, 1536, 5120], P('exp', 'seq'), may hold values from -0.078125 to 0.078125
- w_down: bfloat16 [16, 1536, 5120], P('exp', 'seq'), may hold values from -0.21875 to 0.21875
Outputs:
- attn_out: bfloat16 [1024, 16384], P('seq', 'exp')
- moe_out: bfloat16 [768, 5120], P('exp', 'seq')
Inputs may be any that keep to these rules, and one draw needn't show every extreme that they name: `expert_ids`: each row names 6 different experts; in each aligned block of 48 rows no expert is named by more than 24 rows, and in some block one expert is named by exactly 24.
All inputs are finite; a program needn't handle non-finite values.
Results may differ from a plain program's by a relative error of at most 0.015.
Values may be sent and summed in bfloat16 or wider, within the bound.
No kernel may reach another device: no remote copies, remote signals or barrier semaphores. Data moves between devices by JAX's collectives and lax.ppermute only.
A program may use at most 128 MiB of HBM per device.

v0:
```python
import jax
import jax.numpy as jnp
from jax import lax
from jax.sharding import PartitionSpec as P

eps = 1e-06


def partner(x, axis, bit):
    return lax.ppermute(x, axis, [(i, i ^ 1 << bit) for i in range(lax.axis_size(axis))])


def latent_norm(latent, kv_gain):
    values = latent.astype(jnp.float32)
    spread = lax.rsqrt(jnp.mean(values * values, axis=-1, keepdims=True) + eps)
    return (values * spread * kv_gain).astype(jnp.bfloat16)


def expert_slots(expert_ids, experts, capacity):
    row_count, top_count = expert_ids.shape
    flat_ids = expert_ids.reshape(row_count * top_count)
    onehot = (flat_ids[:, None] == jnp.arange(experts, dtype=jnp.int32)[None, :]).astype(jnp.int32)
    rank_in_expert = jnp.sum((jnp.cumsum(onehot, axis=0) - 1) * onehot, axis=1)
    return flat_ids * capacity + rank_in_expert


def attend(running, query_full, keys_full, latent_width, visible, score_scale):
    run_peak, run_total, run_mixed = running
    scores = (
        jnp.einsum("htc,uc->htu", query_full, keys_full, preferred_element_type=jnp.float32)
        * score_scale
    )
    scores = jnp.where(visible[None], scores, -jnp.inf)
    new_peak = jnp.maximum(run_peak, jnp.max(scores, axis=2))
    weights = jnp.exp(scores - new_peak[:, :, None])
    run_total = jnp.sum(weights, axis=2)
    update = jnp.einsum(
        "htu,uc->htc",
        weights.astype(jnp.bfloat16),
        keys_full[:, :latent_width],
        preferred_element_type=jnp.float32,
    )
    run_mixed = update
    return (new_peak, run_total, run_mixed)


def halve_sum(tensor, along_dim, bit_list, seq_index, send_piece):
    for bit_pos in bit_list:
        half_width = tensor.shape[along_dim] // 2
        upper_half = seq_index >> bit_pos & 1
        kept_part = lax.dynamic_slice_in_dim(tensor, upper_half * half_width, half_width, along_dim)
        sent_part = lax.dynamic_slice_in_dim(
            tensor, (1 - upper_half) * half_width, half_width, along_dim
        )
        tensor = kept_part + send_piece(sent_part, bit_pos)
    return tensor


def combine_rows(returned, flat_ids, slot_rank, gate_scores, low_index, slot_count):
    block_rows, top_count = gate_scores.shape
    column_count = returned.shape[2]
    in_quarter = slot_rank // slot_count == low_index
    local_slot = jnp.where(
        in_quarter, flat_ids * slot_count + slot_rank - low_index * slot_count, 0
    )
    flat_results = returned.reshape(returned.shape[0] * returned.shape[1], column_count)
    picked = flat_results[local_slot].reshape(block_rows, top_count, column_count)
    scaled_gates = jnp.where(in_quarter.reshape(block_rows, top_count), gate_scores, 0.0)
    return jnp.sum(scaled_gates[:, :, None] * picked, axis=1)


def per_device(
    q_nope,
    q_rope,
    slab_latent,
    slab_rope,
    kv_gain,
    cache_latent,
    cache_rope,
    w_uk,
    w_uv,
    prev_rows,
    expert_ids,
    gate_scores,
    w_gate,
    w_up,
    w_down,
):
    queries = q_nope.shape[0]
    head_count, nope_width, latent_width = w_uk.shape
    rope_width = slab_rope.shape[1]
    value_width = w_uv.shape[2]
    score_scale = (nope_width + rope_width) ** (-0.5)
    seq_count = lax.axis_size("seq")
    cache_len = cache_latent.shape[0]
    block_len = cache_len + queries
    cache_total = cache_len * seq_count
    slab_keys = latent_norm(slab_latent, kv_gain)
    query_latent = jnp.einsum(
        "thn,hnc->htc",
        q_nope.reshape(queries, head_count, nope_width),
        w_uk,
        preferred_element_type=jnp.float32,
    ).astype(jnp.bfloat16)
    query_rope = jnp.transpose(q_rope.reshape(queries, head_count, rope_width), (1, 0, 2))
    query_full = jnp.concatenate([query_latent, query_rope], axis=2)
    own_keys = jnp.concatenate(
        [
            jnp.concatenate([cache_latent, cache_rope], axis=1),
            jnp.concatenate([slab_keys, slab_rope], axis=1),
        ],
        axis=0,
    )
    seq_index = lax.axis_index("seq")
    query_pos = cache_total + seq_index * queries + jnp.arange(queries, dtype=jnp.int32)
    first_running = (
        jnp.full((head_count, queries), -1e30, jnp.float32),
        jnp.zeros((head_count, queries), jnp.float32),
        jnp.zeros((head_count, queries, latent_width), jnp.float32),
    )
    piece = lax.all_gather(own_keys, "seq", axis=0, tiled=True)
    gathered_row = jnp.arange(piece.shape[0], dtype=jnp.int32)
    owner = gathered_row // block_len
    offset = gathered_row % block_len
    key_pos = jnp.where(
        offset < cache_len,
        owner * cache_len + offset,
        cache_total + owner * queries + offset - cache_len,
    )
    visible = key_pos[None, :] <= query_pos[:, None]
    run_peak, run_total, run_mixed = attend(
        first_running, query_full, piece, latent_width, visible, score_scale
    )
    mixed_latent = (run_mixed / run_total[:, :, None]).astype(jnp.bfloat16)
    attn_out = (
        jnp.einsum("htc,hcv->thv", mixed_latent, w_uv, preferred_element_type=jnp.float32)
        .astype(jnp.bfloat16)
        .reshape(queries, head_count * value_width)
    )
    block_rows, top_count = expert_ids.shape
    model_width = prev_rows.shape[1]
    exp_count = lax.axis_size("exp")
    seq_bits = seq_count.bit_length() - 1
    low_index = seq_index % 4
    local_experts = w_gate.shape[0]
    experts = local_experts * exp_count
    capacity = 4 * (block_rows * top_count // (3 * experts))
    slot_count = capacity // 4
    slot_index = expert_slots(expert_ids, experts, capacity)
    flat_ids = expert_ids.reshape(block_rows * top_count)
    slot_rank = slot_index - flat_ids * capacity
    source_row = jnp.arange(block_rows * top_count, dtype=jnp.int32) // top_count
    row_table = (
        jnp.zeros((experts * capacity,), jnp.int32)
        .at[slot_index]
        .set(source_row)
        .reshape(experts, capacity)
    )
    occupied = (
        jnp.zeros((experts * capacity,), jnp.bfloat16)
        .at[slot_index]
        .set(1.0)
        .reshape(experts, capacity)
    )
    quarter_rows = lax.dynamic_slice_in_dim(row_table, low_index * slot_count, slot_count, 1)
    quarter_used = lax.dynamic_slice_in_dim(occupied, low_index * slot_count, slot_count, 1)
    outgoing = prev_rows[quarter_rows] * quarter_used[:, :, None]
    unit_gate, unit_up, unit_down = (w_gate, w_up, w_down)
    for bit_pos in range(2):
        arrived_units = partner((unit_gate, unit_up, unit_down), "seq", bit_pos)
        unit_gate = jnp.concatenate([unit_gate, arrived_units[0]], axis=1)
        unit_up = jnp.concatenate([unit_up, arrived_units[1]], axis=1)
        unit_down = jnp.concatenate([unit_down, arrived_units[2]], axis=1)
    arrived = lax.all_to_all(outgoing, "exp", split_axis=0, concat_axis=0, tiled=True)
    item_count = arrived.shape[1]
    grouped = arrived.reshape(exp_count, local_experts, item_count, model_width)
    gate_act = jnp.einsum("sxid,xfd->sxif", grouped, unit_gate, preferred_element_type=jnp.float32)
    up_act = jnp.einsum("sxid,xfd->sxif", grouped, unit_up, preferred_element_type=jnp.float32)
    hidden = (jax.nn.silu(gate_act) * up_act).astype(jnp.bfloat16)
    produced = jnp.einsum("sxif,xfd->sxid", hidden, unit_down, preferred_element_type=jnp.float32)
    partials = produced.reshape(exp_count * local_experts, item_count, model_width)
    returned = lax.all_to_all(
        partials.astype(jnp.bfloat16), "exp", split_axis=0, concat_axis=0, tiled=True
    ).astype(partials.dtype)
    combined = combine_rows(returned, flat_ids, slot_rank, gate_scores, low_index, slot_count)
    moe_sum = halve_sum(
        combined,
        1,
        range(seq_bits - 1, -1, -1),
        seq_index,
        lambda sent_piece, bit_pos: partner(sent_piece.astype(jnp.bfloat16), "seq", bit_pos).astype(
            sent_piece.dtype
        ),
    )
    moe_out = moe_sum.astype(jnp.bfloat16)
    return (attn_out, moe_out)


def solution(mesh):
    placed = (
        P("seq", "exp"),
        P("seq", "exp"),
        P("seq", None),
        P("seq", None),
        P(),
        P("seq", None),
        P("seq", None),
        P("exp", None, None),
        P("exp", None, None),
        P("exp", None),
        P("exp", None),
        P("exp", None),
        P("exp", "seq", None),
        P("exp", "seq", None),
        P("exp", "seq", None),
    )
    return jax.shard_map(
        per_device,
        mesh=mesh,
        in_specs=placed,
        out_specs=(P("seq", "exp"), P("exp", "seq")),
        check_vma=False,
    )
```

profile of v0, /device:TPU:3, one launch (start us, length us, event | category | flops | bytes accessed | tf_op | source)
XLA Modules:
  0.0 274.3 jit_solution(13851704919276346419)
XLA Ops:
  11.4 2.9 %scatter_custom_fusion = s32[384]{0:T(512)S(1)} fusion(s32[288]{0:T(512)S(1)} %get-tuple-element.3, s32[288]{0:T(512)S(1)} %add_select_fusion.2, s32[]{:T(128)} %constant.52.clone.1), kind=kCustom, calls=%fused_computation.128 | custom fusion | bytes 1540 | tf_op jit(solution)/shard_map/scatter | solution.py:156
  14.6 3.2 %gather_fusion = bf16[96,5120]{1,0:T(8,128)(2,1)S(1)} fusion(bf16[48,5120]{1,0:T(8,128)(2,1)} %param.24, s32[1024]{0:T(1024)S(1)} %pad_clamp_fusion.1), kind=kCustom, calls=%fused_computation | custom fusion | bytes 1966464 | tf_op jit(solution)/shard_map/gather | solution.py:167
  18.2 2.4 scatter_custom_fusion.1
  20.7 1.2 broadcast_multiply_fusion
  22.0 9.9 %all-to-all-start = ((bf16[16,6,5120]{2,1,0:T(8,128)(2,1)}), bf16[16,6,5120]{2,1,0:T(8,128)(2,1)}, u32[]{:S(2)}, u32[]{:S(2)}) async-start(bf16[16,6,5120]{2,1,0:T(8,128)(2,1)} %broadcast_multiply_fusion), calls=%async_computation | async-start | bytes 2621440 | tf_op jit(solution)/shard_map/all_to_all | solution.py:174
  32.7 1.6 pad_maximum_fusion.2
  34.4 1.4 collective-permute-start.5
  35.8 2.9 %pad_maximum_fusion.1 = bf16[1,192,5120]{2,1,0:T(8,128)(2,1)} fusion(bf16[1,96,5120]{2,1,0:T(8,128)(2,1)} %collective-permute-done.2, bf16[1,96,5120]{2,1,0:T(8,128)(2,1)} %param.27), kind=kLoop, calls=%fused_computation.38 | loop fusion | flops 3932160 | bytes 3932160 | tf_op jit(solution)/shard_map/concatenate | solution.py:171
  39.8 2.6 pad_maximum_fusion
  42.5 1.3 collective-permute-start.1
  44.7 19.5 %all-to-all-done = bf16[16,6,5120]{2,1,0:T(8,128)(2,1)} async-done(((bf16[16,6,5120]{2,1,0:T(8,128)(2,1)}), bf16[16,6,5120]{2,1,0:T(8,128)(2,1)}, u32[]{:S(2)}, u32[]{:S(2)}) %all-to-all-start) | async-done | bytes 983072 | tf_op jit(solution)/shard_map/all_to_all | solution.py:174
  64.2 27.1 %collective-permute-done.5 = bf16[1,192,5120]{2,1,0:T(8,128)(2,1)} collective-permute-done((bf16[1,192,5120]{2,1,0:T(8,128)(2,1)S(1)}, bf16[1,192,5120]{2,1,0:T(8,128)(2,1)}, u32[]{:S(2)}, u32[]{:S(2)}) %collective-permute-start.5) | collective-permute-done | bytes 1966112 | tf_op jit(solution)/shard_map/ppermute | solution.py:10
  91.3 3.8 %fusion.26 = f32[16,1,6,384]{3,0,2,1:T(8,128)S(1)} fusion(bf16[1,192,5120]{2,1,0:T(8,128)(2,1)} %collective-permute-done.5, bf16[1,96,5120]{2,1,0:T(8,128)(2,1)} %collective-permute-done.4, bf16[1,96,5120]{2,1,0:T(8,128)(2,1)} %param.28, bf16[16,6,5120]{2,1,0:T(8,128)(2,1)} %all-to-all-done), kind=kOutput, calls=%fused_computation.42 | convolution fusion | flops 389283840 | bytes 5062656 | tf_op jit(solution)/shard_map/sxid,xfd->sxif/dot_general | solution.py:178
  95.2 38.3 %collective-permute-done.3 = bf16[1,192,5120]{2,1,0:T(8,128)(2,1)} collective-permute-done((bf16[1,192,5120]{2,1,0:T(8,128)(2,1)}, bf16[1,192,5120]{2,1,0:T(8,128)(2,1)}, u32[]{:S(2)}, u32[]{:S(2)}) %collective-permute-start.3) | collective-permute-done | bytes 1966112 | tf_op jit(solution)/shard_map/ppermute | solution.py:10
  133.5 3.6 %fusion.27 = f32[16,1,6,384]{3,0,2,1:T(8,128)S(1)} fusion(bf16[1,192,5120]{2,1,0:T(8,128)(2,1)} %collective-permute-done.3, bf16[1,96,5120]{2,1,0:T(8,128)(2,1)} %collective-permute-done.2, bf16[1,96,5120]{2,1,0:T(8,128)(2,1)S(1)} %copy-done.2, bf16[16,6,5120]{2,1,0:T(8,128)(2,1)} %all-to-all-done), kind=kOutput, calls=%fused_computation.43 | convolution fusion | flops 389283840 | bytes 5062656 | tf_op jit(solution)/shard_map/sxid,xfd->sxif/dot_general | solution.py:177
  137.0 38.6 %collective-permute-done.1 = bf16[1,192,5120]{2,1,0:T(8,128)(2,1)} collective-permute-done((bf16[1,192,5120]{2,1,0:T(8,128)(2,1)}, bf16[1,192,5120]{2,1,0:T(8,128)(2,1)}, u32[]{:S(2)}, u32[]{:S(2)}) %collective-permute-start.1) | collective-permute-done | bytes 1966112 | tf_op jit(solution)/shard_map/ppermute | solution.py:10
  175.6 2.6 fusion
  178.2 1.6 copy.65
  179.9 9.3 %all-to-all-start.1 = ((bf16[16,6,5120]{2,1,0:T(8,128)(2,1)}), bf16[16,6,5120]{2,1,0:T(8,128)(2,1)}, u32[]{:S(2)}, u32[]{:S(2)}) async-start(bf16[16,6,5120]{2,1,0:T(8,128)(2,1)} %copy.65), calls=%async_computation.1 | async-start | bytes 2621440 | tf_op jit(solution)/shard_map/all_to_all | solution.py:182
  189.9 1.1 convolution_convert_fusion.1
  191.1 30.2 %all-to-all-done.1 = bf16[16,6,5120]{2,1,0:T(8,128)(2,1)} async-done(((bf16[16,6,5120]{2,1,0:T(8,128)(2,1)}), bf16[16,6,5120]{2,1,0:T(8,128)(2,1)}, u32[]{:S(2)}, u32[]{:S(2)}) %all-to-all-start.1) | async-done | bytes 983072 | tf_op jit(solution)/shard_map/all_to_all | solution.py:182
  221.4 1.4 reshape.255
  222.8 4.8 %gather_fusion.1 = f32[288,5120]{1,0:T(8,128)} fusion(f32[96,5120]{1,0:T(8,128)S(1)} %reshape.255, s32[1024]{0:T(1024)S(1)} %pad_clamp_fusion), kind=kCustom, calls=%fused_computation.1 | custom fusion | bytes 11797632 | tf_op jit(solution)/shard_map/gather | solution.py:67
  227.6 7.1 %reshape.252 = f32[48,6,5120]{2,1,0:T(8,128)} reshape(f32[288,5120]{1,0:T(8,128)} %gather_fusion.1) | data formatting | bytes 11796480 | tf_op jit(solution)/shard_map/reshape | solution.py:67
  234.7 6.1 %multiply_reduce_fusion = f32[48,5120]{1,0:T(8,128)S(1)} fusion(f32[48,6,5120]{2,1,0:T(8,128)} %reshape.252, f32[48,6]{1,0:T(8,128)S(1)} %fusion.48), kind=kLoop, calls=%fused_computation.4 | loop fusion | flops 2703360 | bytes 6882432 | tf_op jit(solution)/shard_map/reduce_sum | solution.py:69
  240.8 1.5 collective-permute-start.6
  242.3 3.7 %fusion.15 = (f32[8,64]{1,0:T(8,128)S(1)}, f32[8,64,2048]{2,1,0:T(8,128)S(1)}) fusion(pred[64,2048]{1,0:T(8,128)(4,1)S(1)} %broadcast_compare_fusion, bf16[2048,576]{1,0:T(8,128)(2,1)} %all-gather.2.cloned.1.call-done, bf16[8,64,64]{2,1,0:T(8,128)(2,1)S(1)} %bitcast.76, bf16[8,64,512]{2,1,0:T(8,128)(2,1)S(1)} %copy-done.5), kind=kOutput, calls=%fused_computation.26 | convolution fusion | flops 1212284416 | bytes 7276544 | tf_op jit(solution)/shard_map/htc,uc->htu/dot_general | solution.py:30
  246.2 3.0 %collective-permute-start.7 = (bf16[48,1280]{1,0:T(8,128)(2,1)S(1)}, bf16[48,1280]{1,0:T(8,128)(2,1)S(1)}, u32[]{:S(2)}, u32[]{:S(2)}) collective-permute-start(bf16[48,1280]{1,0:T(8,128)(2,1)S(1)} %dynamic-slice_convert_fusion.1), channel_id=1, source_target_pairs={{0,64},{16,80},{32,96},{48,112},{64,0},{80,16},{96,32},{112,48},{1... | collective-permute-start | bytes 368648 | tf_op jit(solution)/shard_map/ppermute | solution.py:10
  249.3 2.3 collective-permute-done.7
  251.6 1.4 collective-permute-start.8
  255.2 6.4 %collective-permute-start.9 = (bf16[48,320]{1,0:T(8,128)(2,1)S(1)}, bf16[48,320]{1,0:T(8,128)(2,1)S(1)}, u32[]{:S(2)}, u32[]{:S(2)}) collective-permute-start(bf16[48,320]{1,0:T(8,128)(2,1)S(1)} %dynamic-slice_convert_fusion.3), channel_id=1, source_target_pairs={{0,16},{16,0},{32,48},{48,32},{64,80},{80,64},{96,112},{112,96},{1... | collective-permute-start | bytes 92168 | tf_op jit(solution)/shard_map/ppermute | solution.py:10
  261.6 4.5 %fusion.28 = bf16[8,8,8,128]{3,2,1,0:T(8,128)(2,1)S(1)} fusion(bf16[8,512,128]{2,1,0:T(8,128)(2,1)} %param.23, bf16[2048,576]{1,0:T(8,128)(2,1)} %all-gather.2.cloned.1.call-done, f32[8,64,2048]{2,1,0:T(8,128)} %copy-done.1, f32[8,64]{1,0:T(8,128)S(1)} %broadcast_maximum_fusion, pred[64,2048]{1,0:T(8,128)(4,1)S(1)} %broadcast_compare_fusion, ...), kind=kOutput, calls=%fused_computation.44 | convolution fusion | flops 1145634816 | bytes 7606272 | tf_op jit(solution)/shard_map/htc,hcv->thv/dot_general | solution.py:136
  (92 shorter events, 12.5 us)
Async XLA Ops:
  7.2 182.7 %copy-start = (bf16[8,128,512]{2,1,0:T(8,128)(2,1)S(1)}, bf16[8,128,512]{2,1,0:T(8,128)(2,1)}, u32[]{:S(2)}) copy-start(bf16[8,128,512]{2,1,0:T(8,128)(2,1)} %param.22) | copy-start | bytes 3145732
  7.2 25.5 %collective-permute-start.4 = (bf16[1,96,5120]{2,1,0:T(8,128)(2,1)}, bf16[1,96,5120]{2,1,0:T(8,128)(2,1)}, u32[]{:S(2)}, u32[]{:S(2)}) collective-permute-start(bf16[1,96,5120]{2,1,0:T(8,128)(2,1)} %param.28), channel_id=1, source_target_pairs={{0,16},{16,0},{32,48},{48,32},{64,80},{80,64},{96,112},{112,96},{1... | collective-permute-start | bytes 2949128 | tf_op jit(solution)/shard_map/ppermute | solution.py:10
  7.9 27.9 %collective-permute-start.2 = (bf16[1,96,5120]{2,1,0:T(8,128)(2,1)}, bf16[1,96,5120]{2,1,0:T(8,128)(2,1)}, u32[]{:S(2)}, u32[]{:S(2)}) collective-permute-start(bf16[1,96,5120]{2,1,0:T(8,128)(2,1)} %param.27), channel_id=1, source_target_pairs={{0,16},{16,0},{32,48},{48,32},{64,80},{80,64},{96,112},{112,96},{1... | collective-permute-start | bytes 2949128 | tf_op jit(solution)/shard_map/ppermute | solution.py:10
  22.0 42.2 %all-to-all-start = ((bf16[16,6,5120]{2,1,0:T(8,128)(2,1)}), bf16[16,6,5120]{2,1,0:T(8,128)(2,1)}, u32[]{:S(2)}, u32[]{:S(2)}) async-start(bf16[16,6,5120]{2,1,0:T(8,128)(2,1)} %broadcast_multiply_fusion), calls=%async_computation | async-start | bytes 2621440 | tf_op jit(solution)/shard_map/all_to_all | solution.py:174
  31.9 210.4 %all-gather.2.cloned.1.call-start = ((), (), s32[]{:S(2)}) async-start(), calls=%async_computation.2 | async-start | bytes 2785280 | tf_op jit(solution)/shard_map/all_gather | solution.py:121
  31.9 6.9 %collective-permute-start = (bf16[1,96,5120]{2,1,0:T(8,128)(2,1)}, bf16[1,96,5120]{2,1,0:T(8,128)(2,1)S(1)}, u32[]{:S(2)}, u32[]{:S(2)}) collective-permute-start(bf16[1,96,5120]{2,1,0:T(8,128)(2,1)} %param.29), channel_id=1, source_target_pairs={{0,16},{16,0},{32,48},{48,32},{64,80},{80,64},{96,112},{112,96},{1... | collective-permute-start | bytes 2949128 | tf_op jit(solution)/shard_map/ppermute | solution.py:10
  34.3 9.4 %copy-start.6 = (bf16[64,512]{1,0:T(8,128)(2,1)S(1)}, bf16[64,512]{1,0:T(8,128)(2,1)}, u32[]{:S(2)}) copy-start(bf16[64,512]{1,0:T(8,128)(2,1)} %param.17) | copy-start | bytes 196612
  34.4 9.5 %copy-start.13 = (f32[512]{0:T(512)S(1)}, f32[512]{0:T(512)}, u32[]{:S(2)}) copy-start(f32[512]{0:T(512)} %param.19) | copy-start | bytes 6148
  34.4 9.6 %copy-start.8 = (bf16[64,512]{1,0:T(8,128)(2,1)S(1)}, bf16[64,512]{1,0:T(8,128)(2,1)}, u32[]{:S(2)}) copy-start(bf16[64,512]{1,0:T(8,128)(2,1)} %param.20) | copy-start | bytes 196612
  34.4 9.6 %copy-start.10 = (bf16[64,64]{1,0:T(8,128)(2,1)S(1)}, bf16[64,64]{1,0:T(8,128)(2,1)}, u32[]{:S(2)}) copy-start(bf16[64,64]{1,0:T(8,128)(2,1)} %param.18) | copy-start | bytes 24580
  34.4 9.6 %copy-start.11 = (bf16[64,64]{1,0:T(8,128)(2,1)S(1)}, bf16[64,64]{1,0:T(8,128)(2,1)}, u32[]{:S(2)}) copy-start(bf16[64,64]{1,0:T(8,128)(2,1)} %param.21) | copy-start | bytes 24580
  34.4 56.9 %collective-permute-start.5 = (bf16[1,192,5120]{2,1,0:T(8,128)(2,1)S(1)}, bf16[1,192,5120]{2,1,0:T(8,128)(2,1)}, u32[]{:S(2)}, u32[]{:S(2)}) collective-permute-start(bf16[1,192,5120]{2,1,0:T(8,128)(2,1)S(1)} %pad_maximum_fusion.2), channel_id=1, source_target_pairs={{0,32},{16,48},{32,0},{48,16},{64,96},{80,112},{96,64},{112,80},{1... | collective-permute-start | bytes 5898248 | tf_op jit(solution)/shard_map/ppermute | solution.py:10
  38.7 94.8 %collective-permute-start.3 = (bf16[1,192,5120]{2,1,0:T(8,128)(2,1)}, bf16[1,192,5120]{2,1,0:T(8,128)(2,1)}, u32[]{:S(2)}, u32[]{:S(2)}) collective-permute-start(bf16[1,192,5120]{2,1,0:T(8,128)(2,1)} %pad_maximum_fusion.1), channel_id=1, source_target_pairs={{0,32},{16,48},{32,0},{48,16},{64,96},{80,112},{96,64},{112,80},{1... | collective-permute-start | bytes 5898248 | tf_op jit(solution)/shard_map/ppermute | solution.py:10
  38.9 1.0 copy-start.3
  42.5 133.1 %collective-permute-start.1 = (bf16[1,192,5120]{2,1,0:T(8,128)(2,1)}, bf16[1,192,5120]{2,1,0:T(8,128)(2,1)}, u32[]{:S(2)}, u32[]{:S(2)}) collective-permute-start(bf16[1,192,5120]{2,1,0:T(8,128)(2,1)} %pad_maximum_fusion), channel_id=1, source_target_pairs={{0,32},{16,48},{32,0},{48,16},{64,96},{80,112},{96,64},{112,80},{1... | collective-permute-start | bytes 5898248 | tf_op jit(solution)/shard_map/ppermute | solution.py:10
  64.2 69.3 %copy-start.2 = (bf16[1,96,5120]{2,1,0:T(8,128)(2,1)S(1)}, bf16[1,96,5120]{2,1,0:T(8,128)(2,1)}, u32[]{:S(2)}) copy-start(bf16[1,96,5120]{2,1,0:T(8,128)(2,1)} %param.27) | copy-start | bytes 2949124
  95.2 80.4 %copy-start.4 = (bf16[1,96,5120]{2,1,0:T(8,128)(2,1)S(1)}, bf16[1,96,5120]{2,1,0:T(8,128)(2,1)}, u32[]{:S(2)}) copy-start(bf16[1,96,5120]{2,1,0:T(8,128)(2,1)} %copy-done.3) | copy-start | bytes 2949124
  178.2 11.3 %copy-start.12 = (f32[48,6]{0,1:T(8,128)S(1)}, f32[48,6]{0,1:T(8,128)}, u32[]{:S(2)}) copy-start(f32[48,6]{0,1:T(8,128)} %param.26) | copy-start | bytes 3460
  178.2 11.4 %copy-start.9 = (bf16[64,512]{1,0:T(8,128)(2,1)S(1)}, bf16[64,512]{1,0:T(8,128)(2,1)}, u32[]{:S(2)}) copy-start(bf16[64,512]{1,0:T(8,128)(2,1)} %param.16) | copy-start | bytes 196612
  178.2 11.7 %copy-start.7 = (bf16[64,1024]{1,0:T(8,128)(2,1)S(1)}, bf16[64,1024]{1,0:T(8,128)(2,1)}, u32[]{:S(2)}) copy-start(bf16[64,1024]{1,0:T(8,128)(2,1)} %param.15) | copy-start | bytes 393220
  179.9 41.5 %all-to-all-start.1 = ((bf16[16,6,5120]{2,1,0:T(8,128)(2,1)}), bf16[16,6,5120]{2,1,0:T(8,128)(2,1)}, u32[]{:S(2)}, u32[]{:S(2)}) async-start(bf16[16,6,5120]{2,1,0:T(8,128)(2,1)} %copy.65), calls=%async_computation.1 | async-start | bytes 2621440 | tf_op jit(solution)/shard_map/all_to_all | solution.py:182
  234.7 7.6 %copy-start.5 = (bf16[8,64,512]{2,1,0:T(8,128)(2,1)S(1)}, bf16[8,64,512]{2,1,0:T(8,128)(2,1)}, u32[]{:S(2)}) copy-start(bf16[8,64,512]{2,1,0:T(8,128)(2,1)} %convolution_convert_fusion.1) | copy-start | bytes 1572868
  240.8 5.4 %collective-permute-start.6 = (bf16[48,2560]{1,0:T(8,128)(2,1)S(1)}, bf16[48,2560]{1,0:T(8,128)(2,1)S(1)}, u32[]{:S(2)}, u32[]{:S(2)}) collective-permute-start(bf16[48,2560]{1,0:T(8,128)(2,1)S(1)} %dynamic-slice_convert_fusion), channel_id=1, source_target_pairs={{0,128},{16,144},{32,160},{48,176},{64,192},{80,208},{96,224},{112... | collective-permute-start | bytes 737288 | tf_op jit(solution)/shard_map/ppermute | solution.py:10
  246.0 7.0 %copy-start.1 = (f32[8,64,2048]{2,1,0:T(8,128)}, f32[8,64,2048]{2,1,0:T(8,128)S(1)}, u32[]{:S(2)}) copy-start(f32[8,64,2048]{2,1,0:T(8,128)S(1)} %get-tuple-element.7) | copy-start | bytes 12582916
  246.2 5.3 %collective-permute-start.7 = (bf16[48,1280]{1,0:T(8,128)(2,1)S(1)}, bf16[48,1280]{1,0:T(8,128)(2,1)S(1)}, u32[]{:S(2)}, u32[]{:S(2)}) collective-permute-start(bf16[48,1280]{1,0:T(8,128)(2,1)S(1)} %dynamic-slice_convert_fusion.1), channel_id=1, source_target_pairs={{0,64},{16,80},{32,96},{48,112},{64,0},{80,16},{96,32},{112,48},{1... | collective-permute-start | bytes 368648 | tf_op jit(solution)/shard_map/ppermute | solution.py:10
  251.6 3.5 %collective-permute-start.8 = (bf16[48,640]{1,0:T(8,128)(2,1)S(1)}, bf16[48,640]{1,0:T(8,128)(2,1)S(1)}, u32[]{:S(2)}, u32[]{:S(2)}) collective-permute-start(bf16[48,640]{1,0:T(8,128)(2,1)S(1)} %dynamic-slice_convert_fusion.2), channel_id=1, source_target_pairs={{0,32},{16,48},{32,0},{48,16},{64,96},{80,112},{96,64},{112,80},{1... | collective-permute-start | bytes 184328 | tf_op jit(solution)/shard_map/ppermute | solution.py:10
  255.2 11.6 %collective-permute-start.9 = (bf16[48,320]{1,0:T(8,128)(2,1)S(1)}, bf16[48,320]{1,0:T(8,128)(2,1)S(1)}, u32[]{:S(2)}, u32[]{:S(2)}) collective-permute-start(bf16[48,320]{1,0:T(8,128)(2,1)S(1)} %dynamic-slice_convert_fusion.3), channel_id=1, source_target_pairs={{0,16},{16,0},{32,48},{48,32},{64,80},{80,64},{96,112},{112,96},{1... | collective-permute-start | bytes 92168 | tf_op jit(solution)/shard_map/ppermute | solution.py:10
Sparse Core Ops, SparseCore 0:
  44.8 43.3 all-gather.1
where the time goes:
time: 277 us; the launch traced here: 274 us
  waiting for transfers between devices  157 us (57%)
  starting transfers between devices  36 us (13%)
  local copies, waits for them, and re-layouts  28.1 us (10%)
  other arithmetic  19.3 us (7%)
  matrix products  19.3 us (7%)
  between operations  14.5 us (5%)
    ppermute x10, waiting for transfers between devices, partner(): lax.ppermute(x, axis, [(i, i ^ 1 << bit) for i in range(lax.axis_size(axi...  107 us
    all_to_all x1, waiting for transfers between devices, per_device(): lax.all_to_all(partials.astype(jnp.bfloat16), 'exp', split_axis=0, concat...  30.2 us
    all_to_all x1, waiting for transfers between devices, per_device(): lax.all_to_all(outgoing, 'exp', split_axis=0, concat_axis=0, tiled=True)  19.5 us
    ppermute x10, starting transfers between devices, partner(): lax.ppermute(x, axis, [(i, i ^ 1 << bit) for i in range(lax.axis_size(axi...  16.7 us
    all_to_all x1, starting transfers between devices, per_device(): lax.all_to_all(outgoing, 'exp', split_axis=0, concat_axis=0, tiled=True)  9.9 us
    all_to_all x1, starting transfers between devices, per_device(): lax.all_to_all(partials.astype(jnp.bfloat16), 'exp', split_axis=0, concat...  9.34 us
    reshape x1, local copies, waits for them, and re-layouts, combine_rows(): flat_results[local_slot].reshape(block_rows, top_count, column_count)  7.12 us
    reduce_sum x1, other arithmetic, combine_rows(): return jnp.sum(scaled_gates[:, :, None] * picked, axis=1)  6.06 us
  transfers between devices with their start and end apart: 13, of which 8 were waited for; matrix products, arithmetic and copies ran while one was open for 24% of the time, Pallas kernels for 0%

commit v1 on v0

v1 whole, which is shorter than its diff:
```python
import functools
import jax
import jax.numpy as jnp
from jax import lax
from jax.experimental import pallas as pl
from jax.experimental.pallas import tpu as pltpu
from jax.sharding import Mesh, PartitionSpec as P

eps = 1e-06
SEQ = ("xl", "y", "c")
CHIPS = ("xl", "y")
EXP = ("xh", "z")
bf16 = jnp.bfloat16
f32 = jnp.float32
VMEM_LIMIT = 12 << 20
SWAP = [(0, 1), (1, 0)]
UP = [(i, (i + 1) % 4) for i in range(4)]
DOWN = [(i, (i + 3) % 4) for i in range(4)]
NT = (((1,), (1,)), ((), ()))
NN = (((1,), (0,)), ((), ()))


def mm(a, b, dims=NN):
    return lax.dot_general(a, b, dims, preferred_element_type=f32)


def latent_norm(latent, kv_gain):
    values = latent.astype(f32)
    spread = lax.rsqrt(jnp.mean(values * values, axis=-1, keepdims=True) + eps)
    return (values * spread * kv_gain).astype(bf16)


def start_all(pairs, sems):
    copies = [pltpu.make_async_copy(a, b, sem) for (a, b), sem in zip(pairs, sems)]
    for copy in copies:
        copy.start()
    return copies


def wait_all(copies):
    for copy in copies:
        copy.wait()


STEPS = [(dx, dy) for dx in range(2) for dy in range(4)]


def chip_at(dx, dy):
    return (lax.axis_index("xl") ^ dx) * 4 + ((lax.axis_index("y") + dy) & 3)


def prep_kernel(down_ref, latent_ref, gain_ref, rope_ref, cache_ref, cache_rope_ref, *refs):
    out_refs, (latent, gain, rope, cache, cache_rope, sems) = refs[:-6], refs[-6:]
    units = down_ref.shape[0]
    width = out_refs[0].shape[1]
    small = start_all(
        [
            (latent_ref, latent),
            (gain_ref, gain),
            (rope_ref, rope),
            (cache_ref, cache),
            (cache_rope_ref, cache_rope),
        ],
        [sems.at[i] for i in range(5)],
    )
    large = start_all(
        [
            (
                down_ref.at[:, pl.ds(pl.multiple_of(chip_at(*step) * width, 128), width)],
                ref.at[pl.ds(0, units)],
            )
            for step, ref in zip(STEPS, out_refs)
        ],
        [sems.at[5 + i] for i in range(len(out_refs))],
    )
    wait_all(small)
    slab = latent_norm(latent[...], gain[...])
    count, key_width = cache.shape[0], cache.shape[1] + rope.shape[1]
    blank = jnp.zeros((count, width - key_width), bf16)
    top = jnp.concatenate([cache[...], cache_rope[...], blank], axis=1)
    low = jnp.concatenate([slab, rope[...], blank], axis=1)
    keys = jnp.where(lax.axis_index("z") % 2 == 0, top, low)
    for ref in out_refs:
        ref[units:] = keys
    wait_all(large)


def join_kernel(*refs):
    *piece_refs, down_ref, keys_ref = refs
    units = down_ref.shape[1]
    count = piece_refs[0].shape[0] - units
    for (dx, dy), ref in zip(STEPS, piece_refs):
        j = chip_at(dx, -dy)
        down_ref[j] = ref[:units]
        keys_ref[pl.ds(pl.multiple_of(j * count, count), count), :] = ref[units:]


def route_kernel(
    ids_hbm, gates_hbm, rows_hbm, out_ref, mix_ref, ids, gates, held, sems, *, experts, slots
):
    chip, core = chip_at(0, 0), lax.axis_index("c")
    total, width = out_ref.shape
    padded = total // experts
    top, block = ids.shape
    copies = start_all(
        [
            (ids_hbm, ids),
            (gates_hbm, gates),
            (rows_hbm.at[:, pl.ds(pl.multiple_of(chip * width, 128), width)], held),
        ],
        [sems.at[i] for i in range(3)],
    )
    wait_all(copies[:2])
    names = lax.broadcasted_iota(jnp.int32, (experts, block), 0)
    member = jnp.zeros((experts, block), f32)
    gate = jnp.zeros((experts, block), f32)
    for k in range(top):
        hit = ids[k : k + 1, :] == names
        member = jnp.where(hit, 1.0, member)
        gate = jnp.where(hit, gates[k : k + 1, :], gate)
    before = lax.broadcasted_iota(jnp.int32, (block, block), 0) < lax.broadcasted_iota(
        jnp.int32, (block, block), 1
    )
    rank = mm(member.astype(bf16), jnp.where(before, 1.0, 0.0).astype(bf16))
    place = (member * (rank + 1.0)).astype(bf16)
    slot = lax.broadcasted_iota(jnp.int32, (total, experts), 0)
    start = lax.broadcasted_iota(jnp.int32, (total, experts), 1) * padded
    spread = jnp.where((slot >= start) & (slot < start + padded), 1.0, 0.0).astype(bf16)
    numbers = lax.broadcasted_iota(jnp.int32, (experts, block), 0).astype(bf16)
    first = (core * slots).astype(f32)
    position = lax.broadcasted_iota(jnp.int32, (total, block), 0).astype(f32)
    inside = position - mm(spread, numbers) * padded + 1.0
    take = (mm(spread, place) == inside + first) & (inside < slots + 0.5)
    rest = gate
    for part in range(3):
        piece = rest.astype(bf16)
        rest = rest - piece.astype(f32)
        mix_ref[part] = jnp.where(take, mm(spread, piece), 0.0).astype(bf16)
    wait_all(copies[2:])
    out_ref[...] = mm(jnp.where(take, 1.0, 0.0).astype(bf16), held[...]).astype(bf16)


def slot_rows(slots, padded, count, transposed=False):
    shape = (count // slots * padded, count) if transposed else (count, count // slots * padded)
    small = lax.broadcasted_iota(jnp.int32, shape, 1 if transposed else 0)
    large = lax.broadcasted_iota(jnp.int32, shape, 0 if transposed else 1)
    return jnp.where(small + small // slots * (padded - slots) == large, 1.0, 0.0).astype(bf16)


def compact_kernel(rows_ref, *refs, slots, padded):
    out_ref = refs[-1]
    out_ref[...] = mm(slot_rows(slots, padded, out_ref.shape[0]), rows_ref[...]).astype(bf16)


def stack_kernel(gate_own, gate_other, up_own, up_other, out_ref, sems):
    units = gate_own.shape[0]
    wait_all(
        start_all(
            [
                (ref, out_ref.at[pl.ds(i * units, units)])
                for i, ref in enumerate((gate_own, gate_other, up_own, up_other))
            ],
            [sems.at[i] for i in range(4)],
        )
    )


def add_pieces(piece_refs, places, weight_ref, total):
    for (dx, dy), piece in zip(places, piece_refs):
        width = piece.shape[1]
        column = pl.ds(pl.multiple_of(chip_at(dx, dy) * width, 128), width)
        total += mm(weight_ref[:, column], piece[...], NT)
    return total


def early_kernel(*refs, places):
    *piece_refs, weight_ref, out_ref = refs
    out_ref[...] = add_pieces(piece_refs, places, weight_ref, jnp.zeros(out_ref.shape, f32))


def hidden_kernel(*refs, places):
    *piece_refs, weight_ref, early_ref, out_ref = refs
    total = add_pieces(piece_refs, places, weight_ref, early_ref[...])
    units = total.shape[0] // 2
    gate = total[:units]
    hidden = (gate * jax.nn.sigmoid(gate) * total[units:]).T
    half = hidden.shape[0] // 2
    hidden = jnp.concatenate([hidden[:half], hidden[half:]], axis=1).astype(bf16)
    for j in range(out_ref.shape[0]):
        out_ref[j] = hidden


def down_kernel(hidden_ref, own_ref, other_ref, out_ref, *, slots, padded):
    chips, half, units = hidden_ref.shape
    units = units // 2
    width = out_ref.shape[1]
    low = jnp.zeros((half, width), f32)
    high = jnp.zeros((half, width), f32)
    for j in range(chips):
        weight = jnp.concatenate([own_ref[j], other_ref[j]], axis=0)
        low += mm(hidden_ref[j, :, :units], weight)
        high += mm(hidden_ref[j, :, units:], weight)
    total = jnp.concatenate([low, high], axis=0).astype(bf16)
    out_ref[...] = mm(slot_rows(slots, padded, 2 * half, True), total).astype(bf16)


def combine_kernel(mix_ref, back_ref, keep_ref, send_ref):
    back = back_ref[...]
    dims = (((0,), (0,)), ((), ()))
    total = mm(mix_ref[0], back, dims) + mm(mix_ref[1], back, dims) + mm(mix_ref[2], back, dims)
    half = total.shape[1] // 2
    low, high = total[:, :half], total[:, half:]
    first = lax.axis_index("c") == 0
    keep_ref[...] = jnp.where(first, low, high)
    send_ref[...] = jnp.where(first, high, low).astype(bf16)


def finish_kernel(keep_ref, other_ref, out_ref):
    out_ref[...] = (keep_ref[...] + other_ref[...].astype(f32)).astype(bf16)


def absorb_kernel(nope_hbm, rope_hbm, uk_hbm, out_ref, nope, rope, uk, sems):
    heads, nope_width, latent = uk.shape
    queries = nope.shape[0]
    rope_width = rope.shape[1] // heads
    wait_all(
        start_all(
            [(nope_hbm, nope), (rope_hbm, rope), (uk_hbm, uk)], [sems.at[i] for i in range(3)]
        )
    )
    for h in range(heads):
        rows = slice(h * queries, (h + 1) * queries)
        out_ref[rows, :latent] = mm(
            nope[:, h * nope_width : (h + 1) * nope_width], uk[h]
        ).astype(bf16)
        out_ref[rows, latent:] = rope[:, h * rope_width : (h + 1) * rope_width]


def attend_kernel(query_ref, *refs, first, queries, latent, scale):
    *key_refs, out_ref = refs
    count = key_refs[0].shape[0]
    key_width = query_ref.shape[1]
    rows = out_ref.shape[0]
    core, parity = lax.axis_index("c"), lax.axis_index("z") % 2
    me = chip_at(0, 0) * 2 + core
    key = lax.broadcasted_iota(jnp.int32, (queries, count), 1)
    query = lax.broadcasted_iota(jnp.int32, (queries, count), 0)
    owner, offset = key // queries * 2, key % queries
    bias = []
    for slab in (parity, 1 - parity):
        for part in (core, 1 - core):
            seen = (owner + part < me) | ((owner + part == me) & (offset <= query)) | (slab == 0)
            side = jnp.where(seen, 0.0, -jnp.inf)
            bias.append(jnp.concatenate([side, side], axis=0))
    for g in range(0, rows, 2 * queries):
        full = query_ref[first + g : first + g + 2 * queries]
        scores = [
            mm(full, ref[:, :key_width], NT) * scale + side for ref, side in zip(key_refs, bias)
        ]
        peak = functools.reduce(
            jnp.maximum, [jnp.max(part, axis=1, keepdims=True) for part in scores]
        )
        weights = [jnp.exp(part - peak) for part in scores]
        total = sum(jnp.sum(part, axis=1, keepdims=True) for part in weights)
        mixed = sum(
            mm(part.astype(bf16), ref[:, :latent]) for part, ref in zip(weights, key_refs)
        )
        out_ref[g : g + 2 * queries] = (mixed / total).astype(bf16)


def value_kernel(*refs):
    *mixed_refs, uv_hbm, out_ref, uv, sem = refs
    load = pltpu.make_async_copy(uv_hbm, uv, sem)
    load.start()
    queries = out_ref.shape[0]
    value = uv.shape[2]
    load.wait()
    h = 0
    for ref in mixed_refs:
        for row in range(0, ref.shape[0], queries):
            out_ref[:, h * value : (h + 1) * value] = mm(
                ref[row : row + queries], uv[h]
            ).astype(bf16)
            h += 1


def spec(space=pltpu.VMEM):
    return pl.BlockSpec(memory_space=space)


def pinned(dims, dtype=bf16):
    return pltpu.VMEM(dims, dtype)


def call(kernel, out_shape, *args, scratch=(), flops=0, size=0, name=None):
    spaces = {"v": pltpu.VMEM, "a": pl.ANY, "h": pltpu.HBM}
    arrays = [
        x if space == "a" else pltpu.with_memory_space_constraint(x, spaces[space])
        for x, space in args
    ]
    leaves = lambda x: not isinstance(x, (list, tuple))
    return pl.pallas_call(
        kernel,
        out_shape=out_shape,
        in_specs=[spec(spaces[space]) for _, space in args],
        out_specs=jax.tree.map(lambda _: spec(), out_shape, is_leaf=leaves),
        scratch_shapes=list(scratch),
        compiler_params=pltpu.CompilerParams(vmem_limit_bytes=VMEM_LIMIT),
        cost_estimate=pl.CostEstimate(flops=flops, bytes_accessed=size, transcendentals=0),
        name=name,
    )(*arrays)


def shape(dims, dtype=bf16):
    return jax.ShapeDtypeStruct(dims, dtype)


def exchange(x, axes):
    return lax.all_to_all(x, axes, split_axis=0, concat_axis=0, tiled=True)


def after(x, *others):
    return lax.optimization_barrier((x,) + others)[0]


def per_device(
    q_nope,
    q_rope,
    slab_latent,
    slab_rope,
    kv_gain,
    cache_latent,
    cache_rope,
    w_uk,
    w_uv,
    prev_rows,
    expert_ids,
    gate_scores,
    w_gate,
    w_up,
    w_down,
):
    chips, experts, slots, padded = 8, 16, 12, 16
    units = w_gate.shape[1]
    block, model = prev_rows.shape
    width = model // chips
    count = experts * slots
    cache_len, latent = cache_latent.shape
    rope = cache_rope.shape[1]
    queries = q_nope.shape[0]
    heads, nope, _ = w_uk.shape
    value = w_uv.shape[2]
    top = expert_ids.shape[1]
    DMA = pltpu.SemaphoreType.DMA
    gate_own, up_own, down_own = w_gate[0], w_up[0], w_down[0]

    parts = call(
        prep_kernel,
        [pinned((units + queries, width))] * chips,
        (down_own, "h"),
        (slab_latent, "h"),
        (kv_gain.reshape(1, latent), "h"),
        (slab_rope, "h"),
        (cache_latent, "h"),
        (cache_rope, "h"),
        scratch=[
            pltpu.VMEM((queries, latent), bf16),
            pltpu.VMEM((1, latent), f32),
            pltpu.VMEM((queries, rope), bf16),
            pltpu.VMEM((cache_len, latent), bf16),
            pltpu.VMEM((cache_len, rope), bf16),
            DMA((5 + chips,)),
        ],
        size=4 << 20,
        name="prep",
    )

    def send(part, step):
        pairs = [
            (a * 4 + b, (a ^ step[0]) * 4 + (b + step[1]) % 4) for a in range(2) for b in range(4)
        ]
        return lax.ppermute(part, CHIPS, pairs)

    pieces = [parts[0]] + [send(part, step) for part, step in zip(parts[1:], STEPS[1:])]
    down_mine, keys_mine = call(
        join_kernel,
        [pinned((chips, units, width)), pinned((chips * queries, width))],
        *[(piece, "v") for piece in pieces],
        size=4 << 20,
        name="join",
    )

    outgoing, mix = call(
        functools.partial(route_kernel, experts=experts, slots=slots),
        [pinned((experts * padded, width)), pinned((3, experts * padded, block))],
        (after(expert_ids.T, parts[0]), "h"),
        (gate_scores.T, "h"),
        (prev_rows, "h"),
        scratch=[
            pltpu.VMEM((top, block), jnp.int32),
            pltpu.VMEM((top, block), f32),
            pltpu.VMEM((block, width), bf16),
            DMA((3,)),
        ],
        flops=2 * count * block * width,
        size=1 << 20,
        name="route",
    )
    arrived = exchange(outgoing, EXP)
    query = call(
        absorb_kernel,
        pinned((heads * queries, latent + rope)),
        (q_nope, "h"),
        (q_rope, "h"),
        (w_uk, "h"),
        scratch=[
            pltpu.VMEM(q_nope.shape, bf16),
            pltpu.VMEM(q_rope.shape, bf16),
            pltpu.VMEM(w_uk.shape, bf16),
            DMA((3,)),
        ],
        flops=2 * heads * queries * nope * latent,
        size=2 << 20,
        name="absorb",
    )
    own = call(
        functools.partial(compact_kernel, slots=slots, padded=padded),
        pinned((count, width)),
        (after(arrived, keys_mine, query), "v"),
        size=1 << 19,
        name="compact",
    )

    keys_far = lax.ppermute(keys_mine, "z", [(i, i ^ 1) for i in range(8)])
    down_theirs = lax.ppermute(down_mine, "c", SWAP)
    keys = [
        keys_mine,
        lax.ppermute(keys_mine, "c", SWAP),
        keys_far,
        lax.ppermute(keys_far, "c", SWAP),
    ]
    gate_swap, up_swap = after(gate_own, outgoing), after(up_own, outgoing)
    weights = call(
        stack_kernel,
        pinned((4 * units, model)),
        (gate_own, "h"),
        (lax.ppermute(gate_swap, "c", SWAP), "a"),
        (up_own, "h"),
        (lax.ppermute(up_swap, "c", SWAP), "a"),
        scratch=[DMA((4,))],
        size=8 << 20,
        name="stack",
    )

    across = lax.ppermute(own, "xl", SWAP)
    from_below = lax.ppermute(own, "y", UP)
    from_above = lax.ppermute(own, "y", DOWN)
    across_below = lax.ppermute(across, "y", UP)
    across_above = lax.ppermute(across, "y", DOWN)
    far = lax.ppermute(from_below, "y", UP)
    across_far = lax.ppermute(across_above, "y", DOWN)
    flops = 2 * count * width * 4 * units
    early = call(
        functools.partial(early_kernel, places=[(0, 0), (1, 0), (0, -1), (0, 1)]),
        pinned((4 * units, count), f32),
        *[(piece, "v") for piece in (own, across, from_below, from_above)],
        (weights, "v"),
        flops=4 * flops,
        size=3 << 20,
        name="early",
    )
    hidden = call(
        functools.partial(hidden_kernel, places=[(1, -1), (1, 1), (0, 2), (1, 2)]),
        pinned((chips, count // 2, 4 * units)),
        *[(piece, "v") for piece in (across_below, across_above, far, across_far)],
        (weights, "v"),
        (early, "v"),
        flops=4 * flops,
        size=3 << 20,
        name="hidden",
    )

    def attend(first, last, behind):
        return call(
            functools.partial(
                attend_kernel,
                first=first * queries,
                queries=queries,
                latent=latent,
                scale=(nope + rope) ** (-0.5),
            ),
            pinned(((last - first) * queries, latent)),
            (after(query, behind), "v"),
            *[(part, "v") for part in keys],
            flops=8 * (last - first) * queries * chips * queries * (2 * latent + rope),
            size=4 << 20,
            name="attend",
        )

    mixed_0 = attend(0, 4, hidden)
    produced = call(
        functools.partial(down_kernel, slots=slots, padded=padded),
        pinned((experts * padded, width)),
        (after(exchange(hidden, CHIPS), mixed_0), "v"),
        (down_mine, "v"),
        (down_theirs, "v"),
        flops=2 * count * chips * 2 * units * width,
        size=3 << 20,
        name="down",
    )
    mixed_1 = attend(4, 8, produced)
    attn = call(
        value_kernel,
        shape((queries, heads * value)),
        (mixed_0, "v"),
        (mixed_1, "v"),
        (w_uv, "h"),
        scratch=[pltpu.VMEM(w_uv.shape, bf16), DMA],
        flops=2 * heads * queries * latent * value,
        size=2 << 20,
        name="value",
    )
    keep, send_half = call(
        combine_kernel,
        [pinned((block, width // 2), f32), pinned((block, width // 2))],
        (mix, "v"),
        (after(exchange(produced, EXP), attn), "v"),
        flops=6 * count * block * width,
        size=1 << 19,
        name="combine",
    )
    moe_out = call(
        finish_kernel,
        shape((block, width // 2)),
        (keep, "v"),
        (lax.ppermute(send_half, "c", SWAP), "v"),
        name="finish",
    )
    return attn, moe_out


def solution(mesh):
    fine = Mesh(mesh.devices.reshape(2, 4, 2, 2, 8), SEQ + EXP)
    placed = (
        P(SEQ, EXP),
        P(SEQ, EXP),
        P(SEQ, None),
        P(SEQ, None),
        P(),
        P(SEQ, None),
        P(SEQ, None),
        P(EXP, None, None),
        P(EXP, None, None),
        P(EXP, None),
        P(EXP, None),
        P(EXP, None),
        P(EXP, SEQ, None),
        P(EXP, SEQ, None),
        P(EXP, SEQ, None),
    )
    return jax.shard_map(
        per_device,
        mesh=fine,
        in_specs=placed,
        out_specs=(P(SEQ, EXP), P(EXP, SEQ)),
        check_vma=False,
    )
```

time: 277 us -> 118 us (0.43)
  waiting for transfers between devices: 157 us -> 29.7 us
  local copies, waits for them, and re-layouts: 28.1 us -> 1.53 us
  Pallas kernels: 0 us -> 25.9 us
  starting transfers between devices: 36 us -> 58.8 us
  matrix products: 19.3 us -> 0 us
  other arithmetic: 19.3 us -> 0 us
  between operations: 14.5 us -> 0.79 us
    ppermute x10 -> x21, waiting for transfers between devices: 107 us -> 20.1 us  [the longest x7 13.3 us: send(): return lax.ppermute(part, CHIPS, pairs)]
    all_to_all x2 -> x3, waiting for transfers between devices: 49.7 us -> 9.61 us  [exchange(): return lax.all_to_all(x, axes, split_axis=0, concat_axis=0, tiled=True)]
    pallas_call x0 -> x14, Pallas kernels: none -> 25.9 us  [call(): pl.pallas_call(kernel, out_shape=out_shape, in_specs=[spec(spaces[space])...]
    ppermute x10 -> x21, starting transfers between devices: 16.7 us -> 36.6 us  [the longest x7 9.19 us: send(): return lax.ppermute(part, CHIPS, pairs)]
    dot_general x6 -> x0, matrix products: 19.3 us -> none  [the longest x1 4.51 us: per_device(): jnp.einsum('htc,hcv->thv', mixed_latent, w_uv, preferred_element_type=jnp...]
    reshape x7 -> x0, local copies, waits for them, and re-layouts: 9.55 us -> none  [the longest x1 7.12 us: combine_rows(): flat_results[local_slot].reshape(block_rows, top_count, column_count)]
    gather x3 -> x0, local copies, waits for them, and re-layouts: 8.35 us -> none  [the longest x1 4.78 us: combine_rows(): flat_results[local_slot].reshape(block_rows, top_count, column_count)]
    concatenate x4 -> x0, other arithmetic: 7.83 us -> none  [the longest x1 2.9 us: per_device(): unit_gate = jnp.concatenate([unit_gate, arrived_units[0]], axis=1)]
  transfers between devices with their start and end apart: 13 -> 24, of which waited for: 8 -> 10; matrix products, arithmetic and copies ran while one was open for 24% -> 0% of each run, Pallas kernels for 0% -> 16%
where the time goes in v1:
time: 118 us; the launch traced here: 117 us
  starting transfers between devices  58.8 us (50%)
  waiting for transfers between devices  29.7 us (25%)
  Pallas kernels  25.9 us (22%)
  local copies, waits for them, and re-layouts  1.53 us (1%)
    pallas_call x14, Pallas kernels, call(): pl.pallas_call(kernel, out_shape=out_shape, in_specs=[spec(spaces[space])...  25.9 us
    all_to_all x3, starting transfers between devices, exchange(): return lax.all_to_all(x, axes, split_axis=0, concat_axis=0, tiled=True)  22.3 us
    ppermute x7, waiting for transfers between devices, send(): return lax.ppermute(part, CHIPS, pairs)  13.3 us
    all_to_all x3, waiting for transfers between devices, exchange(): return lax.all_to_all(x, axes, split_axis=0, concat_axis=0, tiled=True)  9.61 us
    ppermute x7, starting transfers between devices, send(): return lax.ppermute(part, CHIPS, pairs)  9.19 us
    ppermute x1, starting transfers between devices, per_device(): down_theirs = lax.ppermute(down_mine, 'c', SWAP)  5.84 us
    ppermute x1, starting transfers between devices, per_device(): lax.ppermute(keys_far, 'c', SWAP)  3.58 us
    ppermute x1, starting transfers between devices, per_device(): lax.ppermute(gate_swap, 'c', SWAP)  3.58 us
  transfers between devices with their start and end apart: 24, of which 10 were waited for; matrix products, arithmetic and copies ran while one was open for 0% of the time, Pallas kernels for 16%

profile of v1, /device:TPU:3, one launch (start us, length us, event | category | flops | bytes accessed | tf_op | source)
XLA Modules:
  0.0 116.8 jit_solution(2030304502139450621)
XLA Ops:
  0.6 1.5 %prep.1 = (bf16[160,640]{1,0:T(8,128)(2,1)S(1)}, bf16[160,640]{1,0:T(8,128)(2,1)S(1)}, bf16[160,640]{1,0:T(8,128)(2,1)S(1)}, bf16[160,640]{1,0:T(8,128)(2,1)S(1)...) custom-call(bf16[96,5120]{1,0:T(8,128)(2,1)} %bitcast.12, ...), custom_call_target="tpu_custom_call" | custom-call | bytes 4194304 | tf_op jit(solution)/shard_map/prep/pallas_call | solution.py:302
  2.1 2.0 %route.1 = (bf16[256,640]{1,0:T(8,128)(2,1)}, bf16[3,256,48]{2,1,0:T(8,128)(2,1)S(1)}) custom-call(s32[6,48]{1,0:T(8,128)} %bitcast.17, f32[6,48]{1,0:T(8,128)} %bitcast.18, bf16[48,5120]{1,0:T(8,128)(2,1)} %rows_hbm.1), custom_call_target="tpu_custom_call" | custom-call | flops 11796480 | bytes 1048576 | tf_op jit(solution)/shard_map/route/pallas_call | solution.py:302
  4.9 9.9 %all-to-all-start = ((bf16[16,16,640]{2,1,0:T(8,128)(2,1)}), bf16[16,16,640]{2,1,0:T(8,128)(2,1)S(1)}, u32[]{:S(2)}, u32[]{:S(2)}) async-start(bf16[16,16,640]{2,1,0:T(8,128)(2,1)} %bitcast.4), calls=%async_computation | async-start | bytes 655360 | tf_op jit(solution)/shard_map/all_to_all | solution.py:319
  14.7 1.4 %collective-permute-start = (bf16[160,640]{1,0:T(8,128)(2,1)S(1)}, bf16[160,640]{1,0:T(8,128)(2,1)S(1)}, u32[]{:S(2)}, u32[]{:S(2)}) collective-permute-start(bf16[160,640]{1,0:T(8,128)(2,1)S(1)} %get-tuple-element.27), channel_id=1, source_target_pairs={{0,32},{32,64},{64,96},{96,0},{128,160},{160,192},{192,224},{224,1... | collective-permute-start | bytes 614408 | tf_op jit(solution)/shard_map/ppermute | solution.py:382
  16.1 2.6 %collective-permute-start.1 = (bf16[160,640]{1,0:T(8,128)(2,1)S(1)}, bf16[160,640]{1,0:T(8,128)(2,1)S(1)}, u32[]{:S(2)}, u32[]{:S(2)}) collective-permute-start(bf16[160,640]{1,0:T(8,128)(2,1)S(1)} %get-tuple-element.28), channel_id=1, source_target_pairs={{0,64},{32,96},{64,0},{96,32},{128,192},{160,224},{192,128},{224,1... | collective-permute-start | bytes 614408 | tf_op jit(solution)/shard_map/ppermute | solution.py:382
  19.8 1.2 collective-permute-start.3
  21.8 2.5 %collective-permute-start.5 = (bf16[160,640]{1,0:T(8,128)(2,1)S(1)}, bf16[160,640]{1,0:T(8,128)(2,1)S(1)}, u32[]{:S(2)}, u32[]{:S(2)}) collective-permute-start(bf16[160,640]{1,0:T(8,128)(2,1)S(1)} %get-tuple-element.32), channel_id=1, source_target_pairs={{0,192},{32,224},{64,128},{96,160},{128,64},{160,96},{192,0},{224,... | collective-permute-start | bytes 614408 | tf_op jit(solution)/shard_map/ppermute | solution.py:382
  24.3 2.9 %collective-permute-done.1.refs_2_ = bf16[160,640]{1,0:T(8,128)(2,1)S(1)} collective-permute-done((bf16[160,640]{1,0:T(8,128)(2,1)S(1)}, bf16[160,640]{1,0:T(8,128)(2,1)S(1)}, u32[]{:S(2)}, u32[]{:S(2)}) %collective-permute-start.1) | collective-permute-done | bytes 204832 | tf_op jit(solution)/shard_map/ppermute | solution.py:382
  27.3 3.6 %collective-permute-start.13 = (bf16[96,5120]{1,0:T(8,128)(2,1)}, bf16[96,5120]{1,0:T(8,128)(2,1)S(1)}, u32[]{:S(2)}, u32[]{:S(2)}) collective-permute-start(bf16[96,5120]{1,0:T(8,128)(2,1)} %bitcast.13), channel_id=1, source_target_pairs={{0,16},{16,0},{1,17},{17,1},{2,18},{18,2},{3,19},{19,3},{4,20},{20... | collective-permute-start | bytes 2949128 | tf_op jit(solution)/shard_map/ppermute | solution.py:447
  30.9 1.6 %collective-permute-done.4.refs_5_ = bf16[160,640]{1,0:T(8,128)(2,1)S(1)} collective-permute-done((bf16[160,640]{1,0:T(8,128)(2,1)S(1)}, bf16[160,640]{1,0:T(8,128)(2,1)S(1)}, u32[]{:S(2)}, u32[]{:S(2)}) %collective-permute-start.4) | collective-permute-done | bytes 204832 | tf_op jit(solution)/shard_map/ppermute | solution.py:382
  32.5 4.5 %collective-permute-done.5.refs_6_ = bf16[160,640]{1,0:T(8,128)(2,1)S(1)} collective-permute-done((bf16[160,640]{1,0:T(8,128)(2,1)S(1)}, bf16[160,640]{1,0:T(8,128)(2,1)S(1)}, u32[]{:S(2)}, u32[]{:S(2)}) %collective-permute-start.5) | collective-permute-done | bytes 204832 | tf_op jit(solution)/shard_map/ppermute | solution.py:382
  37.0 3.9 %collective-permute-done.6.refs_7_ = bf16[160,640]{1,0:T(8,128)(2,1)S(1)} collective-permute-done((bf16[160,640]{1,0:T(8,128)(2,1)S(1)}, bf16[160,640]{1,0:T(8,128)(2,1)S(1)}, u32[]{:S(2)}, u32[]{:S(2)}) %collective-permute-start.6) | collective-permute-done | bytes 204832 | tf_op jit(solution)/shard_map/ppermute | solution.py:382
  42.7 1.7 %absorb.1.query_ref = bf16[512,576]{1,0:T(8,128)(2,1)S(1)} custom-call(bf16[64,1024]{1,0:T(8,128)(2,1)} %nope_hbm.1, bf16[64,512]{1,0:T(8,128)(2,1)} %rope_hbm.1, bf16[8,128,512]{2,1,0:T(8,128)(2,1)} %uk_hbm.1), custom_call_target="tpu_custom_call" | custom-call | flops 67108864 | bytes 2097152 | tf_op jit(solution)/shard_map/absorb/pallas_call | solution.py:302
  45.9 1.8 %collective-permute-start.10 = (bf16[192,640]{1,0:T(8,128)(2,1)S(1)}, bf16[192,640]{1,0:T(8,128)(2,1)S(1)}, u32[]{:S(2)}, u32[]{:S(2)}) collective-permute-start(bf16[192,640]{1,0:T(8,128)(2,1)S(1)} %compact.1.refs_0_), channel_id=1, source_target_pairs={{0,32},{32,64},{64,96},{96,0},{1,33},{33,65},{65,97},{97,1},{2,34}... | collective-permute-start | bytes 737288 | tf_op jit(solution)/shard_map/ppermute | solution.py:456
  47.7 3.3 %collective-permute-done.7.refs_1_ = bf16[192,640]{1,0:T(8,128)(2,1)S(1)} collective-permute-done((bf16[192,640]{1,0:T(8,128)(2,1)S(1)}, bf16[192,640]{1,0:T(8,128)(2,1)S(1)}, u32[]{:S(2)}, u32[]{:S(2)}) %collective-permute-start.7) | collective-permute-done | bytes 245792 | tf_op jit(solution)/shard_map/ppermute | solution.py:455
  51.0 1.8 %collective-permute-start.15 = (bf16[192,640]{1,0:T(8,128)(2,1)S(1)}, bf16[192,640]{1,0:T(8,128)(2,1)S(1)}, u32[]{:S(2)}, u32[]{:S(2)}) collective-permute-start(bf16[192,640]{1,0:T(8,128)(2,1)S(1)} %compact.1.refs_0_), channel_id=1, source_target_pairs={{0,96},{32,0},{64,32},{96,64},{1,97},{33,1},{65,33},{97,65},{2,98}... | collective-permute-start | bytes 737288 | tf_op jit(solution)/shard_map/ppermute | solution.py:457
  53.9 2.6 %collective-permute-done.15.refs_3_ = bf16[192,640]{1,0:T(8,128)(2,1)S(1)} collective-permute-done((bf16[192,640]{1,0:T(8,128)(2,1)S(1)}, bf16[192,640]{1,0:T(8,128)(2,1)S(1)}, u32[]{:S(2)}, u32[]{:S(2)}) %collective-permute-start.15) | collective-permute-done | bytes 245792 | tf_op jit(solution)/shard_map/ppermute | solution.py:457
  57.3 5.8 %collective-permute-start.19 = (bf16[8,96,640]{2,1,0:T(8,128)(2,1)S(1)}, bf16[8,96,640]{2,1,0:T(8,128)(2,1)}, u32[]{:S(2)}, u32[]{:S(2)}) collective-permute-start(bf16[8,96,640]{2,1,0:T(8,128)(2,1)S(1)} %get-tuple-element.40.own_ref), channel_id=1, source_target_pairs={{0,16},{16,0},{1,17},{17,1},{2,18},{18,2},{3,19},{19,3},{4,20},{20... | collective-permute-start | bytes 2949128 | tf_op jit(solution)/shard_map/ppermute | solution.py:435
  63.7 2.1 %collective-permute-start.12 = (bf16[192,640]{1,0:T(8,128)(2,1)S(1)}, bf16[192,640]{1,0:T(8,128)(2,1)S(1)}, u32[]{:S(2)}, u32[]{:S(2)}) collective-permute-start(bf16[192,640]{1,0:T(8,128)(2,1)S(1)} %collective-permute-done.9.refs_1_), channel_id=1, source_target_pairs={{0,96},{32,0},{64,32},{96,64},{1,97},{33,1},{65,33},{97,65},{2,98}... | collective-permute-start | bytes 737288 | tf_op jit(solution)/shard_map/ppermute | solution.py:461
  65.9 2.1 %collective-permute-start.16 = (bf16[512,640]{1,0:T(8,128)(2,1)}, bf16[512,640]{1,0:T(8,128)(2,1)}, u32[]{:S(2)}, u32[]{:S(2)}) collective-permute-start(bf16[512,640]{1,0:T(8,128)(2,1)} %get-tuple-element.34.refs_0_), channel_id=1, source_target_pairs={{0,16},{16,0},{1,17},{17,1},{2,18},{18,2},{3,19},{19,3},{4,20},{20... | collective-permute-start | bytes 1966088 | tf_op jit(solution)/shard_map/ppermute | solution.py:438
  68.0 3.6 %collective-permute-start.18 = (bf16[512,640]{1,0:T(8,128)(2,1)}, bf16[512,640]{1,0:T(8,128)(2,1)}, u32[]{:S(2)}, u32[]{:S(2)}) collective-permute-start(bf16[512,640]{1,0:T(8,128)(2,1)} %collective-permute-done.17.refs_2_), channel_id=1, source_target_pairs={{0,16},{16,0},{1,17},{17,1},{2,18},{18,2},{3,19},{19,3},{4,20},{20... | collective-permute-start | bytes 1966088 | tf_op jit(solution)/shard_map/ppermute | solution.py:440
  71.5 1.6 %stack.1.refs_4_ = bf16[384,5120]{1,0:T(8,128)(2,1)S(1)} custom-call(bf16[96,5120]{1,0:T(8,128)(2,1)} %bitcast.14, bf16[96,5120]{1,0:T(8,128)(2,1)S(1)} %collective-permute-done.13.gate_other, bf16[96,5120]{1,0:T(8,128)(2,1)} %bitcast.16, bf16[96,5120]{1,0:T(8,128)(2,1)S(1)} %collective-permute-done.14.up_other), custom_call_target="tpu_custom_call" | custom-call | bytes 8388608 | tf_op jit(solution)/shard_map/stack/pallas_call | solution.py:302
  74.0 1.8 %hidden.1 = bf16[8,96,384]{2,1,0:T(8,128)(2,1)} custom-call(bf16[192,640]{1,0:T(8,128)(2,1)S(1)} %collective-permute-done.8.refs_0_, bf16[192,640]{1,0:T(8,128)(2,1)S(1)} %collective-permute-done.9.refs_1_, bf16[192,640]{1,0:T(8,128)(2,1)S(1)} %collective-permute-done.11.refs_2_, bf16[192,640]{1,0:T(8,128)(2,1)S(1)} %collective-permute-done.12.refs_3_, ...), custom_call_target="tpu_custom_call" | custom-call | flops 377487360 | bytes 3145728 | tf_op jit(solution)/shard_map/hidden/pallas_call | solution.py:302
  75.8 4.6 %all-to-all-start.1 = ((bf16[8,96,384]{2,1,0:T(8,128)(2,1)}), bf16[8,96,384]{2,1,0:T(8,128)(2,1)S(1)}, u32[]{:S(2)}, u32[]{:S(2)}) async-start(bf16[8,96,384]{2,1,0:T(8,128)(2,1)} %hidden.1), calls=%async_computation.1 | async-start | bytes 1179648 | tf_op jit(solution)/shard_map/all_to_all | solution.py:319
  80.4 4.6 %attend.2.refs_0_ = bf16[256,512]{1,0:T(8,128)(2,1)S(1)} custom-call(bf16[512,576]{1,0:T(8,128)(2,1)S(1)} %copy-done.1, bf16[512,640]{1,0:T(8,128)(2,1)} %get-tuple-element.34.refs_0_, bf16[512,640]{1,0:T(8,128)(2,1)} %collective-permute-done.16.refs_1_, bf16[512,640]{1,0:T(8,128)(2,1)} %collective-permute-done.17.refs_2_, ...), custom_call_target="tpu_custom_call" | custom-call | flops 1140850688 | bytes 4194304 | tf_op jit(solution)/shard_map/attend/pallas_call | solution.py:302
  85.0 5.2 %all-to-all-done.1.hidden_ref = bf16[8,96,384]{2,1,0:T(8,128)(2,1)S(1)} async-done(((bf16[8,96,384]{2,1,0:T(8,128)(2,1)}), bf16[8,96,384]{2,1,0:T(8,128)(2,1)S(1)}, u32[]{:S(2)}, u32[]{:S(2)}) %all-to-all-start.1) | async-done | bytes 589856 | tf_op jit(solution)/shard_map/all_to_all | solution.py:319
  90.2 2.9 %down.1 = bf16[256,640]{1,0:T(8,128)(2,1)} custom-call(bf16[8,96,384]{2,1,0:T(8,128)(2,1)S(1)} %all-to-all-done.1.hidden_ref, bf16[8,96,640]{2,1,0:T(8,128)(2,1)S(1)} %get-tuple-element.40.own_ref, bf16[8,96,640]{2,1,0:T(8,128)(2,1)} %collective-permute-done.19.other_ref), custom_call_target="tpu_custom_call" | custom-call | flops 377487360 | bytes 3145728 | tf_op jit(solution)/shard_map/down/pallas_call | solution.py:302
  93.1 7.8 %all-to-all-start.2 = ((bf16[16,16,640]{2,1,0:T(8,128)(2,1)}), bf16[16,16,640]{2,1,0:T(8,128)(2,1)S(1)}, u32[]{:S(2)}, u32[]{:S(2)}) async-start(bf16[16,16,640]{2,1,0:T(8,128)(2,1)} %bitcast.8), calls=%async_computation.2 | async-start | bytes 655360 | tf_op jit(solution)/shard_map/all_to_all | solution.py:319
  100.9 4.6 %attend.3.refs_1_ = bf16[256,512]{1,0:T(8,128)(2,1)S(1)} custom-call(bf16[512,576]{1,0:T(8,128)(2,1)S(1)} %copy-done.1, bf16[512,640]{1,0:T(8,128)(2,1)} %get-tuple-element.34.refs_0_, bf16[512,640]{1,0:T(8,128)(2,1)} %collective-permute-done.16.refs_1_, bf16[512,640]{1,0:T(8,128)(2,1)} %collective-permute-done.17.refs_2_, ...), custom_call_target="tpu_custom_call" | custom-call | flops 1140850688 | bytes 4194304 | tf_op jit(solution)/shard_map/attend/pallas_call | solution.py:302
  105.5 2.2 %value.1 = bf16[64,1024]{1,0:T(8,128)(2,1)} custom-call(bf16[256,512]{1,0:T(8,128)(2,1)S(1)} %attend.2.refs_0_, bf16[256,512]{1,0:T(8,128)(2,1)S(1)} %attend.3.refs_1_, bf16[8,512,128]{2,1,0:T(8,128)(2,1)} %refs_2_.1), custom_call_target="tpu_custom_call" | custom-call | flops 67108864 | bytes 2097152 | tf_op jit(solution)/shard_map/value/pallas_call | solution.py:302
  107.7 4.4 %all-to-all-done.2 = bf16[16,16,640]{2,1,0:T(8,128)(2,1)S(1)} async-done(((bf16[16,16,640]{2,1,0:T(8,128)(2,1)}), bf16[16,16,640]{2,1,0:T(8,128)(2,1)S(1)}, u32[]{:S(2)}, u32[]{:S(2)}) %all-to-all-start.2) | async-done | bytes 327712 | tf_op jit(solution)/shard_map/all_to_all | solution.py:319
  112.5 2.7 %collective-permute-start.20 = (bf16[48,320]{1,0:T(8,128)(2,1)S(1)}, bf16[48,320]{1,0:T(8,128)(2,1)S(1)}, u32[]{:S(2)}, u32[]{:S(2)}) collective-permute-start(bf16[48,320]{1,0:T(8,128)(2,1)S(1)} %get-tuple-element.45), channel_id=1, source_target_pairs={{0,16},{16,0},{1,17},{17,1},{2,18},{18,2},{3,19},{19,3},{4,20},{20... | collective-permute-start | bytes 92168 | tf_op jit(solution)/shard_map/ppermute | solution.py:536
  (38 shorter events, 11.2 us)
Async XLA Ops:
  4.2 0.7 copy-start.2
  4.9 40.4 %all-to-all-start = ((bf16[16,16,640]{2,1,0:T(8,128)(2,1)}), bf16[16,16,640]{2,1,0:T(8,128)(2,1)S(1)}, u32[]{:S(2)}, u32[]{:S(2)}) async-start(bf16[16,16,640]{2,1,0:T(8,128)(2,1)} %bitcast.4), calls=%async_computation | async-start | bytes 655360 | tf_op jit(solution)/shard_map/all_to_all | solution.py:319
  14.7 7.0 %collective-permute-start = (bf16[160,640]{1,0:T(8,128)(2,1)S(1)}, bf16[160,640]{1,0:T(8,128)(2,1)S(1)}, u32[]{:S(2)}, u32[]{:S(2)}) collective-permute-start(bf16[160,640]{1,0:T(8,128)(2,1)S(1)} %get-tuple-element.27), channel_id=1, source_target_pairs={{0,32},{32,64},{64,96},{96,0},{128,160},{160,192},{192,224},{224,1... | collective-permute-start | bytes 614408 | tf_op jit(solution)/shard_map/ppermute | solution.py:382
  16.1 11.2 %collective-permute-start.1 = (bf16[160,640]{1,0:T(8,128)(2,1)S(1)}, bf16[160,640]{1,0:T(8,128)(2,1)S(1)}, u32[]{:S(2)}, u32[]{:S(2)}) collective-permute-start(bf16[160,640]{1,0:T(8,128)(2,1)S(1)} %get-tuple-element.28), channel_id=1, source_target_pairs={{0,64},{32,96},{64,0},{96,32},{128,192},{160,224},{192,128},{224,1... | collective-permute-start | bytes 614408 | tf_op jit(solution)/shard_map/ppermute | solution.py:382
  18.7 8.5 %collective-permute-start.2 = (bf16[160,640]{1,0:T(8,128)(2,1)S(1)}, bf16[160,640]{1,0:T(8,128)(2,1)S(1)}, u32[]{:S(2)}, u32[]{:S(2)}) collective-permute-start(bf16[160,640]{1,0:T(8,128)(2,1)S(1)} %get-tuple-element.29), channel_id=1, source_target_pairs={{0,96},{32,0},{64,32},{96,64},{128,224},{160,128},{192,160},{224,1... | collective-permute-start | bytes 614408 | tf_op jit(solution)/shard_map/ppermute | solution.py:382
  19.8 11.1 %collective-permute-start.3 = (bf16[160,640]{1,0:T(8,128)(2,1)S(1)}, bf16[160,640]{1,0:T(8,128)(2,1)S(1)}, u32[]{:S(2)}, u32[]{:S(2)}) collective-permute-start(bf16[160,640]{1,0:T(8,128)(2,1)S(1)} %get-tuple-element.30), channel_id=1, source_target_pairs={{0,128},{32,160},{64,192},{96,224},{128,0},{160,32},{192,64},{224,... | collective-permute-start | bytes 614408 | tf_op jit(solution)/shard_map/ppermute | solution.py:382
  20.9 11.6 %collective-permute-start.4 = (bf16[160,640]{1,0:T(8,128)(2,1)S(1)}, bf16[160,640]{1,0:T(8,128)(2,1)S(1)}, u32[]{:S(2)}, u32[]{:S(2)}) collective-permute-start(bf16[160,640]{1,0:T(8,128)(2,1)S(1)} %get-tuple-element.31), channel_id=1, source_target_pairs={{0,160},{32,192},{64,224},{96,128},{128,32},{160,64},{192,96},{224... | collective-permute-start | bytes 614408 | tf_op jit(solution)/shard_map/ppermute | solution.py:382
  21.8 15.3 %collective-permute-start.5 = (bf16[160,640]{1,0:T(8,128)(2,1)S(1)}, bf16[160,640]{1,0:T(8,128)(2,1)S(1)}, u32[]{:S(2)}, u32[]{:S(2)}) collective-permute-start(bf16[160,640]{1,0:T(8,128)(2,1)S(1)} %get-tuple-element.32), channel_id=1, source_target_pairs={{0,192},{32,224},{64,128},{96,160},{128,64},{160,96},{192,0},{224,... | collective-permute-start | bytes 614408 | tf_op jit(solution)/shard_map/ppermute | solution.py:382
  27.2 13.7 %collective-permute-start.6 = (bf16[160,640]{1,0:T(8,128)(2,1)S(1)}, bf16[160,640]{1,0:T(8,128)(2,1)S(1)}, u32[]{:S(2)}, u32[]{:S(2)}) collective-permute-start(bf16[160,640]{1,0:T(8,128)(2,1)S(1)} %get-tuple-element.33), channel_id=1, source_target_pairs={{0,224},{32,128},{64,160},{96,192},{128,96},{160,0},{192,32},{224,... | collective-permute-start | bytes 614408 | tf_op jit(solution)/shard_map/ppermute | solution.py:382
  27.3 35.9 %collective-permute-start.13 = (bf16[96,5120]{1,0:T(8,128)(2,1)}, bf16[96,5120]{1,0:T(8,128)(2,1)S(1)}, u32[]{:S(2)}, u32[]{:S(2)}) collective-permute-start(bf16[96,5120]{1,0:T(8,128)(2,1)} %bitcast.13), channel_id=1, source_target_pairs={{0,16},{16,0},{1,17},{17,1},{2,18},{18,2},{3,19},{19,3},{4,20},{20... | collective-permute-start | bytes 2949128 | tf_op jit(solution)/shard_map/ppermute | solution.py:447
  30.8 35.0 %collective-permute-start.14 = (bf16[96,5120]{1,0:T(8,128)(2,1)}, bf16[96,5120]{1,0:T(8,128)(2,1)S(1)}, u32[]{:S(2)}, u32[]{:S(2)}) collective-permute-start(bf16[96,5120]{1,0:T(8,128)(2,1)} %bitcast.15), channel_id=1, source_target_pairs={{0,16},{16,0},{1,17},{17,1},{2,18},{18,2},{3,19},{19,3},{4,20},{20... | collective-permute-start | bytes 2949128 | tf_op jit(solution)/shard_map/ppermute | solution.py:449
  41.9 15.4 %collective-permute-start.17 = (bf16[512,640]{1,0:T(8,128)(2,1)}, bf16[512,640]{1,0:T(8,128)(2,1)}, u32[]{:S(2)}, u32[]{:S(2)}) collective-permute-start(bf16[512,640]{1,0:T(8,128)(2,1)} %get-tuple-element.34.refs_0_), channel_id=1, source_target_pairs={{0,1},{1,0},{2,3},{3,2},{4,5},{5,4},{6,7},{7,6},{8,9},{9,8},{10,11... | collective-permute-start | bytes 1966088 | tf_op jit(solution)/shard_map/ppermute | solution.py:434
  44.4 0.8 copy-start
  45.4 5.5 %collective-permute-start.7 = (bf16[192,640]{1,0:T(8,128)(2,1)S(1)}, bf16[192,640]{1,0:T(8,128)(2,1)S(1)}, u32[]{:S(2)}, u32[]{:S(2)}) collective-permute-start(bf16[192,640]{1,0:T(8,128)(2,1)S(1)} %compact.1.refs_0_), channel_id=1, source_target_pairs={{0,128},{128,0},{1,129},{129,1},{2,130},{130,2},{3,131},{131,3},{4... | collective-permute-start | bytes 737288 | tf_op jit(solution)/shard_map/ppermute | solution.py:455
  45.9 7.0 %collective-permute-start.10 = (bf16[192,640]{1,0:T(8,128)(2,1)S(1)}, bf16[192,640]{1,0:T(8,128)(2,1)S(1)}, u32[]{:S(2)}, u32[]{:S(2)}) collective-permute-start(bf16[192,640]{1,0:T(8,128)(2,1)S(1)} %compact.1.refs_0_), channel_id=1, source_target_pairs={{0,32},{32,64},{64,96},{96,0},{1,33},{33,65},{65,97},{97,1},{2,34}... | collective-permute-start | bytes 737288 | tf_op jit(solution)/shard_map/ppermute | solution.py:456
  51.0 5.4 %collective-permute-start.15 = (bf16[192,640]{1,0:T(8,128)(2,1)S(1)}, bf16[192,640]{1,0:T(8,128)(2,1)S(1)}, u32[]{:S(2)}, u32[]{:S(2)}) collective-permute-start(bf16[192,640]{1,0:T(8,128)(2,1)S(1)} %compact.1.refs_0_), channel_id=1, source_target_pairs={{0,96},{32,0},{64,32},{96,64},{1,97},{33,1},{65,33},{97,65},{2,98}... | collective-permute-start | bytes 737288 | tf_op jit(solution)/shard_map/ppermute | solution.py:457
  52.8 10.9 %collective-permute-start.9 = (bf16[192,640]{1,0:T(8,128)(2,1)S(1)}, bf16[192,640]{1,0:T(8,128)(2,1)S(1)}, u32[]{:S(2)}, u32[]{:S(2)}) collective-permute-start(bf16[192,640]{1,0:T(8,128)(2,1)S(1)} %collective-permute-done.7.refs_1_), channel_id=1, source_target_pairs={{0,96},{32,0},{64,32},{96,64},{1,97},{33,1},{65,33},{97,65},{2,98}... | collective-permute-start | bytes 737288 | tf_op jit(solution)/shard_map/ppermute | solution.py:459
  56.4 11.5 %collective-permute-start.8 = (bf16[192,640]{1,0:T(8,128)(2,1)S(1)}, bf16[192,640]{1,0:T(8,128)(2,1)S(1)}, u32[]{:S(2)}, u32[]{:S(2)}) collective-permute-start(bf16[192,640]{1,0:T(8,128)(2,1)S(1)} %collective-permute-done.7.refs_1_), channel_id=1, source_target_pairs={{0,32},{32,64},{64,96},{96,0},{1,33},{33,65},{65,97},{97,1},{2,34}... | collective-permute-start | bytes 737288 | tf_op jit(solution)/shard_map/ppermute | solution.py:458
  57.3 32.8 %collective-permute-start.19 = (bf16[8,96,640]{2,1,0:T(8,128)(2,1)S(1)}, bf16[8,96,640]{2,1,0:T(8,128)(2,1)}, u32[]{:S(2)}, u32[]{:S(2)}) collective-permute-start(bf16[8,96,640]{2,1,0:T(8,128)(2,1)S(1)} %get-tuple-element.40.own_ref), channel_id=1, source_target_pairs={{0,16},{16,0},{1,17},{17,1},{2,18},{18,2},{3,19},{19,3},{4,20},{20... | collective-permute-start | bytes 2949128 | tf_op jit(solution)/shard_map/ppermute | solution.py:435
  63.2 10.8 %collective-permute-start.11 = (bf16[192,640]{1,0:T(8,128)(2,1)S(1)}, bf16[192,640]{1,0:T(8,128)(2,1)S(1)}, u32[]{:S(2)}, u32[]{:S(2)}) collective-permute-start(bf16[192,640]{1,0:T(8,128)(2,1)S(1)} %collective-permute-done.10.refs_2_), channel_id=1, source_target_pairs={{0,32},{32,64},{64,96},{96,0},{1,33},{33,65},{65,97},{97,1},{2,34}... | collective-permute-start | bytes 737288 | tf_op jit(solution)/shard_map/ppermute | solution.py:460
  63.7 10.3 %collective-permute-start.12 = (bf16[192,640]{1,0:T(8,128)(2,1)S(1)}, bf16[192,640]{1,0:T(8,128)(2,1)S(1)}, u32[]{:S(2)}, u32[]{:S(2)}) collective-permute-start(bf16[192,640]{1,0:T(8,128)(2,1)S(1)} %collective-permute-done.9.refs_1_), channel_id=1, source_target_pairs={{0,96},{32,0},{64,32},{96,64},{1,97},{33,1},{65,33},{97,65},{2,98}... | collective-permute-start | bytes 737288 | tf_op jit(solution)/shard_map/ppermute | solution.py:461
  65.9 14.6 %collective-permute-start.16 = (bf16[512,640]{1,0:T(8,128)(2,1)}, bf16[512,640]{1,0:T(8,128)(2,1)}, u32[]{:S(2)}, u32[]{:S(2)}) collective-permute-start(bf16[512,640]{1,0:T(8,128)(2,1)} %get-tuple-element.34.refs_0_), channel_id=1, source_target_pairs={{0,16},{16,0},{1,17},{17,1},{2,18},{18,2},{3,19},{19,3},{4,20},{20... | collective-permute-start | bytes 1966088 | tf_op jit(solution)/shard_map/ppermute | solution.py:438
  68.0 12.5 %collective-permute-start.18 = (bf16[512,640]{1,0:T(8,128)(2,1)}, bf16[512,640]{1,0:T(8,128)(2,1)}, u32[]{:S(2)}, u32[]{:S(2)}) collective-permute-start(bf16[512,640]{1,0:T(8,128)(2,1)} %collective-permute-done.17.refs_2_), channel_id=1, source_target_pairs={{0,16},{16,0},{1,17},{17,1},{2,18},{18,2},{3,19},{19,3},{4,20},{20... | collective-permute-start | bytes 1966088 | tf_op jit(solution)/shard_map/ppermute | solution.py:440
  74.0 6.5 %copy-start.1 = (bf16[512,576]{1,0:T(8,128)(2,1)S(1)}, bf16[512,576]{1,0:T(8,128)(2,1)}, u32[]{:S(2)}) copy-start(bf16[512,576]{1,0:T(8,128)(2,1)} %copy-done) | copy-start | bytes 1769476
  75.8 14.4 %all-to-all-start.1 = ((bf16[8,96,384]{2,1,0:T(8,128)(2,1)}), bf16[8,96,384]{2,1,0:T(8,128)(2,1)S(1)}, u32[]{:S(2)}, u32[]{:S(2)}) async-start(bf16[8,96,384]{2,1,0:T(8,128)(2,1)} %hidden.1), calls=%async_computation.1 | async-start | bytes 1179648 | tf_op jit(solution)/shard_map/all_to_all | solution.py:319
  93.1 19.0 %copy-start.3 = (bf16[3,256,48]{2,1,0:T(8,128)(2,1)S(1)}, bf16[3,256,48]{2,1,0:T(8,128)(2,1)}, u32[]{:S(2)}) copy-start(bf16[3,256,48]{2,1,0:T(8,128)(2,1)} %copy-done.2) | copy-start | bytes 221188
  93.1 19.0 %all-to-all-start.2 = ((bf16[16,16,640]{2,1,0:T(8,128)(2,1)}), bf16[16,16,640]{2,1,0:T(8,128)(2,1)S(1)}, u32[]{:S(2)}, u32[]{:S(2)}) async-start(bf16[16,16,640]{2,1,0:T(8,128)(2,1)} %bitcast.8), calls=%async_computation.2 | async-start | bytes 655360 | tf_op jit(solution)/shard_map/all_to_all | solution.py:319
  112.5 3.6 %collective-permute-start.20 = (bf16[48,320]{1,0:T(8,128)(2,1)S(1)}, bf16[48,320]{1,0:T(8,128)(2,1)S(1)}, u32[]{:S(2)}, u32[]{:S(2)}) collective-permute-start(bf16[48,320]{1,0:T(8,128)(2,1)S(1)} %get-tuple-element.45), channel_id=1, source_target_pairs={{0,16},{16,0},{1,17},{17,1},{2,18},{18,2},{3,19},{19,3},{4,20},{20... | collective-permute-start | bytes 92168 | tf_op jit(solution)/shard_map/ppermute | solution.py:536

commit v2 on v1

--- a/solution.py
+++ b/solution.py
@@ -42,64 +42,41 @@
         copy.wait()
 
 
-STEPS = [(dx, dy) for dx in range(2) for dy in range(4)]
+EARLY = [(0, 0), (1, 0), (0, -1), (0, 1)]
+LATE = [(1, -1), (1, 1), (0, 2), (1, 2)]
 
 
 def chip_at(dx, dy):
     return (lax.axis_index("xl") ^ dx) * 4 + ((lax.axis_index("y") + dy) & 3)
 
 
-def prep_kernel(down_ref, latent_ref, gain_ref, rope_ref, cache_ref, cache_rope_ref, *refs):
-    out_refs, (latent, gain, rope, cache, cache_rope, sems) = refs[:-6], refs[-6:]
-    units = down_ref.shape[0]
-    width = out_refs[0].shape[1]
-    small = start_all(
-        [
-            (latent_ref, latent),
-            (gain_ref, gain),
-            (rope_ref, rope),
-            (cache_ref, cache),
-            (cache_rope_ref, cache_rope),
-        ],
-        [sems.at[i] for i in range(5)],
-    )
-    large = start_all(
-        [
-            (
-                down_ref.at[:, pl.ds(pl.multiple_of(chip_at(*step) * width, 128), width)],
-                ref.at[pl.ds(0, units)],
-            )
-            for step, ref in zip(STEPS, out_refs)
-        ],
-        [sems.at[5 + i] for i in range(len(out_refs))],
-    )
-    wait_all(small)
+def prep_kernel(latent_ref, gain_ref, rope_ref, cache_ref, cache_rope_ref, out_ref, *scratch):
+    *held, sems = scratch
+    hbm = (latent_ref, gain_ref, rope_ref, cache_ref, cache_rope_ref)
+    wait_all(start_all(list(zip(hbm, held)), [sems.at[i] for i in range(5)]))
+    latent, gain, rope, cache, cache_rope = held
     slab = latent_norm(latent[...], gain[...])
     count, key_width = cache.shape[0], cache.shape[1] + rope.shape[1]
-    blank = jnp.zeros((count, width - key_width), bf16)
-    top = jnp.concatenate([cache[...], cache_rope[...], blank], axis=1)
-    low = jnp.concatenate([slab, rope[...], blank], axis=1)
-    keys = jnp.where(lax.axis_index("z") % 2 == 0, top, low)
-    for ref in out_refs:
-        ref[units:] = keys
-    wait_all(large)
-
-
-def join_kernel(*refs):
-    *piece_refs, down_ref, keys_ref = refs
-    units = down_ref.shape[1]
-    count = piece_refs[0].shape[0] - units
-    for (dx, dy), ref in zip(STEPS, piece_refs):
-        j = chip_at(dx, -dy)
-        down_ref[j] = ref[:units]
-        keys_ref[pl.ds(pl.multiple_of(j * count, count), count), :] = ref[units:]
+    blank = jnp.zeros((count, out_ref.shape[1] - key_width), bf16)
+    out_ref[:count] = jnp.concatenate([cache[...], cache_rope[...], blank], axis=1)
+    out_ref[count:] = jnp.concatenate([slab, rope[...], blank], axis=1)
+
+
+def join_kernel(*refs, places):
+    *piece_refs, keys_ref = refs
+    count = piece_refs[0].shape[0] // 2
+    for place, ref in zip(places, piece_refs):
+        row = pl.multiple_of(chip_at(*place) * count, count)
+        keys_ref[pl.ds(row, count), :] = ref[:count]
+        keys_ref[pl.ds(row + len(places) * count, count), :] = ref[count:]
 
 
 def route_kernel(
     ids_hbm, gates_hbm, rows_hbm, out_ref, mix_ref, ids, gates, held, sems, *, experts, slots
 ):
     chip, core = chip_at(0, 0), lax.axis_index("c")
-    total, width = out_ref.shape
+    total = mix_ref.shape[1]
+    width = out_ref.shape[2]
     padded = total // experts
     top, block = ids.shape
     copies = start_all(
@@ -137,32 +114,27 @@
         rest = rest - piece.astype(f32)
         mix_ref[part] = jnp.where(take, mm(spread, piece), 0.0).astype(bf16)
     wait_all(copies[2:])
-    out_ref[...] = mm(jnp.where(take, 1.0, 0.0).astype(bf16), held[...]).astype(bf16)
-
-
-def slot_rows(slots, padded, count, transposed=False):
-    shape = (count // slots * padded, count) if transposed else (count, count // slots * padded)
-    small = lax.broadcasted_iota(jnp.int32, shape, 1 if transposed else 0)
-    large = lax.broadcasted_iota(jnp.int32, shape, 0 if transposed else 1)
-    return jnp.where(small + small // slots * (padded - slots) == large, 1.0, 0.0).astype(bf16)
-
-
-def compact_kernel(rows_ref, *refs, slots, padded):
-    out_ref = refs[-1]
-    out_ref[...] = mm(slot_rows(slots, padded, out_ref.shape[0]), rows_ref[...]).astype(bf16)
-
-
-def stack_kernel(gate_own, gate_other, up_own, up_other, out_ref, sems):
+    rows = mm(jnp.where(take, 1.0, 0.0).astype(bf16), held[...]).astype(bf16)
+    for e in range(experts):
+        out_ref[e] = rows[e * padded : e * padded + slots]
+
+
+def compact_kernel(rows_ref, out_ref):
+    out_ref[...] = jnp.concatenate(
+        [rows_ref[e].astype(f32) for e in range(rows_ref.shape[0])], axis=0
+    ).astype(bf16)
+
+
+def stack_kernel(gate_own, gate_other, up_own, up_other, down_own, down_other, *refs):
+    in_ref, down_ref, sems = refs
     units = gate_own.shape[0]
-    wait_all(
-        start_all(
-            [
-                (ref, out_ref.at[pl.ds(i * units, units)])
-                for i, ref in enumerate((gate_own, gate_other, up_own, up_other))
-            ],
-            [sems.at[i] for i in range(4)],
-        )
-    )
+    pairs = [
+        (ref, in_ref.at[pl.ds(i * units, units)])
+        for i, ref in enumerate((gate_own, gate_other, up_own, up_other))
+    ] + [
+        (ref, down_ref.at[pl.ds(i * units, units)]) for i, ref in enumerate((down_own, down_other))
+    ]
+    wait_all(start_all(pairs, [sems.at[i] for i in range(6)]))
 
 
 def add_pieces(piece_refs, places, weight_ref, total):
@@ -178,30 +150,24 @@
     out_ref[...] = add_pieces(piece_refs, places, weight_ref, jnp.zeros(out_ref.shape, f32))
 
 
-def hidden_kernel(*refs, places):
-    *piece_refs, weight_ref, early_ref, out_ref = refs
+def expert_kernel(*refs, places):
+    *piece_refs, weight_ref, early_ref, down_ref, out_ref = refs
     total = add_pieces(piece_refs, places, weight_ref, early_ref[...])
     units = total.shape[0] // 2
     gate = total[:units]
-    hidden = (gate * jax.nn.sigmoid(gate) * total[units:]).T
-    half = hidden.shape[0] // 2
-    hidden = jnp.concatenate([hidden[:half], hidden[half:]], axis=1).astype(bf16)
+    hidden = (gate * jax.nn.sigmoid(gate) * total[units:]).T.astype(bf16)
+    width = out_ref.shape[2]
     for j in range(out_ref.shape[0]):
-        out_ref[j] = hidden
-
-
-def down_kernel(hidden_ref, own_ref, other_ref, out_ref, *, slots, padded):
-    chips, half, units = hidden_ref.shape
-    units = units // 2
-    width = out_ref.shape[1]
-    low = jnp.zeros((half, width), f32)
-    high = jnp.zeros((half, width), f32)
-    for j in range(chips):
-        weight = jnp.concatenate([own_ref[j], other_ref[j]], axis=0)
-        low += mm(hidden_ref[j, :, :units], weight)
-        high += mm(hidden_ref[j, :, units:], weight)
-    total = jnp.concatenate([low, high], axis=0).astype(bf16)
-    out_ref[...] = mm(slot_rows(slots, padded, 2 * half, True), total).astype(bf16)
+        out_ref[j] = mm(hidden, down_ref[:, j * width : (j + 1) * width]).astype(bf16)
+
+
+def total_kernel(parts_ref, out_ref, *, slots, padded):
+    total = parts_ref[0].astype(f32)
+    for j in range(1, parts_ref.shape[0]):
+        total += parts_ref[j].astype(f32)
+    out_ref[...] = jnp.zeros_like(out_ref)
+    for e in range(total.shape[0] // slots):
+        out_ref[e * padded : e * padded + slots] = total[e * slots : (e + 1) * slots].astype(bf16)
 
 
 def combine_kernel(mix_ref, back_ref, keep_ref, send_ref):
@@ -238,32 +204,33 @@
 
 def attend_kernel(query_ref, *refs, first, queries, latent, scale):
     *key_refs, out_ref = refs
-    count = key_refs[0].shape[0]
+    count = key_refs[0].shape[0] // 2
     key_width = query_ref.shape[1]
     rows = out_ref.shape[0]
-    core, parity = lax.axis_index("c"), lax.axis_index("z") % 2
+    core = lax.axis_index("c")
     me = chip_at(0, 0) * 2 + core
     key = lax.broadcasted_iota(jnp.int32, (queries, count), 1)
     query = lax.broadcasted_iota(jnp.int32, (queries, count), 0)
     owner, offset = key // queries * 2, key % queries
     bias = []
-    for slab in (parity, 1 - parity):
-        for part in (core, 1 - core):
-            seen = (owner + part < me) | ((owner + part == me) & (offset <= query)) | (slab == 0)
-            side = jnp.where(seen, 0.0, -jnp.inf)
-            bias.append(jnp.concatenate([side, side], axis=0))
+    for part in (core, 1 - core):
+        seen = (owner + part < me) | ((owner + part == me) & (offset <= query))
+        side = jnp.where(seen, 0.0, -jnp.inf)
+        bias.append(jnp.concatenate([side, side], axis=0))
     for g in range(0, rows, 2 * queries):
         full = query_ref[first + g : first + g + 2 * queries]
-        scores = [
-            mm(full, ref[:, :key_width], NT) * scale + side for ref, side in zip(key_refs, bias)
-        ]
+        scores = []
+        for ref, side in zip(key_refs, bias):
+            part = mm(full, ref[:, :key_width], NT) * scale
+            scores += [part[:, :count], part[:, count:] + side]
         peak = functools.reduce(
             jnp.maximum, [jnp.max(part, axis=1, keepdims=True) for part in scores]
         )
         weights = [jnp.exp(part - peak) for part in scores]
         total = sum(jnp.sum(part, axis=1, keepdims=True) for part in weights)
         mixed = sum(
-            mm(part.astype(bf16), ref[:, :latent]) for part, ref in zip(weights, key_refs)
+            mm(jnp.concatenate(weights[2 * i : 2 * i + 2], axis=1).astype(bf16), ref[:, :latent])
+            for i, ref in enumerate(key_refs)
         )
         out_ref[g : g + 2 * queries] = (mixed / total).astype(bf16)
 
@@ -313,6 +280,17 @@
 
 def shape(dims, dtype=bf16):
     return jax.ShapeDtypeStruct(dims, dtype)
+
+
+def gathered(x):
+    across = lax.ppermute(x, "xl", SWAP)
+    below = lax.ppermute(x, "y", UP)
+    above = lax.ppermute(x, "y", DOWN)
+    early = [x, across, below, above]
+    across_below = lax.ppermute(across, "y", UP)
+    across_above = lax.ppermute(across, "y", DOWN)
+    far = lax.ppermute(below, "y", UP)
+    return early, [across_below, across_above, far, lax.ppermute(across_above, "y", DOWN)]
 
 
 def exchange(x, axes):
@@ -354,10 +332,9 @@
     DMA = pltpu.SemaphoreType.DMA
     gate_own, up_own, down_own = w_gate[0], w_up[0], w_down[0]
 
-    parts = call(
+    own_keys = call(
         prep_kernel,
-        [pinned((units + queries, width))] * chips,
-        (down_own, "h"),
+        pinned((2 * queries, width)),
         (slab_latent, "h"),
         (kv_gain.reshape(1, latent), "h"),
         (slab_rope, "h"),
@@ -369,31 +346,25 @@
             pltpu.VMEM((queries, rope), bf16),
             pltpu.VMEM((cache_len, latent), bf16),
             pltpu.VMEM((cache_len, rope), bf16),
-            DMA((5 + chips,)),
+            DMA((5,)),
         ],
-        size=4 << 20,
+        size=1 << 20,
         name="prep",
     )
-
-    def send(part, step):
-        pairs = [
-            (a * 4 + b, (a ^ step[0]) * 4 + (b + step[1]) % 4) for a in range(2) for b in range(4)
-        ]
-        return lax.ppermute(part, CHIPS, pairs)
-
-    pieces = [parts[0]] + [send(part, step) for part, step in zip(parts[1:], STEPS[1:])]
-    down_mine, keys_mine = call(
-        join_kernel,
-        [pinned((chips, units, width)), pinned((chips * queries, width))],
-        *[(piece, "v") for piece in pieces],
+    early_keys, late_keys = gathered(own_keys)
+    keys_mine = call(
+        functools.partial(join_kernel, places=EARLY + LATE),
+        pinned((2 * chips * queries, width)),
+        *[(piece, "v") for piece in early_keys + late_keys],
         size=4 << 20,
         name="join",
     )
+    keys = [keys_mine, lax.ppermute(keys_mine, "c", SWAP)]
 
     outgoing, mix = call(
         functools.partial(route_kernel, experts=experts, slots=slots),
-        [pinned((experts * padded, width)), pinned((3, experts * padded, block))],
-        (after(expert_ids.T, parts[0]), "h"),
+        [pinned((experts, slots, width)), pinned((3, experts * padded, block))],
+        (after(expert_ids.T, own_keys), "h"),
         (gate_scores.T, "h"),
         (prev_rows, "h"),
         scratch=[
@@ -424,60 +395,51 @@
         name="absorb",
     )
     own = call(
-        functools.partial(compact_kernel, slots=slots, padded=padded),
+        compact_kernel,
         pinned((count, width)),
         (after(arrived, keys_mine, query), "v"),
         size=1 << 19,
         name="compact",
     )
 
-    keys_far = lax.ppermute(keys_mine, "z", [(i, i ^ 1) for i in range(8)])
-    down_theirs = lax.ppermute(down_mine, "c", SWAP)
-    keys = [
-        keys_mine,
-        lax.ppermute(keys_mine, "c", SWAP),
-        keys_far,
-        lax.ppermute(keys_far, "c", SWAP),
+    swaps = [
+        lax.ppermute(after(w, outgoing), "c", SWAP) for w in (gate_own, up_own, down_own)
     ]
-    gate_swap, up_swap = after(gate_own, outgoing), after(up_own, outgoing)
-    weights = call(
+    weights, down = call(
         stack_kernel,
-        pinned((4 * units, model)),
+        [pinned((4 * units, model)), pinned((2 * units, model))],
         (gate_own, "h"),
-        (lax.ppermute(gate_swap, "c", SWAP), "a"),
+        (swaps[0], "a"),
         (up_own, "h"),
-        (lax.ppermute(up_swap, "c", SWAP), "a"),
-        scratch=[DMA((4,))],
-        size=8 << 20,
+        (swaps[1], "a"),
+        (down_own, "h"),
+        (swaps[2], "a"),
+        scratch=[DMA((6,))],
+        size=12 << 20,
         name="stack",
     )
 
-    across = lax.ppermute(own, "xl", SWAP)
-    from_below = lax.ppermute(own, "y", UP)
-    from_above = lax.ppermute(own, "y", DOWN)
-    across_below = lax.ppermute(across, "y", UP)
-    across_above = lax.ppermute(across, "y", DOWN)
-    far = lax.ppermute(from_below, "y", UP)
-    across_far = lax.ppermute(across_above, "y", DOWN)
+    early_rows, late_rows = gathered(own)
     flops = 2 * count * width * 4 * units
     early = call(
-        functools.partial(early_kernel, places=[(0, 0), (1, 0), (0, -1), (0, 1)]),
+        functools.partial(early_kernel, places=EARLY),
         pinned((4 * units, count), f32),
-        *[(piece, "v") for piece in (own, across, from_below, from_above)],
+        *[(piece, "v") for piece in early_rows],
         (weights, "v"),
         flops=4 * flops,
         size=3 << 20,
         name="early",
     )
-    hidden = call(
-        functools.partial(hidden_kernel, places=[(1, -1), (1, 1), (0, 2), (1, 2)]),
-        pinned((chips, count // 2, 4 * units)),
-        *[(piece, "v") for piece in (across_below, across_above, far, across_far)],
+    partial = call(
+        functools.partial(expert_kernel, places=LATE),
+        pinned((chips, count, width)),
+        *[(piece, "v") for piece in late_rows],
         (weights, "v"),
         (early, "v"),
-        flops=4 * flops,
+        (down, "v"),
+        flops=6 * flops,
         size=3 << 20,
-        name="hidden",
+        name="expert",
     )
 
     def attend(first, last, behind):
@@ -497,34 +459,29 @@
             name="attend",
         )
 
-    mixed_0 = attend(0, 4, hidden)
-    produced = call(
-        functools.partial(down_kernel, slots=slots, padded=padded),
-        pinned((experts * padded, width)),
-        (after(exchange(hidden, CHIPS), mixed_0), "v"),
-        (down_mine, "v"),
-        (down_theirs, "v"),
-        flops=2 * count * chips * 2 * units * width,
-        size=3 << 20,
-        name="down",
-    )
-    mixed_1 = attend(4, 8, produced)
+    mixed = [attend(0, 4, partial), attend(4, 8, partial)]
     attn = call(
         value_kernel,
         shape((queries, heads * value)),
-        (mixed_0, "v"),
-        (mixed_1, "v"),
+        *[(part, "v") for part in mixed],
         (w_uv, "h"),
         scratch=[pltpu.VMEM(w_uv.shape, bf16), DMA],
         flops=2 * heads * queries * latent * value,
         size=2 << 20,
         name="value",
     )
+    produced = call(
+        functools.partial(total_kernel, slots=slots, padded=padded),
+        pinned((experts * padded, width)),
+        (after(exchange(partial, CHIPS), attn), "v"),
+        size=3 << 20,
+        name="total",
+    )
     keep, send_half = call(
         combine_kernel,
         [pinned((block, width // 2), f32), pinned((block, width // 2))],
         (mix, "v"),
-        (after(exchange(produced, EXP), attn), "v"),
+        (exchange(produced, EXP), "v"),
         flops=6 * count * block * width,
         size=1 << 19,
         name="combine",

time: 118 us -> 110 us (0.932); the launches traced: 117 us -> 110 us
  blocking collectives: 0 us -> 19 us
  starting transfers between devices: 58.8 us -> 47.6 us
  waiting for transfers between devices: 29.7 us -> 19 us
  Pallas kernels: 25.9 us -> 21.7 us
    all_to_all x0 -> x1, blocking collectives: none -> 19 us  [exchange(): return lax.all_to_all(x, axes, split_axis=0, concat_axis=0, tiled=True)]
    ppermute x20 -> x18, waiting for transfers between devices: 19.2 us -> 11.8 us  [the longest x1 2.66 us: per_device(): keys = [keys_mine, lax.ppermute(keys_mine, 'c', SWAP)]]
    all_to_all x3 -> x2, starting transfers between devices: 22.3 us -> 16.1 us  [exchange(): return lax.all_to_all(x, axes, split_axis=0, concat_axis=0, tiled=True)]
    ppermute x20 -> x18, starting transfers between devices: 33.8 us -> 28.4 us  [the longest x1 6.25 us: per_device(): keys = [keys_mine, lax.ppermute(keys_mine, 'c', SWAP)]]
    pallas_call x14, Pallas kernels: 25.9 us -> 21.7 us  [call(): pl.pallas_call(kernel, out_shape=out_shape, in_specs=[spec(spaces[space])...]
    all_to_all x3 -> x2, waiting for transfers between devices: 9.61 us -> 6.3 us  [exchange(): return lax.all_to_all(x, axes, split_axis=0, concat_axis=0, tiled=True)]
  transfers between devices with their start and end apart: 24 -> 21, of which waited for: 10 -> 12; matrix products, arithmetic and copies ran while one was open for 0% -> 0% of each run, Pallas kernels for 16% -> 14%
where the time goes in v2:
time: 110 us
  starting transfers between devices  47.6 us (43%)
  Pallas kernels  21.7 us (20%)
  waiting for transfers between devices  19 us (17%)
  blocking collectives  19 us (17%)
  local copies, waits for them, and re-layouts  1.92 us (2%)
    pallas_call x14, Pallas kernels, call(): pl.pallas_call(kernel, out_shape=out_shape, in_specs=[spec(spaces[space])...  21.7 us
    all_to_all x1, blocking collectives, exchange(): return lax.all_to_all(x, axes, split_axis=0, concat_axis=0, tiled=True)  19 us
    all_to_all x2, starting transfers between devices, exchange(): return lax.all_to_all(x, axes, split_axis=0, concat_axis=0, tiled=True)  16.1 us
    all_to_all x2, waiting for transfers between devices, exchange(): return lax.all_to_all(x, axes, split_axis=0, concat_axis=0, tiled=True)  6.3 us
    ppermute x1, starting transfers between devices, per_device(): keys = [keys_mine, lax.ppermute(keys_mine, 'c', SWAP)]  6.25 us
    ppermute x2, starting transfers between devices, gathered(): lax.ppermute(across_above, 'y', DOWN)  4.52 us
    ppermute x3, starting transfers between devices, per_device(): lax.ppermute(after(w, outgoing), 'c', SWAP)  4.31 us
    ppermute x2, starting transfers between devices, gathered(): across_above = lax.ppermute(across, 'y', DOWN)  4.11 us
  transfers between devices with their start and end apart: 21, of which 12 were waited for; matrix products, arithmetic and copies ran while one was open for 0% of the time, Pallas kernels for 14%

profile of v2, /device:TPU:3, one launch (start us, length us, event | category | flops | bytes accessed | tf_op | source)
XLA Modules:
  0.0 110.0 jit_solution(2475822577213252586)
XLA Ops:
  0.6 1.1 prep.1.refs_0_
  1.8 1.5 %collective-permute-start.1 = (bf16[128,640]{1,0:T(8,128)(2,1)S(1)}, bf16[128,640]{1,0:T(8,128)(2,1)S(1)}, u32[]{:S(2)}, u32[]{:S(2)}) collective-permute-start(bf16[128,640]{1,0:T(8,128)(2,1)S(1)} %prep.1.refs_0_), channel_id=1, source_target_pairs={{0,32},{32,64},{64,96},{96,0},{1,33},{33,65},{65,97},{97,1},{2,34}... | collective-permute-start | bytes 491528 | tf_op jit(solution)/shard_map/ppermute | solution.py:287
  3.3 2.1 %route.1 = (bf16[16,12,640]{2,1,0:T(8,128)(2,1)}, bf16[3,256,48]{2,1,0:T(8,128)(2,1)S(1)}) custom-call(s32[6,48]{1,0:T(8,128)} %bitcast.16, f32[6,48]{1,0:T(8,128)} %bitcast.17, bf16[48,5120]{1,0:T(8,128)(2,1)} %rows_hbm.1), custom_call_target="tpu_custom_call" | custom-call | flops 11796480 | bytes 1048576 | tf_op jit(solution)/shard_map/route/pallas_call | solution.py:269
  5.4 1.5 %collective-permute-start.13 = (bf16[96,5120]{1,0:T(8,128)(2,1)}, bf16[96,5120]{1,0:T(8,128)(2,1)S(1)}, u32[]{:S(2)}, u32[]{:S(2)}) collective-permute-start(bf16[96,5120]{1,0:T(8,128)(2,1)} %bitcast.10), channel_id=1, source_target_pairs={{0,16},{16,0},{1,17},{17,1},{2,18},{18,2},{3,19},{19,3},{4,20},{20... | collective-permute-start | bytes 2949128 | tf_op jit(solution)/shard_map/ppermute | solution.py:406
  7.0 10.0 %all-to-all-start = ((bf16[16,12,640]{2,1,0:T(8,128)(2,1)}), bf16[16,12,640]{2,1,0:T(8,128)(2,1)S(1)}, u32[]{:S(2)}, u32[]{:S(2)}) async-start(bf16[16,12,640]{2,1,0:T(8,128)(2,1)} %get-tuple-element.16), calls=%async_computation | async-start | bytes 655360 | tf_op jit(solution)/shard_map/all_to_all | solution.py:297
  17.0 1.5 %collective-permute-start.2 = (bf16[128,640]{1,0:T(8,128)(2,1)S(1)}, bf16[128,640]{1,0:T(8,128)(2,1)S(1)}, u32[]{:S(2)}, u32[]{:S(2)}) collective-permute-start(bf16[128,640]{1,0:T(8,128)(2,1)S(1)} %prep.1.refs_0_), channel_id=1, source_target_pairs={{0,96},{32,0},{64,32},{96,64},{1,97},{33,1},{65,33},{97,65},{2,98}... | collective-permute-start | bytes 491528 | tf_op jit(solution)/shard_map/ppermute | solution.py:288
  18.4 1.5 %collective-permute-start.4 = (bf16[128,640]{1,0:T(8,128)(2,1)S(1)}, bf16[128,640]{1,0:T(8,128)(2,1)S(1)}, u32[]{:S(2)}, u32[]{:S(2)}) collective-permute-start(bf16[128,640]{1,0:T(8,128)(2,1)S(1)} %collective-permute-done.refs_1_), channel_id=1, source_target_pairs={{0,96},{32,0},{64,32},{96,64},{1,97},{33,1},{65,33},{97,65},{2,98}... | collective-permute-start | bytes 491528 | tf_op jit(solution)/shard_map/ppermute | solution.py:291
  20.0 2.1 %collective-permute-done.2.refs_3_ = bf16[128,640]{1,0:T(8,128)(2,1)S(1)} collective-permute-done((bf16[128,640]{1,0:T(8,128)(2,1)S(1)}, bf16[128,640]{1,0:T(8,128)(2,1)S(1)}, u32[]{:S(2)}, u32[]{:S(2)}) %collective-permute-start.2) | collective-permute-done | bytes 163872 | tf_op jit(solution)/shard_map/ppermute | solution.py:288
  22.1 2.7 %collective-permute-start.15 = (bf16[96,5120]{1,0:T(8,128)(2,1)}, bf16[96,5120]{1,0:T(8,128)(2,1)}, u32[]{:S(2)}, u32[]{:S(2)}) collective-permute-start(bf16[96,5120]{1,0:T(8,128)(2,1)} %bitcast.14), channel_id=1, source_target_pairs={{0,16},{16,0},{1,17},{17,1},{2,18},{18,2},{3,19},{19,3},{4,20},{20... | collective-permute-start | bytes 2949128 | tf_op jit(solution)/shard_map/ppermute | solution.py:406
  25.6 1.3 %collective-permute-start.5 = (bf16[128,640]{1,0:T(8,128)(2,1)S(1)}, bf16[128,640]{1,0:T(8,128)(2,1)S(1)}, u32[]{:S(2)}, u32[]{:S(2)}) collective-permute-start(bf16[128,640]{1,0:T(8,128)(2,1)S(1)} %collective-permute-done.1.refs_2_), channel_id=1, source_target_pairs={{0,32},{32,64},{64,96},{96,0},{1,33},{33,65},{65,97},{97,1},{2,34}... | collective-permute-start | bytes 491528 | tf_op jit(solution)/shard_map/ppermute | solution.py:292
  26.9 1.4 %collective-permute-start.6 = (bf16[128,640]{1,0:T(8,128)(2,1)S(1)}, bf16[128,640]{1,0:T(8,128)(2,1)S(1)}, u32[]{:S(2)}, u32[]{:S(2)}) collective-permute-start(bf16[128,640]{1,0:T(8,128)(2,1)S(1)} %collective-permute-done.4.refs_5_), channel_id=1, source_target_pairs={{0,96},{32,0},{64,32},{96,64},{1,97},{33,1},{65,33},{97,65},{2,98}... | collective-permute-start | bytes 491528 | tf_op jit(solution)/shard_map/ppermute | solution.py:293
  28.3 1.7 %absorb.1.query_ref = bf16[512,576]{1,0:T(8,128)(2,1)S(1)} custom-call(bf16[64,1024]{1,0:T(8,128)(2,1)} %nope_hbm.1, bf16[64,512]{1,0:T(8,128)(2,1)} %rope_hbm.1, bf16[8,128,512]{2,1,0:T(8,128)(2,1)} %uk_hbm.1), custom_call_target="tpu_custom_call" | custom-call | flops 67108864 | bytes 2097152 | tf_op jit(solution)/shard_map/absorb/pallas_call | solution.py:269
  31.3 1.6 %collective-permute-start.7 = (bf16[192,640]{1,0:T(8,128)(2,1)S(1)}, bf16[192,640]{1,0:T(8,128)(2,1)S(1)}, u32[]{:S(2)}, u32[]{:S(2)}) collective-permute-start(bf16[192,640]{1,0:T(8,128)(2,1)S(1)} %compact.1.refs_0_), channel_id=1, source_target_pairs={{0,128},{128,0},{1,129},{129,1},{2,130},{130,2},{3,131},{131,3},{4... | collective-permute-start | bytes 737288 | tf_op jit(solution)/shard_map/ppermute | solution.py:286
  32.9 1.3 %collective-permute-start.10 = (bf16[192,640]{1,0:T(8,128)(2,1)S(1)}, bf16[192,640]{1,0:T(8,128)(2,1)S(1)}, u32[]{:S(2)}, u32[]{:S(2)}) collective-permute-start(bf16[192,640]{1,0:T(8,128)(2,1)S(1)} %compact.1.refs_0_), channel_id=1, source_target_pairs={{0,32},{32,64},{64,96},{96,0},{1,33},{33,65},{65,97},{97,1},{2,34}... | collective-permute-start | bytes 737288 | tf_op jit(solution)/shard_map/ppermute | solution.py:287
  34.2 2.3 %collective-permute-done.7.refs_1_ = bf16[192,640]{1,0:T(8,128)(2,1)S(1)} collective-permute-done((bf16[192,640]{1,0:T(8,128)(2,1)S(1)}, bf16[192,640]{1,0:T(8,128)(2,1)S(1)}, u32[]{:S(2)}, u32[]{:S(2)}) %collective-permute-start.7) | collective-permute-done | bytes 245792 | tf_op jit(solution)/shard_map/ppermute | solution.py:286
  36.5 2.6 %collective-permute-start.9 = (bf16[192,640]{1,0:T(8,128)(2,1)S(1)}, bf16[192,640]{1,0:T(8,128)(2,1)S(1)}, u32[]{:S(2)}, u32[]{:S(2)}) collective-permute-start(bf16[192,640]{1,0:T(8,128)(2,1)S(1)} %collective-permute-done.7.refs_1_), channel_id=1, source_target_pairs={{0,96},{32,0},{64,32},{96,64},{1,97},{33,1},{65,33},{97,65},{2,98}... | collective-permute-start | bytes 737288 | tf_op jit(solution)/shard_map/ppermute | solution.py:291
  39.2 1.7 %collective-permute-start.16 = (bf16[192,640]{1,0:T(8,128)(2,1)S(1)}, bf16[192,640]{1,0:T(8,128)(2,1)S(1)}, u32[]{:S(2)}, u32[]{:S(2)}) collective-permute-start(bf16[192,640]{1,0:T(8,128)(2,1)S(1)} %compact.1.refs_0_), channel_id=1, source_target_pairs={{0,96},{32,0},{64,32},{96,64},{1,97},{33,1},{65,33},{97,65},{2,98}... | collective-permute-start | bytes 737288 | tf_op jit(solution)/shard_map/ppermute | solution.py:288
  41.1 1.1 %collective-permute-done.9.refs_1_ = bf16[192,640]{1,0:T(8,128)(2,1)S(1)} collective-permute-done((bf16[192,640]{1,0:T(8,128)(2,1)S(1)}, bf16[192,640]{1,0:T(8,128)(2,1)S(1)}, u32[]{:S(2)}, u32[]{:S(2)}) %collective-permute-start.9) | collective-permute-done | bytes 245792 | tf_op jit(solution)/shard_map/ppermute | solution.py:291
  42.2 3.1 %collective-permute-start.12 = (bf16[192,640]{1,0:T(8,128)(2,1)S(1)}, bf16[192,640]{1,0:T(8,128)(2,1)S(1)}, u32[]{:S(2)}, u32[]{:S(2)}) collective-permute-start(bf16[192,640]{1,0:T(8,128)(2,1)S(1)} %collective-permute-done.9.refs_1_), channel_id=1, source_target_pairs={{0,96},{32,0},{64,32},{96,64},{1,97},{33,1},{65,33},{97,65},{2,98}... | collective-permute-start | bytes 737288 | tf_op jit(solution)/shard_map/ppermute | solution.py:293
  45.4 2.5 %stack.1 = (bf16[384,5120]{1,0:T(8,128)(2,1)S(1)}, bf16[192,5120]{1,0:T(8,128)(2,1)S(1)}) custom-call(bf16[96,5120]{1,0:T(8,128)(2,1)} %bitcast.11, bf16[96,5120]{1,0:T(8,128)(2,1)S(1)} %collective-permute-done.13.gate_other, bf16[96,5120]{1,0:T(8,128)(2,1)} %bitcast.13, bf16[96,5120]{1,0:T(8,128)(2,1)} %collective-permute-done.14.up_other, ...), custom_call_target="tpu_custom_call" | custom-call | bytes 12582912 | tf_op jit(solution)/shard_map/stack/pallas_call | solution.py:269
  49.7 1.5 %collective-permute-done.12.refs_3_ = bf16[192,640]{1,0:T(8,128)(2,1)S(1)} collective-permute-done((bf16[192,640]{1,0:T(8,128)(2,1)S(1)}, bf16[192,640]{1,0:T(8,128)(2,1)S(1)}, u32[]{:S(2)}, u32[]{:S(2)}) %collective-permute-start.12) | collective-permute-done | bytes 245792 | tf_op jit(solution)/shard_map/ppermute | solution.py:293
  51.2 4.1 %expert.1 = bf16[8,192,640]{2,1,0:T(8,128)(2,1)} custom-call(bf16[192,640]{1,0:T(8,128)(2,1)S(1)} %collective-permute-done.8.refs_0_, bf16[192,640]{1,0:T(8,128)(2,1)S(1)} %collective-permute-done.9.refs_1_, bf16[192,640]{1,0:T(8,128)(2,1)S(1)} %collective-permute-done.11.refs_2_, bf16[192,640]{1,0:T(8,128)(2,1)S(1)} %collective-permute-done.12.refs_3_, ...), custom_call_target="tpu_custom_call" | custom-call | flops 566231040 | bytes 3145728 | tf_op jit(solution)/shard_map/expert/pallas_call | solution.py:269
  55.3 6.1 %all-to-all-start.1 = ((bf16[8,192,640]{2,1,0:T(8,128)(2,1)}), bf16[8,192,640]{2,1,0:T(8,128)(2,1)S(1)}, u32[]{:S(2)}, u32[]{:S(2)}) async-start(bf16[8,192,640]{2,1,0:T(8,128)(2,1)} %expert.1), calls=%async_computation.1 | async-start | bytes 3932160 | tf_op jit(solution)/shard_map/all_to_all | solution.py:297
  61.4 6.3 %collective-permute-start.17 = (bf16[1024,640]{1,0:T(8,128)(2,1)S(1)}, bf16[1024,640]{1,0:T(8,128)(2,1)S(1)}, u32[]{:S(2)}, u32[]{:S(2)}) collective-permute-start(bf16[1024,640]{1,0:T(8,128)(2,1)S(1)} %join.1.refs_0_), channel_id=1, source_target_pairs={{0,16},{16,0},{1,17},{17,1},{2,18},{18,2},{3,19},{19,3},{4,20},{20... | collective-permute-start | bytes 3932168 | tf_op jit(solution)/shard_map/ppermute | solution.py:362
  67.7 2.7 %collective-permute-done.17.refs_1_ = bf16[1024,640]{1,0:T(8,128)(2,1)S(1)} collective-permute-done((bf16[1024,640]{1,0:T(8,128)(2,1)S(1)}, bf16[1024,640]{1,0:T(8,128)(2,1)S(1)}, u32[]{:S(2)}, u32[]{:S(2)}) %collective-permute-start.17) | collective-permute-done | bytes 1310752 | tf_op jit(solution)/shard_map/ppermute | solution.py:362
  70.3 1.1 copy-done.1
  71.4 2.9 %attend.3.refs_1_ = bf16[256,512]{1,0:T(8,128)(2,1)S(1)} custom-call(bf16[512,576]{1,0:T(8,128)(2,1)S(1)} %copy-done.1, bf16[1024,640]{1,0:T(8,128)(2,1)S(1)} %join.1.refs_0_, bf16[1024,640]{1,0:T(8,128)(2,1)S(1)} %collective-permute-done.17.refs_1_), custom_call_target="tpu_custom_call" | custom-call | flops 1140850688 | bytes 4194304 | tf_op jit(solution)/shard_map/attend/pallas_call | solution.py:269
  74.3 2.9 %attend.2.refs_0_ = bf16[256,512]{1,0:T(8,128)(2,1)S(1)} custom-call(bf16[512,576]{1,0:T(8,128)(2,1)S(1)} %copy-done.1, bf16[1024,640]{1,0:T(8,128)(2,1)S(1)} %join.1.refs_0_, bf16[1024,640]{1,0:T(8,128)(2,1)S(1)} %collective-permute-done.17.refs_1_), custom_call_target="tpu_custom_call" | custom-call | flops 1140850688 | bytes 4194304 | tf_op jit(solution)/shard_map/attend/pallas_call | solution.py:269
  77.3 2.2 %value.1 = bf16[64,1024]{1,0:T(8,128)(2,1)} custom-call(bf16[256,512]{1,0:T(8,128)(2,1)S(1)} %attend.2.refs_0_, bf16[256,512]{1,0:T(8,128)(2,1)S(1)} %attend.3.refs_1_, bf16[8,512,128]{2,1,0:T(8,128)(2,1)} %refs_2_.1), custom_call_target="tpu_custom_call" | custom-call | flops 67108864 | bytes 2097152 | tf_op jit(solution)/shard_map/value/pallas_call | solution.py:269
  79.5 6.3 %all-to-all-done.1.parts_ref = bf16[8,192,640]{2,1,0:T(8,128)(2,1)S(1)} async-done(((bf16[8,192,640]{2,1,0:T(8,128)(2,1)}), bf16[8,192,640]{2,1,0:T(8,128)(2,1)S(1)}, u32[]{:S(2)}, u32[]{:S(2)}) %all-to-all-start.1) | async-done | bytes 1966112 | tf_op jit(solution)/shard_map/all_to_all | solution.py:297
  86.0 19.0 %all_to_all.21 = bf16[16,16,640]{2,1,0:T(8,128)(2,1)S(1)} all-to-all(bf16[16,16,640]{2,1,0:T(8,128)(2,1)S(1)} %bitcast.8), channel_id=1, replica_groups=mesh['xl'=2,'y'=4,'c'=2,'xh'=2,'z'=8] {'xh','z'}, dimensions={0} | all-to-all | bytes 655360 | tf_op jit(solution)/shard_map/all_to_all | solution.py:297
  105.4 3.1 %collective-permute-start.18 = (bf16[48,320]{1,0:T(8,128)(2,1)S(1)}, bf16[48,320]{1,0:T(8,128)(2,1)S(1)}, u32[]{:S(2)}, u32[]{:S(2)}) collective-permute-start(bf16[48,320]{1,0:T(8,128)(2,1)S(1)} %get-tuple-element.27), channel_id=1, source_target_pairs={{0,16},{16,0},{1,17},{17,1},{2,18},{18,2},{3,19},{19,3},{4,20},{20... | collective-permute-start | bytes 92168 | tf_op jit(solution)/shard_map/ppermute | solution.py:493
  (29 shorter events, 6.6 us)
Async XLA Ops:
  1.7 16.7 %collective-permute-start = (bf16[128,640]{1,0:T(8,128)(2,1)S(1)}, bf16[128,640]{1,0:T(8,128)(2,1)S(1)}, u32[]{:S(2)}, u32[]{:S(2)}) collective-permute-start(bf16[128,640]{1,0:T(8,128)(2,1)S(1)} %prep.1.refs_0_), channel_id=1, source_target_pairs={{0,128},{128,0},{1,129},{129,1},{2,130},{130,2},{3,131},{131,3},{4... | collective-permute-start | bytes 491528 | tf_op jit(solution)/shard_map/ppermute | solution.py:286
  1.8 18.2 %collective-permute-start.1 = (bf16[128,640]{1,0:T(8,128)(2,1)S(1)}, bf16[128,640]{1,0:T(8,128)(2,1)S(1)}, u32[]{:S(2)}, u32[]{:S(2)}) collective-permute-start(bf16[128,640]{1,0:T(8,128)(2,1)S(1)} %prep.1.refs_0_), channel_id=1, source_target_pairs={{0,32},{32,64},{64,96},{96,0},{1,33},{33,65},{65,97},{97,1},{2,34}... | collective-permute-start | bytes 491528 | tf_op jit(solution)/shard_map/ppermute | solution.py:287
  5.4 35.4 %collective-permute-start.13 = (bf16[96,5120]{1,0:T(8,128)(2,1)}, bf16[96,5120]{1,0:T(8,128)(2,1)S(1)}, u32[]{:S(2)}, u32[]{:S(2)}) collective-permute-start(bf16[96,5120]{1,0:T(8,128)(2,1)} %bitcast.10), channel_id=1, source_target_pairs={{0,16},{16,0},{1,17},{17,1},{2,18},{18,2},{3,19},{19,3},{4,20},{20... | collective-permute-start | bytes 2949128 | tf_op jit(solution)/shard_map/ppermute | solution.py:406
  6.9 33.9 %collective-permute-start.14 = (bf16[96,5120]{1,0:T(8,128)(2,1)}, bf16[96,5120]{1,0:T(8,128)(2,1)}, u32[]{:S(2)}, u32[]{:S(2)}) collective-permute-start(bf16[96,5120]{1,0:T(8,128)(2,1)} %bitcast.12), channel_id=1, source_target_pairs={{0,16},{16,0},{1,17},{17,1},{2,18},{18,2},{3,19},{19,3},{4,20},{20... | collective-permute-start | bytes 2949128 | tf_op jit(solution)/shard_map/ppermute | solution.py:406
  7.0 24.2 %all-to-all-start = ((bf16[16,12,640]{2,1,0:T(8,128)(2,1)}), bf16[16,12,640]{2,1,0:T(8,128)(2,1)S(1)}, u32[]{:S(2)}, u32[]{:S(2)}) async-start(bf16[16,12,640]{2,1,0:T(8,128)(2,1)} %get-tuple-element.16), calls=%async_computation | async-start | bytes 655360 | tf_op jit(solution)/shard_map/all_to_all | solution.py:297
  17.0 5.1 %collective-permute-start.2 = (bf16[128,640]{1,0:T(8,128)(2,1)S(1)}, bf16[128,640]{1,0:T(8,128)(2,1)S(1)}, u32[]{:S(2)}, u32[]{:S(2)}) collective-permute-start(bf16[128,640]{1,0:T(8,128)(2,1)S(1)} %prep.1.refs_0_), channel_id=1, source_target_pairs={{0,96},{32,0},{64,32},{96,64},{1,97},{33,1},{65,33},{97,65},{2,98}... | collective-permute-start | bytes 491528 | tf_op jit(solution)/shard_map/ppermute | solution.py:288
  18.4 7.2 %collective-permute-start.4 = (bf16[128,640]{1,0:T(8,128)(2,1)S(1)}, bf16[128,640]{1,0:T(8,128)(2,1)S(1)}, u32[]{:S(2)}, u32[]{:S(2)}) collective-permute-start(bf16[128,640]{1,0:T(8,128)(2,1)S(1)} %collective-permute-done.refs_1_), channel_id=1, source_target_pairs={{0,96},{32,0},{64,32},{96,64},{1,97},{33,1},{65,33},{97,65},{2,98}... | collective-permute-start | bytes 491528 | tf_op jit(solution)/shard_map/ppermute | solution.py:291
  20.0 7.0 %collective-permute-start.3 = (bf16[128,640]{1,0:T(8,128)(2,1)S(1)}, bf16[128,640]{1,0:T(8,128)(2,1)S(1)}, u32[]{:S(2)}, u32[]{:S(2)}) collective-permute-start(bf16[128,640]{1,0:T(8,128)(2,1)S(1)} %collective-permute-done.refs_1_), channel_id=1, source_target_pairs={{0,32},{32,64},{64,96},{96,0},{1,33},{33,65},{65,97},{97,1},{2,34}... | collective-permute-start | bytes 491528 | tf_op jit(solution)/shard_map/ppermute | solution.py:290
  22.1 23.2 %collective-permute-start.15 = (bf16[96,5120]{1,0:T(8,128)(2,1)}, bf16[96,5120]{1,0:T(8,128)(2,1)}, u32[]{:S(2)}, u32[]{:S(2)}) collective-permute-start(bf16[96,5120]{1,0:T(8,128)(2,1)} %bitcast.14), channel_id=1, source_target_pairs={{0,16},{16,0},{1,17},{17,1},{2,18},{18,2},{3,19},{19,3},{4,20},{20... | collective-permute-start | bytes 2949128 | tf_op jit(solution)/shard_map/ppermute | solution.py:406
  25.6 5.4 %collective-permute-start.5 = (bf16[128,640]{1,0:T(8,128)(2,1)S(1)}, bf16[128,640]{1,0:T(8,128)(2,1)S(1)}, u32[]{:S(2)}, u32[]{:S(2)}) collective-permute-start(bf16[128,640]{1,0:T(8,128)(2,1)S(1)} %collective-permute-done.1.refs_2_), channel_id=1, source_target_pairs={{0,32},{32,64},{64,96},{96,0},{1,33},{33,65},{65,97},{97,1},{2,34}... | collective-permute-start | bytes 491528 | tf_op jit(solution)/shard_map/ppermute | solution.py:292
  26.9 4.2 %collective-permute-start.6 = (bf16[128,640]{1,0:T(8,128)(2,1)S(1)}, bf16[128,640]{1,0:T(8,128)(2,1)S(1)}, u32[]{:S(2)}, u32[]{:S(2)}) collective-permute-start(bf16[128,640]{1,0:T(8,128)(2,1)S(1)} %collective-permute-done.4.refs_5_), channel_id=1, source_target_pairs={{0,96},{32,0},{64,32},{96,64},{1,97},{33,1},{65,33},{97,65},{2,98}... | collective-permute-start | bytes 491528 | tf_op jit(solution)/shard_map/ppermute | solution.py:293
  30.0 0.8 copy-start
  31.3 5.2 %collective-permute-start.7 = (bf16[192,640]{1,0:T(8,128)(2,1)S(1)}, bf16[192,640]{1,0:T(8,128)(2,1)S(1)}, u32[]{:S(2)}, u32[]{:S(2)}) collective-permute-start(bf16[192,640]{1,0:T(8,128)(2,1)S(1)} %compact.1.refs_0_), channel_id=1, source_target_pairs={{0,128},{128,0},{1,129},{129,1},{2,130},{130,2},{3,131},{131,3},{4... | collective-permute-start | bytes 737288 | tf_op jit(solution)/shard_map/ppermute | solution.py:286
  32.9 6.3 %collective-permute-start.10 = (bf16[192,640]{1,0:T(8,128)(2,1)S(1)}, bf16[192,640]{1,0:T(8,128)(2,1)S(1)}, u32[]{:S(2)}, u32[]{:S(2)}) collective-permute-start(bf16[192,640]{1,0:T(8,128)(2,1)S(1)} %compact.1.refs_0_), channel_id=1, source_target_pairs={{0,32},{32,64},{64,96},{96,0},{1,33},{33,65},{65,97},{97,1},{2,34}... | collective-permute-start | bytes 737288 | tf_op jit(solution)/shard_map/ppermute | solution.py:287
  36.5 5.7 %collective-permute-start.9 = (bf16[192,640]{1,0:T(8,128)(2,1)S(1)}, bf16[192,640]{1,0:T(8,128)(2,1)S(1)}, u32[]{:S(2)}, u32[]{:S(2)}) collective-permute-start(bf16[192,640]{1,0:T(8,128)(2,1)S(1)} %collective-permute-done.7.refs_1_), channel_id=1, source_target_pairs={{0,96},{32,0},{64,32},{96,64},{1,97},{33,1},{65,33},{97,65},{2,98}... | collective-permute-start | bytes 737288 | tf_op jit(solution)/shard_map/ppermute | solution.py:291
  39.2 8.7 %collective-permute-start.16 = (bf16[192,640]{1,0:T(8,128)(2,1)S(1)}, bf16[192,640]{1,0:T(8,128)(2,1)S(1)}, u32[]{:S(2)}, u32[]{:S(2)}) collective-permute-start(bf16[192,640]{1,0:T(8,128)(2,1)S(1)} %compact.1.refs_0_), channel_id=1, source_target_pairs={{0,96},{32,0},{64,32},{96,64},{1,97},{33,1},{65,33},{97,65},{2,98}... | collective-permute-start | bytes 737288 | tf_op jit(solution)/shard_map/ppermute | solution.py:288
  40.8 7.9 %collective-permute-start.8 = (bf16[192,640]{1,0:T(8,128)(2,1)S(1)}, bf16[192,640]{1,0:T(8,128)(2,1)S(1)}, u32[]{:S(2)}, u32[]{:S(2)}) collective-permute-start(bf16[192,640]{1,0:T(8,128)(2,1)S(1)} %collective-permute-done.7.refs_1_), channel_id=1, source_target_pairs={{0,32},{32,64},{64,96},{96,0},{1,33},{33,65},{65,97},{97,1},{2,34}... | collective-permute-start | bytes 737288 | tf_op jit(solution)/shard_map/ppermute | solution.py:290
  40.8 8.9 %collective-permute-start.11 = (bf16[192,640]{1,0:T(8,128)(2,1)S(1)}, bf16[192,640]{1,0:T(8,128)(2,1)S(1)}, u32[]{:S(2)}, u32[]{:S(2)}) collective-permute-start(bf16[192,640]{1,0:T(8,128)(2,1)S(1)} %collective-permute-done.10.refs_2_), channel_id=1, source_target_pairs={{0,32},{32,64},{64,96},{96,0},{1,33},{33,65},{65,97},{97,1},{2,34}... | collective-permute-start | bytes 737288 | tf_op jit(solution)/shard_map/ppermute | solution.py:292
  42.2 9.0 %collective-permute-start.12 = (bf16[192,640]{1,0:T(8,128)(2,1)S(1)}, bf16[192,640]{1,0:T(8,128)(2,1)S(1)}, u32[]{:S(2)}, u32[]{:S(2)}) collective-permute-start(bf16[192,640]{1,0:T(8,128)(2,1)S(1)} %collective-permute-done.9.refs_1_), channel_id=1, source_target_pairs={{0,96},{32,0},{64,32},{96,64},{1,97},{33,1},{65,33},{97,65},{2,98}... | collective-permute-start | bytes 737288 | tf_op jit(solution)/shard_map/ppermute | solution.py:293
  55.3 30.5 %all-to-all-start.1 = ((bf16[8,192,640]{2,1,0:T(8,128)(2,1)}), bf16[8,192,640]{2,1,0:T(8,128)(2,1)S(1)}, u32[]{:S(2)}, u32[]{:S(2)}) async-start(bf16[8,192,640]{2,1,0:T(8,128)(2,1)} %expert.1), calls=%async_computation.1 | async-start | bytes 3932160 | tf_op jit(solution)/shard_map/all_to_all | solution.py:297
  61.4 8.9 %collective-permute-start.17 = (bf16[1024,640]{1,0:T(8,128)(2,1)S(1)}, bf16[1024,640]{1,0:T(8,128)(2,1)S(1)}, u32[]{:S(2)}, u32[]{:S(2)}) collective-permute-start(bf16[1024,640]{1,0:T(8,128)(2,1)S(1)} %join.1.refs_0_), channel_id=1, source_target_pairs={{0,16},{16,0},{1,17},{17,1},{2,18},{18,2},{3,19},{19,3},{4,20},{20... | collective-permute-start | bytes 3932168 | tf_op jit(solution)/shard_map/ppermute | solution.py:362
  70.3 1.1 copy-start.1
  105.4 3.9 %collective-permute-start.18 = (bf16[48,320]{1,0:T(8,128)(2,1)S(1)}, bf16[48,320]{1,0:T(8,128)(2,1)S(1)}, u32[]{:S(2)}, u32[]{:S(2)}) collective-permute-start(bf16[48,320]{1,0:T(8,128)(2,1)S(1)} %get-tuple-element.27), channel_id=1, source_target_pairs={{0,16},{16,0},{1,17},{17,1},{2,18},{18,2},{3,19},{19,3},{4,20},{20... | collective-permute-start | bytes 92168 | tf_op jit(solution)/shard_map/ppermute | solution.py:493

commit v3 on v2

--- a/solution.py
+++ b/solution.py
@@ -282,11 +282,13 @@
     return jax.ShapeDtypeStruct(dims, dtype)
 
 
-def gathered(x):
+def gathered(x, in_turn):
     across = lax.ppermute(x, "xl", SWAP)
     below = lax.ppermute(x, "y", UP)
     above = lax.ppermute(x, "y", DOWN)
     early = [x, across, below, above]
+    if in_turn:
+        across, below, above = lax.optimization_barrier((across, below, above))
     across_below = lax.ppermute(across, "y", UP)
     across_above = lax.ppermute(across, "y", DOWN)
     far = lax.ppermute(below, "y", UP)
@@ -351,7 +353,7 @@
         size=1 << 20,
         name="prep",
     )
-    early_keys, late_keys = gathered(own_keys)
+    early_keys, late_keys = gathered(own_keys, True)
     keys_mine = call(
         functools.partial(join_kernel, places=EARLY + LATE),
         pinned((2 * chips * queries, width)),
@@ -419,7 +421,7 @@
         name="stack",
     )
 
-    early_rows, late_rows = gathered(own)
+    early_rows, late_rows = gathered(own, False)
     flops = 2 * count * width * 4 * units
     early = call(
         functools.partial(early_kernel, places=EARLY),

time: 110 us -> 109 us (level)
  starting transfers between devices: 47.6 us -> 40.2 us
  waiting for transfers between devices: 19 us -> 24.9 us
    ppermute x2, waiting for transfers between devices: 0.01 us -> 2.33 us  [gathered(): across_below = lax.ppermute(across, 'y', UP)]
    all_to_all x2, starting transfers between devices: 16.1 us -> 13.9 us  [exchange(): return lax.all_to_all(x, axes, split_axis=0, concat_axis=0, tiled=True)]
    ppermute x2, waiting for transfers between devices: 2.14 us -> 0.01 us  [gathered(): above = lax.ppermute(x, 'y', DOWN)]
    ppermute x2, starting transfers between devices: 4.52 us -> 2.78 us  [gathered(): lax.ppermute(across_above, 'y', DOWN)]
    ppermute x2, waiting for transfers between devices: 1.89 us -> 3.27 us  [gathered(): across_above = lax.ppermute(across, 'y', DOWN)]
    ppermute x2, starting transfers between devices: 2.84 us -> 1.54 us  [gathered(): below = lax.ppermute(x, 'y', UP)]
    ppermute x2, waiting for transfers between devices: 2.29 us -> 3.59 us  [gathered(): across = lax.ppermute(x, 'xl', SWAP)]
    ppermute x2, starting transfers between devices: 1.56 us -> 0.35 us  [gathered(): far = lax.ppermute(below, 'y', UP)]
where the time goes in v3:
time: 109 us; the launch traced here: 108 us
  starting transfers between devices  40.2 us (37%)
  waiting for transfers between devices  24.9 us (23%)
  Pallas kernels  21.7 us (20%)
  blocking collectives  18.8 us (17%)
  local copies, waits for them, and re-layouts  1.92 us (2%)
    pallas_call x14, Pallas kernels, call(): pl.pallas_call(kernel, out_shape=out_shape, in_specs=[spec(spaces[space])...  21.7 us
    all_to_all x1, blocking collectives, exchange(): return lax.all_to_all(x, axes, split_axis=0, concat_axis=0, tiled=True)  18.8 us
    all_to_all x2, starting transfers between devices, exchange(): return lax.all_to_all(x, axes, split_axis=0, concat_axis=0, tiled=True)  13.9 us
    all_to_all x2, waiting for transfers between devices, exchange(): return lax.all_to_all(x, axes, split_axis=0, concat_axis=0, tiled=True)  6.3 us
    ppermute x1, starting transfers between devices, per_device(): keys = [keys_mine, lax.ppermute(keys_mine, 'c', SWAP)]  6.25 us
    ppermute x3, starting transfers between devices, per_device(): lax.ppermute(after(w, outgoing), 'c', SWAP)  4.57 us
    ppermute x2, waiting for transfers between devices, gathered(): across = lax.ppermute(x, 'xl', SWAP)  3.59 us
    ppermute x2, waiting for transfers between devices, gathered(): across_above = lax.ppermute(across, 'y', DOWN)  3.27 us
  transfers between devices with their start and end apart: 21, of which 12 were waited for; matrix products, arithmetic and copies ran while one was open for 0% of the time, Pallas kernels for 14%

profile of v3, /device:TPU:3, one launch (start us, length us, event | category | flops | bytes accessed | tf_op | source)
XLA Modules:
  0.0 108.3 jit_solution(7800004285383412087)
XLA Ops:
  0.6 1.1 prep.1.refs_0_
  1.8 1.5 %collective-permute-start.1 = (bf16[128,640]{1,0:T(8,128)(2,1)S(1)}, bf16[128,640]{1,0:T(8,128)(2,1)S(1)}, u32[]{:S(2)}, u32[]{:S(2)}) collective-permute-start(bf16[128,640]{1,0:T(8,128)(2,1)S(1)} %prep.1.refs_0_), channel_id=1, source_target_pairs={{0,32},{32,64},{64,96},{96,0},{1,33},{33,65},{65,97},{97,1},{2,34}... | collective-permute-start | bytes 491528 | tf_op jit(solution)/shard_map/ppermute | solution.py:287
  3.3 1.4 %collective-permute-start.2 = (bf16[128,640]{1,0:T(8,128)(2,1)S(1)}, bf16[128,640]{1,0:T(8,128)(2,1)S(1)}, u32[]{:S(2)}, u32[]{:S(2)}) collective-permute-start(bf16[128,640]{1,0:T(8,128)(2,1)S(1)} %prep.1.refs_0_), channel_id=1, source_target_pairs={{0,96},{32,0},{64,32},{96,64},{1,97},{33,1},{65,33},{97,65},{2,98}... | collective-permute-start | bytes 491528 | tf_op jit(solution)/shard_map/ppermute | solution.py:288
  4.8 2.1 %route.1 = (bf16[16,12,640]{2,1,0:T(8,128)(2,1)}, bf16[3,256,48]{2,1,0:T(8,128)(2,1)S(1)}) custom-call(s32[6,48]{1,0:T(8,128)} %bitcast.16, f32[6,48]{1,0:T(8,128)} %bitcast.17, bf16[48,5120]{1,0:T(8,128)(2,1)} %rows_hbm.1), custom_call_target="tpu_custom_call" | custom-call | flops 11796480 | bytes 1048576 | tf_op jit(solution)/shard_map/route/pallas_call | solution.py:269
  6.8 3.3 %collective-permute-start.13 = (bf16[96,5120]{1,0:T(8,128)(2,1)}, bf16[96,5120]{1,0:T(8,128)(2,1)S(1)}, u32[]{:S(2)}, u32[]{:S(2)}) collective-permute-start(bf16[96,5120]{1,0:T(8,128)(2,1)} %bitcast.10), channel_id=1, source_target_pairs={{0,16},{16,0},{1,17},{17,1},{2,18},{18,2},{3,19},{19,3},{4,20},{20... | collective-permute-start | bytes 2949128 | tf_op jit(solution)/shard_map/ppermute | solution.py:408
  10.2 8.4 %all-to-all-start = ((bf16[16,12,640]{2,1,0:T(8,128)(2,1)}), bf16[16,12,640]{2,1,0:T(8,128)(2,1)S(1)}, u32[]{:S(2)}, u32[]{:S(2)}) async-start(bf16[16,12,640]{2,1,0:T(8,128)(2,1)} %get-tuple-element.18), calls=%async_computation | async-start | bytes 655360 | tf_op jit(solution)/shard_map/all_to_all | solution.py:299
  18.7 1.6 %collective-permute-start.4 = (bf16[128,640]{1,0:T(8,128)(2,1)S(1)}, bf16[128,640]{1,0:T(8,128)(2,1)S(1)}, u32[]{:S(2)}, u32[]{:S(2)}) collective-permute-start(bf16[128,640]{1,0:T(8,128)(2,1)S(1)} %collective-permute-done.refs_1_), channel_id=1, source_target_pairs={{0,96},{32,0},{64,32},{96,64},{1,97},{33,1},{65,33},{97,65},{2,98}... | collective-permute-start | bytes 491528 | tf_op jit(solution)/shard_map/ppermute | solution.py:293
  20.3 1.2 %collective-permute-start.15 = (bf16[96,5120]{1,0:T(8,128)(2,1)}, bf16[96,5120]{1,0:T(8,128)(2,1)}, u32[]{:S(2)}, u32[]{:S(2)}) collective-permute-start(bf16[96,5120]{1,0:T(8,128)(2,1)} %bitcast.14), channel_id=1, source_target_pairs={{0,16},{16,0},{1,17},{17,1},{2,18},{18,2},{3,19},{19,3},{4,20},{20... | collective-permute-start | bytes 2949128 | tf_op jit(solution)/shard_map/ppermute | solution.py:408
  21.5 2.3 %collective-permute-done.4.refs_5_ = bf16[128,640]{1,0:T(8,128)(2,1)S(1)} collective-permute-done((bf16[128,640]{1,0:T(8,128)(2,1)S(1)}, bf16[128,640]{1,0:T(8,128)(2,1)S(1)}, u32[]{:S(2)}, u32[]{:S(2)}) %collective-permute-start.4) | collective-permute-done | bytes 163872 | tf_op jit(solution)/shard_map/ppermute | solution.py:293
  23.9 2.3 %collective-permute-done.3.refs_4_ = bf16[128,640]{1,0:T(8,128)(2,1)S(1)} collective-permute-done((bf16[128,640]{1,0:T(8,128)(2,1)S(1)}, bf16[128,640]{1,0:T(8,128)(2,1)S(1)}, u32[]{:S(2)}, u32[]{:S(2)}) %collective-permute-start.3) | collective-permute-done | bytes 163872 | tf_op jit(solution)/shard_map/ppermute | solution.py:292
  26.5 1.7 %absorb.1.query_ref = bf16[512,576]{1,0:T(8,128)(2,1)S(1)} custom-call(bf16[64,1024]{1,0:T(8,128)(2,1)} %nope_hbm.1, bf16[64,512]{1,0:T(8,128)(2,1)} %rope_hbm.1, bf16[8,128,512]{2,1,0:T(8,128)(2,1)} %uk_hbm.1), custom_call_target="tpu_custom_call" | custom-call | flops 67108864 | bytes 2097152 | tf_op jit(solution)/shard_map/absorb/pallas_call | solution.py:269
  29.5 1.1 %collective-permute-done.6.refs_7_ = bf16[128,640]{1,0:T(8,128)(2,1)S(1)} collective-permute-done((bf16[128,640]{1,0:T(8,128)(2,1)S(1)}, bf16[128,640]{1,0:T(8,128)(2,1)S(1)}, u32[]{:S(2)}, u32[]{:S(2)}) %collective-permute-start.6) | collective-permute-done | bytes 163872 | tf_op jit(solution)/shard_map/ppermute | solution.py:295
  30.9 1.6 %collective-permute-start.7 = (bf16[192,640]{1,0:T(8,128)(2,1)S(1)}, bf16[192,640]{1,0:T(8,128)(2,1)S(1)}, u32[]{:S(2)}, u32[]{:S(2)}) collective-permute-start(bf16[192,640]{1,0:T(8,128)(2,1)S(1)} %compact.1.refs_0_), channel_id=1, source_target_pairs={{0,128},{128,0},{1,129},{129,1},{2,130},{130,2},{3,131},{131,3},{4... | collective-permute-start | bytes 737288 | tf_op jit(solution)/shard_map/ppermute | solution.py:286
  32.5 3.6 %collective-permute-done.7.refs_1_ = bf16[192,640]{1,0:T(8,128)(2,1)S(1)} collective-permute-done((bf16[192,640]{1,0:T(8,128)(2,1)S(1)}, bf16[192,640]{1,0:T(8,128)(2,1)S(1)}, u32[]{:S(2)}, u32[]{:S(2)}) %collective-permute-start.7) | collective-permute-done | bytes 245792 | tf_op jit(solution)/shard_map/ppermute | solution.py:286
  36.1 1.5 %collective-permute-start.9 = (bf16[192,640]{1,0:T(8,128)(2,1)S(1)}, bf16[192,640]{1,0:T(8,128)(2,1)S(1)}, u32[]{:S(2)}, u32[]{:S(2)}) collective-permute-start(bf16[192,640]{1,0:T(8,128)(2,1)S(1)} %collective-permute-done.7.refs_1_), channel_id=1, source_target_pairs={{0,96},{32,0},{64,32},{96,64},{1,97},{33,1},{65,33},{97,65},{2,98}... | collective-permute-start | bytes 737288 | tf_op jit(solution)/shard_map/ppermute | solution.py:293
  37.6 1.1 %collective-permute-done.10.refs_2_ = bf16[192,640]{1,0:T(8,128)(2,1)S(1)} collective-permute-done((bf16[192,640]{1,0:T(8,128)(2,1)S(1)}, bf16[192,640]{1,0:T(8,128)(2,1)S(1)}, u32[]{:S(2)}, u32[]{:S(2)}) %collective-permute-start.10) | collective-permute-done | bytes 245792 | tf_op jit(solution)/shard_map/ppermute | solution.py:287
  40.5 0.9 collective-permute-done.9.refs_1_
  41.4 2.5 %collective-permute-start.12 = (bf16[192,640]{1,0:T(8,128)(2,1)S(1)}, bf16[192,640]{1,0:T(8,128)(2,1)S(1)}, u32[]{:S(2)}, u32[]{:S(2)}) collective-permute-start(bf16[192,640]{1,0:T(8,128)(2,1)S(1)} %collective-permute-done.9.refs_1_), channel_id=1, source_target_pairs={{0,96},{32,0},{64,32},{96,64},{1,97},{33,1},{65,33},{97,65},{2,98}... | collective-permute-start | bytes 737288 | tf_op jit(solution)/shard_map/ppermute | solution.py:295
  43.9 2.5 %stack.1 = (bf16[384,5120]{1,0:T(8,128)(2,1)S(1)}, bf16[192,5120]{1,0:T(8,128)(2,1)S(1)}) custom-call(bf16[96,5120]{1,0:T(8,128)(2,1)} %bitcast.11, bf16[96,5120]{1,0:T(8,128)(2,1)S(1)} %collective-permute-done.13.gate_other, bf16[96,5120]{1,0:T(8,128)(2,1)} %bitcast.13, bf16[96,5120]{1,0:T(8,128)(2,1)} %collective-permute-done.14.up_other, ...), custom_call_target="tpu_custom_call" | custom-call | bytes 12582912 | tf_op jit(solution)/shard_map/stack/pallas_call | solution.py:269
  47.2 1.7 %collective-permute-done.11.refs_2_ = bf16[192,640]{1,0:T(8,128)(2,1)S(1)} collective-permute-done((bf16[192,640]{1,0:T(8,128)(2,1)S(1)}, bf16[192,640]{1,0:T(8,128)(2,1)S(1)}, u32[]{:S(2)}, u32[]{:S(2)}) %collective-permute-start.11) | collective-permute-done | bytes 245792 | tf_op jit(solution)/shard_map/ppermute | solution.py:294
  48.9 1.4 %collective-permute-done.12.refs_3_ = bf16[192,640]{1,0:T(8,128)(2,1)S(1)} collective-permute-done((bf16[192,640]{1,0:T(8,128)(2,1)S(1)}, bf16[192,640]{1,0:T(8,128)(2,1)S(1)}, u32[]{:S(2)}, u32[]{:S(2)}) %collective-permute-start.12) | collective-permute-done | bytes 245792 | tf_op jit(solution)/shard_map/ppermute | solution.py:295
  50.3 4.1 %expert.1 = bf16[8,192,640]{2,1,0:T(8,128)(2,1)} custom-call(bf16[192,640]{1,0:T(8,128)(2,1)S(1)} %collective-permute-done.8.refs_0_, bf16[192,640]{1,0:T(8,128)(2,1)S(1)} %collective-permute-done.9.refs_1_, bf16[192,640]{1,0:T(8,128)(2,1)S(1)} %collective-permute-done.11.refs_2_, bf16[192,640]{1,0:T(8,128)(2,1)S(1)} %collective-permute-done.12.refs_3_, ...), custom_call_target="tpu_custom_call" | custom-call | flops 566231040 | bytes 3145728 | tf_op jit(solution)/shard_map/expert/pallas_call | solution.py:269
  54.4 5.5 %all-to-all-start.1 = ((bf16[8,192,640]{2,1,0:T(8,128)(2,1)}), bf16[8,192,640]{2,1,0:T(8,128)(2,1)S(1)}, u32[]{:S(2)}, u32[]{:S(2)}) async-start(bf16[8,192,640]{2,1,0:T(8,128)(2,1)} %expert.1), calls=%async_computation.1 | async-start | bytes 3932160 | tf_op jit(solution)/shard_map/all_to_all | solution.py:299
  59.9 6.3 %collective-permute-start.17 = (bf16[1024,640]{1,0:T(8,128)(2,1)S(1)}, bf16[1024,640]{1,0:T(8,128)(2,1)S(1)}, u32[]{:S(2)}, u32[]{:S(2)}) collective-permute-start(bf16[1024,640]{1,0:T(8,128)(2,1)S(1)} %join.1.refs_0_), channel_id=1, source_target_pairs={{0,16},{16,0},{1,17},{17,1},{2,18},{18,2},{3,19},{19,3},{4,20},{20... | collective-permute-start | bytes 3932168 | tf_op jit(solution)/shard_map/ppermute | solution.py:364
  66.2 2.7 %collective-permute-done.17.refs_1_ = bf16[1024,640]{1,0:T(8,128)(2,1)S(1)} collective-permute-done((bf16[1024,640]{1,0:T(8,128)(2,1)S(1)}, bf16[1024,640]{1,0:T(8,128)(2,1)S(1)}, u32[]{:S(2)}, u32[]{:S(2)}) %collective-permute-start.17) | collective-permute-done | bytes 1310752 | tf_op jit(solution)/shard_map/ppermute | solution.py:364
  68.9 1.1 %copy-done.1 = bf16[512,576]{1,0:T(8,128)(2,1)S(1)} copy-done((bf16[512,576]{1,0:T(8,128)(2,1)S(1)}, bf16[512,576]{1,0:T(8,128)(2,1)}, u32[]{:S(2)}) %copy-start.1) | copy-done | bytes 589848
  69.9 2.9 %attend.3.refs_1_ = bf16[256,512]{1,0:T(8,128)(2,1)S(1)} custom-call(bf16[512,576]{1,0:T(8,128)(2,1)S(1)} %copy-done.1, bf16[1024,640]{1,0:T(8,128)(2,1)S(1)} %join.1.refs_0_, bf16[1024,640]{1,0:T(8,128)(2,1)S(1)} %collective-permute-done.17.refs_1_), custom_call_target="tpu_custom_call" | custom-call | flops 1140850688 | bytes 4194304 | tf_op jit(solution)/shard_map/attend/pallas_call | solution.py:269
  72.9 2.9 %attend.2.refs_0_ = bf16[256,512]{1,0:T(8,128)(2,1)S(1)} custom-call(bf16[512,576]{1,0:T(8,128)(2,1)S(1)} %copy-done.1, bf16[1024,640]{1,0:T(8,128)(2,1)S(1)} %join.1.refs_0_, bf16[1024,640]{1,0:T(8,128)(2,1)S(1)} %collective-permute-done.17.refs_1_), custom_call_target="tpu_custom_call" | custom-call | flops 1140850688 | bytes 4194304 | tf_op jit(solution)/shard_map/attend/pallas_call | solution.py:269
  75.8 2.2 %value.1 = bf16[64,1024]{1,0:T(8,128)(2,1)} custom-call(bf16[256,512]{1,0:T(8,128)(2,1)S(1)} %attend.2.refs_0_, bf16[256,512]{1,0:T(8,128)(2,1)S(1)} %attend.3.refs_1_, bf16[8,512,128]{2,1,0:T(8,128)(2,1)} %refs_2_.1), custom_call_target="tpu_custom_call" | custom-call | flops 67108864 | bytes 2097152 | tf_op jit(solution)/shard_map/value/pallas_call | solution.py:269
  78.0 6.3 %all-to-all-done.1.parts_ref = bf16[8,192,640]{2,1,0:T(8,128)(2,1)S(1)} async-done(((bf16[8,192,640]{2,1,0:T(8,128)(2,1)}), bf16[8,192,640]{2,1,0:T(8,128)(2,1)S(1)}, u32[]{:S(2)}, u32[]{:S(2)}) %all-to-all-start.1) | async-done | bytes 1966112 | tf_op jit(solution)/shard_map/all_to_all | solution.py:299
  84.6 18.8 %all_to_all.21 = bf16[16,16,640]{2,1,0:T(8,128)(2,1)S(1)} all-to-all(bf16[16,16,640]{2,1,0:T(8,128)(2,1)S(1)} %bitcast.8), channel_id=1, replica_groups=mesh['xl'=2,'y'=4,'c'=2,'xh'=2,'z'=8] {'xh','z'}, dimensions={0} | all-to-all | bytes 655360 | tf_op jit(solution)/shard_map/all_to_all | solution.py:299
  103.8 3.1 %collective-permute-start.18 = (bf16[48,320]{1,0:T(8,128)(2,1)S(1)}, bf16[48,320]{1,0:T(8,128)(2,1)S(1)}, u32[]{:S(2)}, u32[]{:S(2)}) collective-permute-start(bf16[48,320]{1,0:T(8,128)(2,1)S(1)} %get-tuple-element.31), channel_id=1, source_target_pairs={{0,16},{16,0},{1,17},{17,1},{2,18},{18,2},{3,19},{19,3},{4,20},{20... | collective-permute-start | bytes 92168 | tf_op jit(solution)/shard_map/ppermute | solution.py:495
  (29 shorter events, 6.8 us)
Async XLA Ops:
  1.7 16.9 %collective-permute-start = (bf16[128,640]{1,0:T(8,128)(2,1)S(1)}, bf16[128,640]{1,0:T(8,128)(2,1)S(1)}, u32[]{:S(2)}, u32[]{:S(2)}) collective-permute-start(bf16[128,640]{1,0:T(8,128)(2,1)S(1)} %prep.1.refs_0_), channel_id=1, source_target_pairs={{0,128},{128,0},{1,129},{129,1},{2,130},{130,2},{3,131},{131,3},{4... | collective-permute-start | bytes 491528 | tf_op jit(solution)/shard_map/ppermute | solution.py:286
  1.8 16.9 %collective-permute-start.1 = (bf16[128,640]{1,0:T(8,128)(2,1)S(1)}, bf16[128,640]{1,0:T(8,128)(2,1)S(1)}, u32[]{:S(2)}, u32[]{:S(2)}) collective-permute-start(bf16[128,640]{1,0:T(8,128)(2,1)S(1)} %prep.1.refs_0_), channel_id=1, source_target_pairs={{0,32},{32,64},{64,96},{96,0},{1,33},{33,65},{65,97},{97,1},{2,34}... | collective-permute-start | bytes 491528 | tf_op jit(solution)/shard_map/ppermute | solution.py:287
  3.3 15.3 %collective-permute-start.2 = (bf16[128,640]{1,0:T(8,128)(2,1)S(1)}, bf16[128,640]{1,0:T(8,128)(2,1)S(1)}, u32[]{:S(2)}, u32[]{:S(2)}) collective-permute-start(bf16[128,640]{1,0:T(8,128)(2,1)S(1)} %prep.1.refs_0_), channel_id=1, source_target_pairs={{0,96},{32,0},{64,32},{96,64},{1,97},{33,1},{65,33},{97,65},{2,98}... | collective-permute-start | bytes 491528 | tf_op jit(solution)/shard_map/ppermute | solution.py:288
  6.8 32.5 %collective-permute-start.13 = (bf16[96,5120]{1,0:T(8,128)(2,1)}, bf16[96,5120]{1,0:T(8,128)(2,1)S(1)}, u32[]{:S(2)}, u32[]{:S(2)}) collective-permute-start(bf16[96,5120]{1,0:T(8,128)(2,1)} %bitcast.10), channel_id=1, source_target_pairs={{0,16},{16,0},{1,17},{17,1},{2,18},{18,2},{3,19},{19,3},{4,20},{20... | collective-permute-start | bytes 2949128 | tf_op jit(solution)/shard_map/ppermute | solution.py:408
  10.1 30.1 %collective-permute-start.14 = (bf16[96,5120]{1,0:T(8,128)(2,1)}, bf16[96,5120]{1,0:T(8,128)(2,1)}, u32[]{:S(2)}, u32[]{:S(2)}) collective-permute-start(bf16[96,5120]{1,0:T(8,128)(2,1)} %bitcast.12), channel_id=1, source_target_pairs={{0,16},{16,0},{1,17},{17,1},{2,18},{18,2},{3,19},{19,3},{4,20},{20... | collective-permute-start | bytes 2949128 | tf_op jit(solution)/shard_map/ppermute | solution.py:408
  10.2 20.6 %all-to-all-start = ((bf16[16,12,640]{2,1,0:T(8,128)(2,1)}), bf16[16,12,640]{2,1,0:T(8,128)(2,1)S(1)}, u32[]{:S(2)}, u32[]{:S(2)}) async-start(bf16[16,12,640]{2,1,0:T(8,128)(2,1)} %get-tuple-element.18), calls=%async_computation | async-start | bytes 655360 | tf_op jit(solution)/shard_map/all_to_all | solution.py:299
  18.7 5.1 %collective-permute-start.4 = (bf16[128,640]{1,0:T(8,128)(2,1)S(1)}, bf16[128,640]{1,0:T(8,128)(2,1)S(1)}, u32[]{:S(2)}, u32[]{:S(2)}) collective-permute-start(bf16[128,640]{1,0:T(8,128)(2,1)S(1)} %collective-permute-done.refs_1_), channel_id=1, source_target_pairs={{0,96},{32,0},{64,32},{96,64},{1,97},{33,1},{65,33},{97,65},{2,98}... | collective-permute-start | bytes 491528 | tf_op jit(solution)/shard_map/ppermute | solution.py:293
  20.3 5.9 %collective-permute-start.3 = (bf16[128,640]{1,0:T(8,128)(2,1)S(1)}, bf16[128,640]{1,0:T(8,128)(2,1)S(1)}, u32[]{:S(2)}, u32[]{:S(2)}) collective-permute-start(bf16[128,640]{1,0:T(8,128)(2,1)S(1)} %collective-permute-done.refs_1_), channel_id=1, source_target_pairs={{0,32},{32,64},{64,96},{96,0},{1,33},{33,65},{65,97},{97,1},{2,34}... | collective-permute-start | bytes 491528 | tf_op jit(solution)/shard_map/ppermute | solution.py:292
  20.3 23.6 %collective-permute-start.15 = (bf16[96,5120]{1,0:T(8,128)(2,1)}, bf16[96,5120]{1,0:T(8,128)(2,1)}, u32[]{:S(2)}, u32[]{:S(2)}) collective-permute-start(bf16[96,5120]{1,0:T(8,128)(2,1)} %bitcast.14), channel_id=1, source_target_pairs={{0,16},{16,0},{1,17},{17,1},{2,18},{18,2},{3,19},{19,3},{4,20},{20... | collective-permute-start | bytes 2949128 | tf_op jit(solution)/shard_map/ppermute | solution.py:408
  23.8 5.7 %collective-permute-start.5 = (bf16[128,640]{1,0:T(8,128)(2,1)S(1)}, bf16[128,640]{1,0:T(8,128)(2,1)S(1)}, u32[]{:S(2)}, u32[]{:S(2)}) collective-permute-start(bf16[128,640]{1,0:T(8,128)(2,1)S(1)} %collective-permute-done.1.refs_2_), channel_id=1, source_target_pairs={{0,32},{32,64},{64,96},{96,0},{1,33},{33,65},{65,97},{97,1},{2,34}... | collective-permute-start | bytes 491528 | tf_op jit(solution)/shard_map/ppermute | solution.py:294
  26.2 4.5 %collective-permute-start.6 = (bf16[128,640]{1,0:T(8,128)(2,1)S(1)}, bf16[128,640]{1,0:T(8,128)(2,1)S(1)}, u32[]{:S(2)}, u32[]{:S(2)}) collective-permute-start(bf16[128,640]{1,0:T(8,128)(2,1)S(1)} %collective-permute-done.4.refs_5_), channel_id=1, source_target_pairs={{0,96},{32,0},{64,32},{96,64},{1,97},{33,1},{65,33},{97,65},{2,98}... | collective-permute-start | bytes 491528 | tf_op jit(solution)/shard_map/ppermute | solution.py:295
  28.2 0.8 copy-start
  30.9 5.2 %collective-permute-start.7 = (bf16[192,640]{1,0:T(8,128)(2,1)S(1)}, bf16[192,640]{1,0:T(8,128)(2,1)S(1)}, u32[]{:S(2)}, u32[]{:S(2)}) collective-permute-start(bf16[192,640]{1,0:T(8,128)(2,1)S(1)} %compact.1.refs_0_), channel_id=1, source_target_pairs={{0,128},{128,0},{1,129},{129,1},{2,130},{130,2},{3,131},{131,3},{4... | collective-permute-start | bytes 737288 | tf_op jit(solution)/shard_map/ppermute | solution.py:286
  32.5 6.3 %collective-permute-start.10 = (bf16[192,640]{1,0:T(8,128)(2,1)S(1)}, bf16[192,640]{1,0:T(8,128)(2,1)S(1)}, u32[]{:S(2)}, u32[]{:S(2)}) collective-permute-start(bf16[192,640]{1,0:T(8,128)(2,1)S(1)} %compact.1.refs_0_), channel_id=1, source_target_pairs={{0,32},{32,64},{64,96},{96,0},{1,33},{33,65},{65,97},{97,1},{2,34}... | collective-permute-start | bytes 737288 | tf_op jit(solution)/shard_map/ppermute | solution.py:287
  36.1 5.3 %collective-permute-start.9 = (bf16[192,640]{1,0:T(8,128)(2,1)S(1)}, bf16[192,640]{1,0:T(8,128)(2,1)S(1)}, u32[]{:S(2)}, u32[]{:S(2)}) collective-permute-start(bf16[192,640]{1,0:T(8,128)(2,1)S(1)} %collective-permute-done.7.refs_1_), channel_id=1, source_target_pairs={{0,96},{32,0},{64,32},{96,64},{1,97},{33,1},{65,33},{97,65},{2,98}... | collective-permute-start | bytes 737288 | tf_op jit(solution)/shard_map/ppermute | solution.py:293
  38.7 7.7 %collective-permute-start.16 = (bf16[192,640]{1,0:T(8,128)(2,1)S(1)}, bf16[192,640]{1,0:T(8,128)(2,1)S(1)}, u32[]{:S(2)}, u32[]{:S(2)}) collective-permute-start(bf16[192,640]{1,0:T(8,128)(2,1)S(1)} %compact.1.refs_0_), channel_id=1, source_target_pairs={{0,96},{32,0},{64,32},{96,64},{1,97},{33,1},{65,33},{97,65},{2,98}... | collective-permute-start | bytes 737288 | tf_op jit(solution)/shard_map/ppermute | solution.py:288
  39.4 7.8 %collective-permute-start.8 = (bf16[192,640]{1,0:T(8,128)(2,1)S(1)}, bf16[192,640]{1,0:T(8,128)(2,1)S(1)}, u32[]{:S(2)}, u32[]{:S(2)}) collective-permute-start(bf16[192,640]{1,0:T(8,128)(2,1)S(1)} %collective-permute-done.7.refs_1_), channel_id=1, source_target_pairs={{0,32},{32,64},{64,96},{96,0},{1,33},{33,65},{65,97},{97,1},{2,34}... | collective-permute-start | bytes 737288 | tf_op jit(solution)/shard_map/ppermute | solution.py:292
  40.2 8.7 %collective-permute-start.11 = (bf16[192,640]{1,0:T(8,128)(2,1)S(1)}, bf16[192,640]{1,0:T(8,128)(2,1)S(1)}, u32[]{:S(2)}, u32[]{:S(2)}) collective-permute-start(bf16[192,640]{1,0:T(8,128)(2,1)S(1)} %collective-permute-done.10.refs_2_), channel_id=1, source_target_pairs={{0,32},{32,64},{64,96},{96,0},{1,33},{33,65},{65,97},{97,1},{2,34}... | collective-permute-start | bytes 737288 | tf_op jit(solution)/shard_map/ppermute | solution.py:294
  41.4 8.9 %collective-permute-start.12 = (bf16[192,640]{1,0:T(8,128)(2,1)S(1)}, bf16[192,640]{1,0:T(8,128)(2,1)S(1)}, u32[]{:S(2)}, u32[]{:S(2)}) collective-permute-start(bf16[192,640]{1,0:T(8,128)(2,1)S(1)} %collective-permute-done.9.refs_1_), channel_id=1, source_target_pairs={{0,96},{32,0},{64,32},{96,64},{1,97},{33,1},{65,33},{97,65},{2,98}... | collective-permute-start | bytes 737288 | tf_op jit(solution)/shard_map/ppermute | solution.py:295
  54.4 29.9 %all-to-all-start.1 = ((bf16[8,192,640]{2,1,0:T(8,128)(2,1)}), bf16[8,192,640]{2,1,0:T(8,128)(2,1)S(1)}, u32[]{:S(2)}, u32[]{:S(2)}) async-start(bf16[8,192,640]{2,1,0:T(8,128)(2,1)} %expert.1), calls=%async_computation.1 | async-start | bytes 3932160 | tf_op jit(solution)/shard_map/all_to_all | solution.py:299
  59.9 8.9 %collective-permute-start.17 = (bf16[1024,640]{1,0:T(8,128)(2,1)S(1)}, bf16[1024,640]{1,0:T(8,128)(2,1)S(1)}, u32[]{:S(2)}, u32[]{:S(2)}) collective-permute-start(bf16[1024,640]{1,0:T(8,128)(2,1)S(1)} %join.1.refs_0_), channel_id=1, source_target_pairs={{0,16},{16,0},{1,17},{17,1},{2,18},{18,2},{3,19},{19,3},{4,20},{20... | collective-permute-start | bytes 3932168 | tf_op jit(solution)/shard_map/ppermute | solution.py:364
  68.9 1.1 %copy-start.1 = (bf16[512,576]{1,0:T(8,128)(2,1)S(1)}, bf16[512,576]{1,0:T(8,128)(2,1)}, u32[]{:S(2)}) copy-start(bf16[512,576]{1,0:T(8,128)(2,1)} %copy-done) | copy-start | bytes 1769476
  103.8 3.9 %collective-permute-start.18 = (bf16[48,320]{1,0:T(8,128)(2,1)S(1)}, bf16[48,320]{1,0:T(8,128)(2,1)S(1)}, u32[]{:S(2)}, u32[]{:S(2)}) collective-permute-start(bf16[48,320]{1,0:T(8,128)(2,1)S(1)} %get-tuple-element.31), channel_id=1, source_target_pairs={{0,16},{16,0},{1,17},{17,1},{2,18},{18,2},{3,19},{19,3},{4,20},{20... | collective-permute-start | bytes 92168 | tf_op jit(solution)/shard_map/ppermute | solution.py:495

commit v4 on v3

--- a/solution.py
+++ b/solution.py
@@ -380,26 +380,10 @@
         name="route",
     )
     arrived = exchange(outgoing, EXP)
-    query = call(
-        absorb_kernel,
-        pinned((heads * queries, latent + rope)),
-        (q_nope, "h"),
-        (q_rope, "h"),
-        (w_uk, "h"),
-        scratch=[
-            pltpu.VMEM(q_nope.shape, bf16),
-            pltpu.VMEM(q_rope.shape, bf16),
-            pltpu.VMEM(w_uk.shape, bf16),
-            DMA((3,)),
-        ],
-        flops=2 * heads * queries * nope * latent,
-        size=2 << 20,
-        name="absorb",
-    )
     own = call(
         compact_kernel,
         pinned((count, width)),
-        (after(arrived, keys_mine, query), "v"),
+        (after(arrived, keys_mine), "v"),
         size=1 << 19,
         name="compact",
     )
@@ -444,6 +428,22 @@
         name="expert",
     )
 
+    query = call(
+        absorb_kernel,
+        pinned((heads * queries, latent + rope)),
+        (after(q_nope, partial), "h"),
+        (q_rope, "h"),
+        (w_uk, "h"),
+        scratch=[
+            pltpu.VMEM(q_nope.shape, bf16),
+            pltpu.VMEM(q_rope.shape, bf16),
+            pltpu.VMEM(w_uk.shape, bf16),
+            DMA((3,)),
+        ],
+        flops=2 * heads * queries * nope * latent,
+        size=2 << 20,
+        name="absorb",
+    )
     def attend(first, last, behind):
         return call(
             functools.partial(

time: 109 us -> 109 us (level)
  waiting for transfers between devices: 24.9 us -> 27 us
  local copies, waits for them, and re-layouts: 1.92 us -> 0 us
    ppermute x2, waiting for transfers between devices: 2.15 us -> 4.67 us  [gathered(): far = lax.ppermute(below, 'y', UP)]
    unnamed x4 -> x0, local copies, waits for them, and re-layouts: 1.92 us -> none
    ppermute x1, waiting for transfers between devices: 2.66 us -> 0.98 us  [per_device(): keys = [keys_mine, lax.ppermute(keys_mine, 'c', SWAP)]]
where the time goes in v4:
time: 109 us; the launch traced here: 108 us
  starting transfers between devices  40.1 us (37%)
  waiting for transfers between devices  27 us (25%)
  Pallas kernels  21.7 us (20%)
  blocking collectives  18.8 us (17%)
    pallas_call x14, Pallas kernels, call(): pl.pallas_call(kernel, out_shape=out_shape, in_specs=[spec(spaces[space])...  21.7 us
    all_to_all x1, blocking collectives, exchange(): return lax.all_to_all(x, axes, split_axis=0, concat_axis=0, tiled=True)  18.8 us
    all_to_all x2, starting transfers between devices, exchange(): return lax.all_to_all(x, axes, split_axis=0, concat_axis=0, tiled=True)  13.9 us
    all_to_all x2, waiting for transfers between devices, exchange(): return lax.all_to_all(x, axes, split_axis=0, concat_axis=0, tiled=True)  7.39 us
    ppermute x1, starting transfers between devices, per_device(): keys = [keys_mine, lax.ppermute(keys_mine, 'c', SWAP)]  6.25 us
    ppermute x2, waiting for transfers between devices, gathered(): far = lax.ppermute(below, 'y', UP)  4.67 us
    ppermute x3, starting transfers between devices, per_device(): lax.ppermute(after(w, outgoing), 'c', SWAP)  4.57 us
    ppermute x2, waiting for transfers between devices, gathered(): across = lax.ppermute(x, 'xl', SWAP)  3.59 us
  transfers between devices with their start and end apart: 21, of which 12 were waited for; matrix products, arithmetic and copies ran while one was open for 0% of the time, Pallas kernels for 14%

profile of v4, /device:TPU:3, one launch (start us, length us, event | category | flops | bytes accessed | tf_op | source)
XLA Modules:
  0.0 108.3 jit_solution(2037623062513093513)
XLA Ops:
  0.6 1.1 prep.1.refs_0_
  1.8 1.5 %collective-permute-start.1 = (bf16[128,640]{1,0:T(8,128)(2,1)S(1)}, bf16[128,640]{1,0:T(8,128)(2,1)S(1)}, u32[]{:S(2)}, u32[]{:S(2)}) collective-permute-start(bf16[128,640]{1,0:T(8,128)(2,1)S(1)} %prep.1.refs_0_), channel_id=1, source_target_pairs={{0,32},{32,64},{64,96},{96,0},{1,33},{33,65},{65,97},{97,1},{2,34}... | collective-permute-start | bytes 491528 | tf_op jit(solution)/shard_map/ppermute | solution.py:287
  3.3 1.4 %collective-permute-start.2 = (bf16[128,640]{1,0:T(8,128)(2,1)S(1)}, bf16[128,640]{1,0:T(8,128)(2,1)S(1)}, u32[]{:S(2)}, u32[]{:S(2)}) collective-permute-start(bf16[128,640]{1,0:T(8,128)(2,1)S(1)} %prep.1.refs_0_), channel_id=1, source_target_pairs={{0,96},{32,0},{64,32},{96,64},{1,97},{33,1},{65,33},{97,65},{2,98}... | collective-permute-start | bytes 491528 | tf_op jit(solution)/shard_map/ppermute | solution.py:288
  4.8 2.0 %route.1 = (bf16[16,12,640]{2,1,0:T(8,128)(2,1)}, bf16[3,256,48]{2,1,0:T(8,128)(2,1)S(1)}) custom-call(s32[6,48]{1,0:T(8,128)} %bitcast.16, f32[6,48]{1,0:T(8,128)} %bitcast.17, bf16[48,5120]{1,0:T(8,128)(2,1)} %rows_hbm.1), custom_call_target="tpu_custom_call" | custom-call | flops 11796480 | bytes 1048576 | tf_op jit(solution)/shard_map/route/pallas_call | solution.py:269
  6.8 3.3 %collective-permute-start.13 = (bf16[96,5120]{1,0:T(8,128)(2,1)}, bf16[96,5120]{1,0:T(8,128)(2,1)S(1)}, u32[]{:S(2)}, u32[]{:S(2)}) collective-permute-start(bf16[96,5120]{1,0:T(8,128)(2,1)} %bitcast.10), channel_id=1, source_target_pairs={{0,16},{16,0},{1,17},{17,1},{2,18},{18,2},{3,19},{19,3},{4,20},{20... | collective-permute-start | bytes 2949128 | tf_op jit(solution)/shard_map/ppermute | solution.py:392
  10.2 8.4 %all-to-all-start = ((bf16[16,12,640]{2,1,0:T(8,128)(2,1)}), bf16[16,12,640]{2,1,0:T(8,128)(2,1)S(1)}, u32[]{:S(2)}, u32[]{:S(2)}) async-start(bf16[16,12,640]{2,1,0:T(8,128)(2,1)} %get-tuple-element.19), calls=%async_computation | async-start | bytes 655360 | tf_op jit(solution)/shard_map/all_to_all | solution.py:299
  18.6 1.6 %collective-permute-start.4 = (bf16[128,640]{1,0:T(8,128)(2,1)S(1)}, bf16[128,640]{1,0:T(8,128)(2,1)S(1)}, u32[]{:S(2)}, u32[]{:S(2)}) collective-permute-start(bf16[128,640]{1,0:T(8,128)(2,1)S(1)} %collective-permute-done.refs_1_), channel_id=1, source_target_pairs={{0,96},{32,0},{64,32},{96,64},{1,97},{33,1},{65,33},{97,65},{2,98}... | collective-permute-start | bytes 491528 | tf_op jit(solution)/shard_map/ppermute | solution.py:293
  20.3 1.2 %collective-permute-start.15 = (bf16[96,5120]{1,0:T(8,128)(2,1)}, bf16[96,5120]{1,0:T(8,128)(2,1)}, u32[]{:S(2)}, u32[]{:S(2)}) collective-permute-start(bf16[96,5120]{1,0:T(8,128)(2,1)} %bitcast.14), channel_id=1, source_target_pairs={{0,16},{16,0},{1,17},{17,1},{2,18},{18,2},{3,19},{19,3},{4,20},{20... | collective-permute-start | bytes 2949128 | tf_op jit(solution)/shard_map/ppermute | solution.py:392
  21.4 2.3 %collective-permute-done.4.refs_5_ = bf16[128,640]{1,0:T(8,128)(2,1)S(1)} collective-permute-done((bf16[128,640]{1,0:T(8,128)(2,1)S(1)}, bf16[128,640]{1,0:T(8,128)(2,1)S(1)}, u32[]{:S(2)}, u32[]{:S(2)}) %collective-permute-start.4) | collective-permute-done | bytes 163872 | tf_op jit(solution)/shard_map/ppermute | solution.py:293
  23.9 2.3 %collective-permute-done.3.refs_4_ = bf16[128,640]{1,0:T(8,128)(2,1)S(1)} collective-permute-done((bf16[128,640]{1,0:T(8,128)(2,1)S(1)}, bf16[128,640]{1,0:T(8,128)(2,1)S(1)}, u32[]{:S(2)}, u32[]{:S(2)}) %collective-permute-start.3) | collective-permute-done | bytes 163872 | tf_op jit(solution)/shard_map/ppermute | solution.py:292
  26.5 3.0 %collective-permute-done.5.refs_6_ = bf16[128,640]{1,0:T(8,128)(2,1)S(1)} collective-permute-done((bf16[128,640]{1,0:T(8,128)(2,1)S(1)}, bf16[128,640]{1,0:T(8,128)(2,1)S(1)}, u32[]{:S(2)}, u32[]{:S(2)}) %collective-permute-start.5) | collective-permute-done | bytes 163872 | tf_op jit(solution)/shard_map/ppermute | solution.py:294
  29.5 1.1 %collective-permute-done.6.refs_7_ = bf16[128,640]{1,0:T(8,128)(2,1)S(1)} collective-permute-done((bf16[128,640]{1,0:T(8,128)(2,1)S(1)}, bf16[128,640]{1,0:T(8,128)(2,1)S(1)}, u32[]{:S(2)}, u32[]{:S(2)}) %collective-permute-start.6) | collective-permute-done | bytes 163872 | tf_op jit(solution)/shard_map/ppermute | solution.py:295
  30.8 1.6 %collective-permute-start.7 = (bf16[192,640]{1,0:T(8,128)(2,1)S(1)}, bf16[192,640]{1,0:T(8,128)(2,1)S(1)}, u32[]{:S(2)}, u32[]{:S(2)}) collective-permute-start(bf16[192,640]{1,0:T(8,128)(2,1)S(1)} %compact.1.refs_0_), channel_id=1, source_target_pairs={{0,128},{128,0},{1,129},{129,1},{2,130},{130,2},{3,131},{131,3},{4... | collective-permute-start | bytes 737288 | tf_op jit(solution)/shard_map/ppermute | solution.py:286
  32.5 3.6 %collective-permute-done.7.refs_1_ = bf16[192,640]{1,0:T(8,128)(2,1)S(1)} collective-permute-done((bf16[192,640]{1,0:T(8,128)(2,1)S(1)}, bf16[192,640]{1,0:T(8,128)(2,1)S(1)}, u32[]{:S(2)}, u32[]{:S(2)}) %collective-permute-start.7) | collective-permute-done | bytes 245792 | tf_op jit(solution)/shard_map/ppermute | solution.py:286
  36.0 1.5 %collective-permute-start.9 = (bf16[192,640]{1,0:T(8,128)(2,1)S(1)}, bf16[192,640]{1,0:T(8,128)(2,1)S(1)}, u32[]{:S(2)}, u32[]{:S(2)}) collective-permute-start(bf16[192,640]{1,0:T(8,128)(2,1)S(1)} %collective-permute-done.7.refs_1_), channel_id=1, source_target_pairs={{0,96},{32,0},{64,32},{96,64},{1,97},{33,1},{65,33},{97,65},{2,98}... | collective-permute-start | bytes 737288 | tf_op jit(solution)/shard_map/ppermute | solution.py:293
  37.6 1.1 %collective-permute-done.10.refs_2_ = bf16[192,640]{1,0:T(8,128)(2,1)S(1)} collective-permute-done((bf16[192,640]{1,0:T(8,128)(2,1)S(1)}, bf16[192,640]{1,0:T(8,128)(2,1)S(1)}, u32[]{:S(2)}, u32[]{:S(2)}) %collective-permute-start.10) | collective-permute-done | bytes 245792 | tf_op jit(solution)/shard_map/ppermute | solution.py:287
  40.3 1.1 %collective-permute-done.9.refs_1_ = bf16[192,640]{1,0:T(8,128)(2,1)S(1)} collective-permute-done((bf16[192,640]{1,0:T(8,128)(2,1)S(1)}, bf16[192,640]{1,0:T(8,128)(2,1)S(1)}, u32[]{:S(2)}, u32[]{:S(2)}) %collective-permute-start.9) | collective-permute-done | bytes 245792 | tf_op jit(solution)/shard_map/ppermute | solution.py:293
  41.4 2.5 %collective-permute-start.12 = (bf16[192,640]{1,0:T(8,128)(2,1)S(1)}, bf16[192,640]{1,0:T(8,128)(2,1)S(1)}, u32[]{:S(2)}, u32[]{:S(2)}) collective-permute-start(bf16[192,640]{1,0:T(8,128)(2,1)S(1)} %collective-permute-done.9.refs_1_), channel_id=1, source_target_pairs={{0,96},{32,0},{64,32},{96,64},{1,97},{33,1},{65,33},{97,65},{2,98}... | collective-permute-start | bytes 737288 | tf_op jit(solution)/shard_map/ppermute | solution.py:295
  43.8 2.5 %stack.1 = (bf16[384,5120]{1,0:T(8,128)(2,1)S(1)}, bf16[192,5120]{1,0:T(8,128)(2,1)S(1)}) custom-call(bf16[96,5120]{1,0:T(8,128)(2,1)} %bitcast.11, bf16[96,5120]{1,0:T(8,128)(2,1)S(1)} %collective-permute-done.13.gate_other, bf16[96,5120]{1,0:T(8,128)(2,1)} %bitcast.13, bf16[96,5120]{1,0:T(8,128)(2,1)} %collective-permute-done.14.up_other, ...), custom_call_target="tpu_custom_call" | custom-call | bytes 12582912 | tf_op jit(solution)/shard_map/stack/pallas_call | solution.py:269
  47.2 1.7 %collective-permute-done.11.refs_2_ = bf16[192,640]{1,0:T(8,128)(2,1)S(1)} collective-permute-done((bf16[192,640]{1,0:T(8,128)(2,1)S(1)}, bf16[192,640]{1,0:T(8,128)(2,1)S(1)}, u32[]{:S(2)}, u32[]{:S(2)}) %collective-permute-start.11) | collective-permute-done | bytes 245792 | tf_op jit(solution)/shard_map/ppermute | solution.py:294
  48.9 1.4 %collective-permute-done.12.refs_3_ = bf16[192,640]{1,0:T(8,128)(2,1)S(1)} collective-permute-done((bf16[192,640]{1,0:T(8,128)(2,1)S(1)}, bf16[192,640]{1,0:T(8,128)(2,1)S(1)}, u32[]{:S(2)}, u32[]{:S(2)}) %collective-permute-start.12) | collective-permute-done | bytes 245792 | tf_op jit(solution)/shard_map/ppermute | solution.py:295
  50.3 4.1 %expert.1 = bf16[8,192,640]{2,1,0:T(8,128)(2,1)} custom-call(bf16[192,640]{1,0:T(8,128)(2,1)S(1)} %collective-permute-done.8.refs_0_, bf16[192,640]{1,0:T(8,128)(2,1)S(1)} %collective-permute-done.9.refs_1_, bf16[192,640]{1,0:T(8,128)(2,1)S(1)} %collective-permute-done.11.refs_2_, bf16[192,640]{1,0:T(8,128)(2,1)S(1)} %collective-permute-done.12.refs_3_, ...), custom_call_target="tpu_custom_call" | custom-call | flops 566231040 | bytes 3145728 | tf_op jit(solution)/shard_map/expert/pallas_call | solution.py:269
  54.4 5.5 %all-to-all-start.1 = ((bf16[8,192,640]{2,1,0:T(8,128)(2,1)}), bf16[8,192,640]{2,1,0:T(8,128)(2,1)S(1)}, u32[]{:S(2)}, u32[]{:S(2)}) async-start(bf16[8,192,640]{2,1,0:T(8,128)(2,1)} %expert.1), calls=%async_computation.1 | async-start | bytes 3932160 | tf_op jit(solution)/shard_map/all_to_all | solution.py:299
  59.9 6.3 %collective-permute-start.17 = (bf16[1024,640]{1,0:T(8,128)(2,1)S(1)}, bf16[1024,640]{1,0:T(8,128)(2,1)S(1)}, u32[]{:S(2)}, u32[]{:S(2)}) collective-permute-start(bf16[1024,640]{1,0:T(8,128)(2,1)S(1)} %join.1.refs_0_), channel_id=1, source_target_pairs={{0,16},{16,0},{1,17},{17,1},{2,18},{18,2},{3,19},{19,3},{4,20},{20... | collective-permute-start | bytes 3932168 | tf_op jit(solution)/shard_map/ppermute | solution.py:364
  66.2 1.7 %absorb.1.query_ref = bf16[512,576]{1,0:T(8,128)(2,1)S(1)} custom-call(bf16[64,1024]{1,0:T(8,128)(2,1)} %nope_hbm, bf16[64,512]{1,0:T(8,128)(2,1)} %rope_hbm.1, bf16[8,128,512]{2,1,0:T(8,128)(2,1)} %uk_hbm.1), custom_call_target="tpu_custom_call" | custom-call | flops 67108864 | bytes 2097152 | tf_op jit(solution)/shard_map/absorb/pallas_call | solution.py:269
  67.8 1.0 collective-permute-done.17.refs_1_
  68.8 2.9 %attend.3.refs_1_ = bf16[256,512]{1,0:T(8,128)(2,1)S(1)} custom-call(bf16[512,576]{1,0:T(8,128)(2,1)S(1)} %absorb.1.query_ref, bf16[1024,640]{1,0:T(8,128)(2,1)S(1)} %join.1.refs_0_, bf16[1024,640]{1,0:T(8,128)(2,1)S(1)} %collective-permute-done.17.refs_1_), custom_call_target="tpu_custom_call" | custom-call | flops 1140850688 | bytes 4194304 | tf_op jit(solution)/shard_map/attend/pallas_call | solution.py:269
  71.8 2.9 %attend.2.refs_0_ = bf16[256,512]{1,0:T(8,128)(2,1)S(1)} custom-call(bf16[512,576]{1,0:T(8,128)(2,1)S(1)} %absorb.1.query_ref, bf16[1024,640]{1,0:T(8,128)(2,1)S(1)} %join.1.refs_0_, bf16[1024,640]{1,0:T(8,128)(2,1)S(1)} %collective-permute-done.17.refs_1_), custom_call_target="tpu_custom_call" | custom-call | flops 1140850688 | bytes 4194304 | tf_op jit(solution)/shard_map/attend/pallas_call | solution.py:269
  74.7 2.2 %value.1 = bf16[64,1024]{1,0:T(8,128)(2,1)} custom-call(bf16[256,512]{1,0:T(8,128)(2,1)S(1)} %attend.2.refs_0_, bf16[256,512]{1,0:T(8,128)(2,1)S(1)} %attend.3.refs_1_, bf16[8,512,128]{2,1,0:T(8,128)(2,1)} %refs_2_.1), custom_call_target="tpu_custom_call" | custom-call | flops 67108864 | bytes 2097152 | tf_op jit(solution)/shard_map/value/pallas_call | solution.py:269
  76.9 7.4 %all-to-all-done.1.parts_ref = bf16[8,192,640]{2,1,0:T(8,128)(2,1)S(1)} async-done(((bf16[8,192,640]{2,1,0:T(8,128)(2,1)}), bf16[8,192,640]{2,1,0:T(8,128)(2,1)S(1)}, u32[]{:S(2)}, u32[]{:S(2)}) %all-to-all-start.1) | async-done | bytes 1966112 | tf_op jit(solution)/shard_map/all_to_all | solution.py:299
  84.6 18.8 %all_to_all.21 = bf16[16,16,640]{2,1,0:T(8,128)(2,1)S(1)} all-to-all(bf16[16,16,640]{2,1,0:T(8,128)(2,1)S(1)} %bitcast.8), channel_id=1, replica_groups=mesh['xl'=2,'y'=4,'c'=2,'xh'=2,'z'=8] {'xh','z'}, dimensions={0} | all-to-all | bytes 655360 | tf_op jit(solution)/shard_map/all_to_all | solution.py:299
  103.7 3.1 %collective-permute-start.18 = (bf16[48,320]{1,0:T(8,128)(2,1)S(1)}, bf16[48,320]{1,0:T(8,128)(2,1)S(1)}, u32[]{:S(2)}, u32[]{:S(2)}) collective-permute-start(bf16[48,320]{1,0:T(8,128)(2,1)S(1)} %get-tuple-element.33), channel_id=1, source_target_pairs={{0,16},{16,0},{1,17},{17,1},{2,18},{18,2},{3,19},{19,3},{4,20},{20... | collective-permute-start | bytes 92168 | tf_op jit(solution)/shard_map/ppermute | solution.py:495
  (25 shorter events, 5.3 us)
Async XLA Ops:
  1.7 16.9 %collective-permute-start = (bf16[128,640]{1,0:T(8,128)(2,1)S(1)}, bf16[128,640]{1,0:T(8,128)(2,1)S(1)}, u32[]{:S(2)}, u32[]{:S(2)}) collective-permute-start(bf16[128,640]{1,0:T(8,128)(2,1)S(1)} %prep.1.refs_0_), channel_id=1, source_target_pairs={{0,128},{128,0},{1,129},{129,1},{2,130},{130,2},{3,131},{131,3},{4... | collective-permute-start | bytes 491528 | tf_op jit(solution)/shard_map/ppermute | solution.py:286
  1.8 16.8 %collective-permute-start.1 = (bf16[128,640]{1,0:T(8,128)(2,1)S(1)}, bf16[128,640]{1,0:T(8,128)(2,1)S(1)}, u32[]{:S(2)}, u32[]{:S(2)}) collective-permute-start(bf16[128,640]{1,0:T(8,128)(2,1)S(1)} %prep.1.refs_0_), channel_id=1, source_target_pairs={{0,32},{32,64},{64,96},{96,0},{1,33},{33,65},{65,97},{97,1},{2,34}... | collective-permute-start | bytes 491528 | tf_op jit(solution)/shard_map/ppermute | solution.py:287
  3.3 15.3 %collective-permute-start.2 = (bf16[128,640]{1,0:T(8,128)(2,1)S(1)}, bf16[128,640]{1,0:T(8,128)(2,1)S(1)}, u32[]{:S(2)}, u32[]{:S(2)}) collective-permute-start(bf16[128,640]{1,0:T(8,128)(2,1)S(1)} %prep.1.refs_0_), channel_id=1, source_target_pairs={{0,96},{32,0},{64,32},{96,64},{1,97},{33,1},{65,33},{97,65},{2,98}... | collective-permute-start | bytes 491528 | tf_op jit(solution)/shard_map/ppermute | solution.py:288
  6.8 32.5 %collective-permute-start.13 = (bf16[96,5120]{1,0:T(8,128)(2,1)}, bf16[96,5120]{1,0:T(8,128)(2,1)S(1)}, u32[]{:S(2)}, u32[]{:S(2)}) collective-permute-start(bf16[96,5120]{1,0:T(8,128)(2,1)} %bitcast.10), channel_id=1, source_target_pairs={{0,16},{16,0},{1,17},{17,1},{2,18},{18,2},{3,19},{19,3},{4,20},{20... | collective-permute-start | bytes 2949128 | tf_op jit(solution)/shard_map/ppermute | solution.py:392
  10.1 30.1 %collective-permute-start.14 = (bf16[96,5120]{1,0:T(8,128)(2,1)}, bf16[96,5120]{1,0:T(8,128)(2,1)}, u32[]{:S(2)}, u32[]{:S(2)}) collective-permute-start(bf16[96,5120]{1,0:T(8,128)(2,1)} %bitcast.12), channel_id=1, source_target_pairs={{0,16},{16,0},{1,17},{17,1},{2,18},{18,2},{3,19},{19,3},{4,20},{20... | collective-permute-start | bytes 2949128 | tf_op jit(solution)/shard_map/ppermute | solution.py:392
  10.2 20.6 %all-to-all-start = ((bf16[16,12,640]{2,1,0:T(8,128)(2,1)}), bf16[16,12,640]{2,1,0:T(8,128)(2,1)S(1)}, u32[]{:S(2)}, u32[]{:S(2)}) async-start(bf16[16,12,640]{2,1,0:T(8,128)(2,1)} %get-tuple-element.19), calls=%async_computation | async-start | bytes 655360 | tf_op jit(solution)/shard_map/all_to_all | solution.py:299
  18.6 5.1 %collective-permute-start.4 = (bf16[128,640]{1,0:T(8,128)(2,1)S(1)}, bf16[128,640]{1,0:T(8,128)(2,1)S(1)}, u32[]{:S(2)}, u32[]{:S(2)}) collective-permute-start(bf16[128,640]{1,0:T(8,128)(2,1)S(1)} %collective-permute-done.refs_1_), channel_id=1, source_target_pairs={{0,96},{32,0},{64,32},{96,64},{1,97},{33,1},{65,33},{97,65},{2,98}... | collective-permute-start | bytes 491528 | tf_op jit(solution)/shard_map/ppermute | solution.py:293
  20.2 5.9 %collective-permute-start.3 = (bf16[128,640]{1,0:T(8,128)(2,1)S(1)}, bf16[128,640]{1,0:T(8,128)(2,1)S(1)}, u32[]{:S(2)}, u32[]{:S(2)}) collective-permute-start(bf16[128,640]{1,0:T(8,128)(2,1)S(1)} %collective-permute-done.refs_1_), channel_id=1, source_target_pairs={{0,32},{32,64},{64,96},{96,0},{1,33},{33,65},{65,97},{97,1},{2,34}... | collective-permute-start | bytes 491528 | tf_op jit(solution)/shard_map/ppermute | solution.py:292
  20.3 23.6 %collective-permute-start.15 = (bf16[96,5120]{1,0:T(8,128)(2,1)}, bf16[96,5120]{1,0:T(8,128)(2,1)}, u32[]{:S(2)}, u32[]{:S(2)}) collective-permute-start(bf16[96,5120]{1,0:T(8,128)(2,1)} %bitcast.14), channel_id=1, source_target_pairs={{0,16},{16,0},{1,17},{17,1},{2,18},{18,2},{3,19},{19,3},{4,20},{20... | collective-permute-start | bytes 2949128 | tf_op jit(solution)/shard_map/ppermute | solution.py:392
  23.8 5.7 %collective-permute-start.5 = (bf16[128,640]{1,0:T(8,128)(2,1)S(1)}, bf16[128,640]{1,0:T(8,128)(2,1)S(1)}, u32[]{:S(2)}, u32[]{:S(2)}) collective-permute-start(bf16[128,640]{1,0:T(8,128)(2,1)S(1)} %collective-permute-done.1.refs_2_), channel_id=1, source_target_pairs={{0,32},{32,64},{64,96},{96,0},{1,33},{33,65},{65,97},{97,1},{2,34}... | collective-permute-start | bytes 491528 | tf_op jit(solution)/shard_map/ppermute | solution.py:294
  26.2 4.5 %collective-permute-start.6 = (bf16[128,640]{1,0:T(8,128)(2,1)S(1)}, bf16[128,640]{1,0:T(8,128)(2,1)S(1)}, u32[]{:S(2)}, u32[]{:S(2)}) collective-permute-start(bf16[128,640]{1,0:T(8,128)(2,1)S(1)} %collective-permute-done.4.refs_5_), channel_id=1, source_target_pairs={{0,96},{32,0},{64,32},{96,64},{1,97},{33,1},{65,33},{97,65},{2,98}... | collective-permute-start | bytes 491528 | tf_op jit(solution)/shard_map/ppermute | solution.py:295
  30.8 5.2 %collective-permute-start.7 = (bf16[192,640]{1,0:T(8,128)(2,1)S(1)}, bf16[192,640]{1,0:T(8,128)(2,1)S(1)}, u32[]{:S(2)}, u32[]{:S(2)}) collective-permute-start(bf16[192,640]{1,0:T(8,128)(2,1)S(1)} %compact.1.refs_0_), channel_id=1, source_target_pairs={{0,128},{128,0},{1,129},{129,1},{2,130},{130,2},{3,131},{131,3},{4... | collective-permute-start | bytes 737288 | tf_op jit(solution)/shard_map/ppermute | solution.py:286
  32.5 6.3 %collective-permute-start.10 = (bf16[192,640]{1,0:T(8,128)(2,1)S(1)}, bf16[192,640]{1,0:T(8,128)(2,1)S(1)}, u32[]{:S(2)}, u32[]{:S(2)}) collective-permute-start(bf16[192,640]{1,0:T(8,128)(2,1)S(1)} %compact.1.refs_0_), channel_id=1, source_target_pairs={{0,32},{32,64},{64,96},{96,0},{1,33},{33,65},{65,97},{97,1},{2,34}... | collective-permute-start | bytes 737288 | tf_op jit(solution)/shard_map/ppermute | solution.py:287
  36.0 5.3 %collective-permute-start.9 = (bf16[192,640]{1,0:T(8,128)(2,1)S(1)}, bf16[192,640]{1,0:T(8,128)(2,1)S(1)}, u32[]{:S(2)}, u32[]{:S(2)}) collective-permute-start(bf16[192,640]{1,0:T(8,128)(2,1)S(1)} %collective-permute-done.7.refs_1_), channel_id=1, source_target_pairs={{0,96},{32,0},{64,32},{96,64},{1,97},{33,1},{65,33},{97,65},{2,98}... | collective-permute-start | bytes 737288 | tf_op jit(solution)/shard_map/ppermute | solution.py:293
  38.7 7.7 %collective-permute-start.16 = (bf16[192,640]{1,0:T(8,128)(2,1)S(1)}, bf16[192,640]{1,0:T(8,128)(2,1)S(1)}, u32[]{:S(2)}, u32[]{:S(2)}) collective-permute-start(bf16[192,640]{1,0:T(8,128)(2,1)S(1)} %compact.1.refs_0_), channel_id=1, source_target_pairs={{0,96},{32,0},{64,32},{96,64},{1,97},{33,1},{65,33},{97,65},{2,98}... | collective-permute-start | bytes 737288 | tf_op jit(solution)/shard_map/ppermute | solution.py:288
  39.3 7.8 %collective-permute-start.8 = (bf16[192,640]{1,0:T(8,128)(2,1)S(1)}, bf16[192,640]{1,0:T(8,128)(2,1)S(1)}, u32[]{:S(2)}, u32[]{:S(2)}) collective-permute-start(bf16[192,640]{1,0:T(8,128)(2,1)S(1)} %collective-permute-done.7.refs_1_), channel_id=1, source_target_pairs={{0,32},{32,64},{64,96},{96,0},{1,33},{33,65},{65,97},{97,1},{2,34}... | collective-permute-start | bytes 737288 | tf_op jit(solution)/shard_map/ppermute | solution.py:292
  40.2 8.7 %collective-permute-start.11 = (bf16[192,640]{1,0:T(8,128)(2,1)S(1)}, bf16[192,640]{1,0:T(8,128)(2,1)S(1)}, u32[]{:S(2)}, u32[]{:S(2)}) collective-permute-start(bf16[192,640]{1,0:T(8,128)(2,1)S(1)} %collective-permute-done.10.refs_2_), channel_id=1, source_target_pairs={{0,32},{32,64},{64,96},{96,0},{1,33},{33,65},{65,97},{97,1},{2,34}... | collective-permute-start | bytes 737288 | tf_op jit(solution)/shard_map/ppermute | solution.py:294
  41.4 8.9 %collective-permute-start.12 = (bf16[192,640]{1,0:T(8,128)(2,1)S(1)}, bf16[192,640]{1,0:T(8,128)(2,1)S(1)}, u32[]{:S(2)}, u32[]{:S(2)}) collective-permute-start(bf16[192,640]{1,0:T(8,128)(2,1)S(1)} %collective-permute-done.9.refs_1_), channel_id=1, source_target_pairs={{0,96},{32,0},{64,32},{96,64},{1,97},{33,1},{65,33},{97,65},{2,98}... | collective-permute-start | bytes 737288 | tf_op jit(solution)/shard_map/ppermute | solution.py:295
  54.4 29.9 %all-to-all-start.1 = ((bf16[8,192,640]{2,1,0:T(8,128)(2,1)}), bf16[8,192,640]{2,1,0:T(8,128)(2,1)S(1)}, u32[]{:S(2)}, u32[]{:S(2)}) async-start(bf16[8,192,640]{2,1,0:T(8,128)(2,1)} %expert.1), calls=%async_computation.1 | async-start | bytes 3932160 | tf_op jit(solution)/shard_map/all_to_all | solution.py:299
  59.9 8.9 %collective-permute-start.17 = (bf16[1024,640]{1,0:T(8,128)(2,1)S(1)}, bf16[1024,640]{1,0:T(8,128)(2,1)S(1)}, u32[]{:S(2)}, u32[]{:S(2)}) collective-permute-start(bf16[1024,640]{1,0:T(8,128)(2,1)S(1)} %join.1.refs_0_), channel_id=1, source_target_pairs={{0,16},{16,0},{1,17},{17,1},{2,18},{18,2},{3,19},{19,3},{4,20},{20... | collective-permute-start | bytes 3932168 | tf_op jit(solution)/shard_map/ppermute | solution.py:364
  103.7 3.9 %collective-permute-start.18 = (bf16[48,320]{1,0:T(8,128)(2,1)S(1)}, bf16[48,320]{1,0:T(8,128)(2,1)S(1)}, u32[]{:S(2)}, u32[]{:S(2)}) collective-permute-start(bf16[48,320]{1,0:T(8,128)(2,1)S(1)} %get-tuple-element.33), channel_id=1, source_target_pairs={{0,16},{16,0},{1,17},{17,1},{2,18},{18,2},{3,19},{19,3},{4,20},{20... | collective-permute-start | bytes 92168 | tf_op jit(solution)/shard_map/ppermute | solution.py:495
